TPU v7x, 32 devices: a whole 2x2x4 slice. The times are simulated.
32 devices in a mesh: gx: 4 (over y, core), gy: 8 (over z, x).
Axes of the slice: x: 2, y: 2, z: 4, core: 2. Of those that a mesh axis runs over, the one named last changes fastest.
Arguments:
- tracers: float32 [2016, 2, 20, 1024], P(('gx', 'gy')), may hold values from -6 to 6
- diffusion: float32 [20], replicated, may hold values from 0.03 to 0.24
- layer_weight: float32 [2, 20], replicated, may hold values from -2 to 2
- surface_term: float32 [1280, 1792], P('gy', 'gx'), may hold values from 0.05 to 2
- clinic_blocks: int32 [2016], P(('gx', 'gy')), may hold values from 0 to 2239, as said below
- halo_source: int32 [2016, 4], P(('gx', 'gy')), may hold values from 0 to 8064, as said below
Outputs:
- tracers_next: float32 [2016, 2, 20, 1024], P(('gx', 'gy'))
- pressure: float32 [2016, 1024], P(('gx', 'gy'))
Inputs may be any that keep to these rules, and one draw needn't show every extreme that they name: `clinic_blocks`: each entry is a grid block, each block at most once; blocks that no entry names are land. Region (a, b) holds blocks bx in [a 14, (a + 1) * 14) and by in [b * 5, (b + 1) * 5). The slots of the device at mesh index (i, j), d = i * 8 + j, are slots d * 63 to (d + 1) * 63 - 1, and their blocks lie in region (i, j) or region (i, (j + 1) mod 8); those in region (i, (j + 1) mod 8) are the device's last slots, at most 22 of them, and some device has exactly 22. halo_source[s, t] is 4 s' + t' for the ocean block beside side t of slot s's block (t' the side facing it; periodic along the columns), or 8064 where that block is land or beyond the first or last row. Slot s' lies on the device of slot s or on one of the eight devices around it in the mesh (periodic along gx and gy); where its gx index differs, t' is 0 or 1.
All inputs are finite; a program needn't handle non-finite values.
Results may differ from a plain program's by a relative error of at most 0.0001.
Values sent between devices are 32-bit elements; how exact they have to be, the bound alone decides.
No kernel may reach another device: no remote copies, remote signals or barrier semaphores. Data moves between devices by JAX's collectives and lax.ppermute only.
A program may use at most 320 MiB of HBM per device.

v0:
```python
import jax
import jax.numpy as jnp
from jax import lax
from jax.sharding import PartitionSpec as P

BLOCK = 32
LEVELS = 20
TRACER = 2
REG_X = 14
REG_Y = 5
ITERS = 3


def with_halo(block, sides, width):
    for axis, dim in sides:
        count = lax.axis_size(axis)
        forward = [(i, i + 1) for i in range(count - 1)]
        forward.append((count - 1, 0))
        backward = [(target, source) for source, target in forward]
        low = lax.ppermute(
            lax.slice_in_dim(block, block.shape[dim] - width, None, axis=dim), axis, forward
        )
        high = lax.ppermute(lax.slice_in_dim(block, 0, width, axis=dim), axis, backward)
        block = jnp.concatenate([low, block, high], axis=dim)
    return block


def shifted(x, axis, by):
    length = lax.axis_size(axis)
    return lax.ppermute(x, axis, [(i, (i + by) % length) for i in range(length)])


def edge_strips(tracer_grid):
    west_edge = tracer_grid[..., :, 0]
    east_edge = tracer_grid[..., :, -1]
    south_edge = tracer_grid[..., 0, :]
    north_edge = tracer_grid[..., -1, :]
    stacked = jnp.stack([west_edge, east_edge, south_edge, north_edge], axis=1)
    return stacked.reshape(tracer_grid.shape[0] * 4, -1)


def diffuse_flat(flat, halo_rows, opened, diffusion):
    slot_count = flat.shape[0]
    area = BLOCK * BLOCK
    halo_grid = halo_rows.reshape(slot_count, 4, TRACER, LEVELS, BLOCK)
    gate = opened.reshape(slot_count, 4, 1, 1, 1)
    cells = jnp.arange(area)
    column = cells % BLOCK
    row_pos = cells // BLOCK
    pad_one = jnp.zeros((slot_count, TRACER, LEVELS, 1), jnp.float32)
    pad_row = jnp.zeros((slot_count, TRACER, LEVELS, BLOCK), jnp.float32)
    left_cells = jnp.concatenate([pad_one, flat[..., :-1]], axis=-1)
    right_cells = jnp.concatenate([flat[..., 1:], pad_one], axis=-1)
    below_cells = jnp.concatenate([pad_row, flat[..., :-BLOCK]], axis=-1)
    above_cells = jnp.concatenate([flat[..., BLOCK:], pad_row], axis=-1)
    west_side = jnp.repeat(halo_grid[:, 0], BLOCK, axis=-1)
    east_side = jnp.repeat(halo_grid[:, 1], BLOCK, axis=-1)
    south_side = jnp.tile(halo_grid[:, 2], (1, 1, 1, BLOCK))
    north_side = jnp.tile(halo_grid[:, 3], (1, 1, 1, BLOCK))
    from_west = jnp.where(column == 0, (west_side - flat) * gate[:, 0], left_cells - flat)
    from_east = jnp.where(column == BLOCK - 1, (east_side - flat) * gate[:, 1], right_cells - flat)
    from_south = jnp.where(row_pos == 0, (south_side - flat) * gate[:, 2], below_cells - flat)
    from_north = jnp.where(
        row_pos == BLOCK - 1, (north_side - flat) * gate[:, 3], above_cells - flat
    )
    laplace = from_west + from_east + from_south + from_north
    return flat + diffusion[None, None, :, None] * laplace


def to_field(blocks):
    return (
        blocks.reshape(REG_Y, REG_X, BLOCK, BLOCK)
        .transpose(0, 2, 1, 3)
        .reshape(REG_Y * BLOCK, REG_X * BLOCK)
    )


def from_field(values):
    return (
        values.reshape(REG_Y, BLOCK, REG_X, BLOCK)
        .transpose(0, 2, 1, 3)
        .reshape(REG_Y * REG_X, BLOCK * BLOCK)
    )


def norm_total(residual, precond):
    return lax.psum(jnp.sum(residual * precond), ("gx", "gy"))


def on_device(tracers, diffusion, layer_weight, surface_term, clinic_blocks, halo_source):
    slot_count = tracers.shape[0]
    tracer_grid = tracers.reshape(slot_count, TRACER, LEVELS, BLOCK, BLOCK)
    strips = edge_strips(tracer_grid)
    strip_width = strips.shape[1]
    count_gx = lax.axis_size("gx")
    count_gy = lax.axis_size("gy")
    column_at = lax.axis_index("gx")
    row_at = lax.axis_index("gy")
    grid_columns = REG_X * count_gx
    own_row = clinic_blocks // grid_columns
    own_col = clinic_blocks % grid_columns
    source = halo_source.reshape(-1)
    missing = source >= 4 * slot_count * count_gx * count_gy
    source_slot = jnp.where(missing, 0, source) // 4
    source_side = source % 4
    owner_flat = source_slot // slot_count
    local_slot = source_slot % slot_count
    step_gx = (owner_flat // count_gy - column_at + count_gx + 1) % count_gx
    step_gy = (owner_flat % count_gy - row_at + count_gy + 1) % count_gy
    count_all = slot_count * 4
    beside_all = with_halo(strips.reshape(1, 1, count_all, strip_width), (("gx", 0), ("gy", 1)), 1)
    lookup = beside_all.reshape(9 * count_all, strip_width)
    row_index = (step_gx * 3 + step_gy) * count_all + local_slot * 4 + source_side
    row_index = jnp.where(missing, 0, row_index)
    halo_rows = jnp.take(lookup, row_index, axis=0, mode="clip")
    opened = jnp.where(missing, 0.0, 1.0).astype(jnp.float32)
    updated = diffuse_flat(tracers, halo_rows, opened, diffusion)
    forcing = jnp.sum(updated * layer_weight[None, :, :, None], axis=(1, 2))
    came_forcing, came_blocks = shifted((forcing, clinic_blocks), "gy", 1)
    all_forcing = jnp.concatenate([forcing, came_forcing], axis=0)
    all_blocks = jnp.concatenate([clinic_blocks, came_blocks], axis=0)
    block_col = all_blocks % grid_columns
    block_row = all_blocks // grid_columns
    inside = (block_col // REG_X == column_at) & (block_row // REG_Y == row_at)
    region_slot = block_row % REG_Y * REG_X + block_col % REG_X
    placement = (
        (region_slot[None, :] == jnp.arange(REG_X * REG_Y)[:, None]) & inside[None, :]
    ).astype(jnp.float32)
    region_forcing = jnp.dot(placement, all_forcing, precision=lax.Precision.HIGHEST)
    region_mask = jnp.sum(placement, axis=1)
    rhs_field = to_field(region_forcing)
    mask_field = to_field(jnp.broadcast_to(region_mask[:, None], (REG_X * REG_Y, BLOCK * BLOCK)))
    diagonal = 6.0 + surface_term
    first_row = row_at == 0
    last_row = row_at == count_gy - 1
    solution = jnp.zeros_like(rhs_field)
    residual = rhs_field
    precond = residual / diagonal
    direction = precond
    norm_now = norm_total(residual, precond)
    for iteration in range(ITERS):
        padded = with_halo(direction, (("gx", 1), ("gy", 0)), 1)
        pad_rows = jnp.arange(padded.shape[0])
        keep_rows = jnp.where(
            (pad_rows == 0) & first_row | (pad_rows == padded.shape[0] - 1) & last_row, 0.0, 1.0
        )
        padded = padded * keep_rows[:, None]
        edge_sum = padded[2:, 1:-1] + padded[:-2, 1:-1] + padded[1:-1, 2:] + padded[1:-1, :-2]
        corners = padded[2:, 2:] + padded[2:, :-2] + padded[:-2, 2:] + padded[:-2, :-2]
        applied = mask_field * (diagonal * direction - edge_sum - 0.5 * corners)
        step_length = norm_now / lax.psum(jnp.sum(direction * applied), ("gx", "gy"))
        solution = solution + step_length * direction
        if iteration + 1 < ITERS:
            residual = residual - step_length * applied
            precond = residual / diagonal
            norm_next = norm_total(residual, precond)
            direction = precond + norm_next / norm_now * direction
            norm_now = norm_next
    solution_blocks = from_field(solution)
    own_region = own_row // REG_Y == row_at
    slot_place = own_row % REG_Y * REG_X + own_col % REG_X
    own_values = jnp.take(solution_blocks, slot_place, axis=0)
    next_blocks = shifted(solution_blocks, "gy", -1)
    other_values = jnp.take(next_blocks, slot_place, axis=0)
    pressure = jnp.where(own_region[:, None], own_values, other_values)
    return (updated, pressure)


def solution(mesh):
    placed = (
        P(("gx", "gy"), None, None, None),
        P(),
        P(),
        P("gy", "gx"),
        P(("gx", "gy")),
        P(("gx", "gy"), None),
    )
    return jax.shard_map(
        on_device,
        mesh=mesh,
        in_specs=placed,
        out_specs=(P(("gx", "gy"), None, None, None), P(("gx", "gy"), None)),
        check_vma=False,
    )
```

profile of v0, /device:TPU:0, one launch (start us, length us, event | category | flops | bytes accessed | tf_op | source)
XLA Modules:
  0.0 631.3 jit_solution(8563851166526220389)
XLA Ops:
  0.6 19.4 %copy.109 = f32[63,2,20,1024]{0,3,2,1:T(8,128)} copy(f32[63,2,20,1024]{3,1,2,0:T(2,128)} %param.8) | data formatting | bytes 20643840 | tf_op args[0]
  20.1 5.3 fusion.66
  25.4 1.4 slice_bitcast_fusion.5
  27.2 6.0 copy.83
  33.2 4.4 reshape_reshape.3
  37.6 1.3 copy.84
  39.4 2.0 collective-permute-start.1
  41.5 2.2 collective-permute-start.4
  44.0 23.7 %collective-permute-done = f32[1,1,252,1280]{3,1,2,0:T(1,128)} collective-permute-done((f32[1,1,252,1280]{3,1,2,0:T(1,128)S(1)}, f32[1,1,252,1280]{3,1,2,0:T(1,128)}, u32[]{:S(2)}, u32[]{:S(2)}) %collective-permute-start) | collective-permute-done | bytes 1290272 | tf_op jit(solution)/shard_map/ppermute | solution.py:20
  67.7 1.4 copy_dynamic-update-slice_fusion.1
  69.2 0.9 collective-permute-done.1
  70.1 1.4 copy_dynamic-update-slice_fusion
  71.5 1.9 copy-done
  73.4 5.8 copy.88
  79.3 2.2 collective-permute-start.2
  81.5 3.3 collective-permute-start.3
  84.8 28.3 %fusion.65 = (f32[63,2,20,992]{0,3,2,1:T(8,128)}, f32[63,2,20,992]{0,3,2,1:T(8,128)}) fusion(f32[63,2,20,1024]{0,3,2,1:T(8,128)} %copy.109), kind=kLoop, calls=%fused_computation.177 | loop fusion | bytes 39997440 | tf_op jit(solution)/shard_map/slice | solution.py:54
  113.2 14.2 %fusion.64 = (f32[63,2,20,1023]{0,3,2,1:T(8,128)}, f32[63,2,20,1023]{0,3,2,1:T(8,128)}) fusion(f32[63,2,20,1024]{0,3,2,1:T(8,128)S(1)} %bitcast.85), kind=kLoop, calls=%fused_computation.176 | loop fusion | bytes 41247360 | tf_op jit(solution)/shard_map/slice | solution.py:52
  127.3 120.7 %collective-permute-done.2 = f32[3,1,252,1280]{3,1,2,0:T(1,128)} collective-permute-done((f32[3,1,252,1280]{3,1,2,0:T(1,128)}, f32[3,1,252,1280]{3,1,2,0:T(1,128)}, u32[]{:S(2)}, u32[]{:S(2)}) %collective-permute-start.2) | collective-permute-done | bytes 3870752 | tf_op jit(solution)/shard_map/ppermute | solution.py:20
  248.0 2.5 copy.90
  250.5 2.5 copy.91
  253.0 4.7 pad_maximum_fusion
  257.7 9.6 %reshape.492 = f32[2268,1280]{1,0:T(8,128)} reshape(f32[3,3,252,1280]{3,2,1,0:T(8,128)} %pad_maximum_fusion) | data formatting | bytes 23224320 | tf_op jit(solution)/shard_map/reshape | solution.py:112
  267.2 6.1 gather_fusion
  273.3 5.0 reshape.494
  278.3 4.9 slice_bitcast_fusion.3
  283.3 2.8 copy.101
  286.0 2.8 copy.105
  288.8 1.4 copy.93
  290.3 0.6 copy.97
  290.9 44.3 %multiply_reduce_fusion = (f32[63,1024]{0,1:T(8,128)S(1)}, f32[63,2,20,1024]{0,3,2,1:T(8,128)}) fusion(f32[2,20]{1,0:T(2,128)S(1)} %copy-done.5, f32[63,2,20,1024]{0,3,2,1:T(8,128)} %copy.109, f32[63,2,20,992]{0,3,2,1:T(8,128)} %get-tuple-element.30, f32[63]{0:T(128)S(1)} %get-tuple-element.52, f32[63,2,20,32]{0,3,2,1:T(8,128)} %copy.105, ...), kind=kLoop, calls=%fused_computation.20 | loop fusion | flops 59286528 | bytes 62819872 | tf_op jit(solution)/shard_map/reduce_sum | solution.py:118
  335.2 2.5 collective-permute-start.5
  337.8 14.4 %collective-permute-done.5 = f32[63,1024]{0,1:T(8,128)S(1)} collective-permute-done((f32[63,1024]{0,1:T(8,128)S(1)}, f32[63,1024]{0,1:T(8,128)S(1)}, u32[]{:S(2)}, u32[]{:S(2)}) %collective-permute-start.5) | collective-permute-done | bytes 258080 | tf_op jit(solution)/shard_map/ppermute | solution.py:30
  353.1 0.7 copy.119
  354.5 1.7 collective-permute-start.7
  356.2 2.4 collective-permute-done.6
  358.7 4.7 collective-permute-start.9
  364.3 0.7 collective-permute-done.8
  365.2 1.1 multiply_reduce_fusion.4
  366.3 39.0 %all-reduce.4 = (f32[]{:T(128)}, f32[]{:T(128)}) all-reduce(f32[]{:T(128)} %get-tuple-element.10, f32[]{:T(128)} %get-tuple-element.9), channel_id=1, replica_groups=mesh['gx'=4,'gy'=8] {'gx','gy'}, use_global_device_ids=true, to_apply=%region_2.3 | all-reduce | flops 2 | bytes 16 | tf_op jit(solution)/shard_map/psum | solution.py:87
  406.7 0.7 multiply_reduce_fusion.3
  407.4 42.4 %psum.44 = f32[]{:T(128)} all-reduce(f32[]{:T(128)} %get-tuple-element.19), channel_id=1, replica_groups=mesh['gx'=4,'gy'=8] {'gx','gy'}, use_global_device_ids=true, to_apply=%region_7.8 | all-reduce | flops 1 | bytes 8 | tf_op jit(solution)/shard_map/psum | solution.py:87
  451.3 1.7 collective-permute-start.11
  453.0 2.1 collective-permute-done.10
  455.2 0.6 collective-permute-done.11
  455.8 1.9 collective-permute-start.12
  457.7 2.8 collective-permute-start.13
  460.5 1.6 collective-permute-done.12
  462.3 1.1 multiply_reduce_fusion.2
  463.4 41.4 %psum.45 = f32[]{:T(128)} all-reduce(f32[]{:T(128)} %get-tuple-element.17), channel_id=1, replica_groups=mesh['gx'=4,'gy'=8] {'gx','gy'}, use_global_device_ids=true, to_apply=%region_9.10 | all-reduce | flops 1 | bytes 8 | tf_op jit(solution)/shard_map/psum | solution.py:151
  506.1 0.7 multiply_reduce_fusion.1
  506.9 40.7 %psum.46 = f32[]{:T(128)} all-reduce(f32[]{:T(128)} %multiply_reduce_fusion.1), channel_id=1, replica_groups=mesh['gx'=4,'gy'=8] {'gx','gy'}, use_global_device_ids=true, to_apply=%region_11.12 | all-reduce | flops 1 | bytes 8 | tf_op jit(solution)/shard_map/psum | solution.py:87
  549.4 1.7 collective-permute-start.15
  551.2 2.1 collective-permute-done.14
  553.9 2.1 collective-permute-start.16
  556.1 2.6 collective-permute-start.17
  558.7 1.6 collective-permute-done.16
  560.4 1.1 fusion.21
  561.6 41.5 %psum.47 = f32[]{:T(128)} all-reduce(f32[]{:T(128)} %fusion.21), channel_id=1, replica_groups=mesh['gx'=4,'gy'=8] {'gx','gy'}, use_global_device_ids=true, to_apply=%region_13.14 | all-reduce | flops 1 | bytes 8 | tf_op jit(solution)/shard_map/psum | solution.py:151
  605.8 3.3 collective-permute-start.18
  609.1 20.0 %copy.112 = f32[63,2,20,1024]{3,1,2,0:T(2,128)} copy(f32[63,2,20,1024]{0,3,2,1:T(8,128)} %get-tuple-element.26) | data formatting | bytes 20643840
  629.1 0.7 gather_fusion.1
  629.8 0.7 gather_fusion.2
  630.5 0.8 select_select_fusion
  (76 shorter events, 7.4 us)
Async XLA Ops:
  26.8 14.6 %copy-start.4 = (s32[63]{0:T(128)S(1)}, s32[63]{0:T(128)}, u32[]{:S(2)}) copy-start(s32[63]{0:T(128)} %param.12) | copy-start | bytes 760
  26.8 16.8 %copy-start.3 = (s32[63,4]{0,1:T(4,128)S(1)}, s32[63,4]{0,1:T(4,128)}, u32[]{:S(2)}) copy-start(s32[63,4]{0,1:T(4,128)} %param.13) | copy-start | bytes 3028
  38.9 28.8 %collective-permute-start = (f32[1,1,252,1280]{3,1,2,0:T(1,128)S(1)}, f32[1,1,252,1280]{3,1,2,0:T(1,128)}, u32[]{:S(2)}, u32[]{:S(2)}) collective-permute-start(f32[1,1,252,1280]{3,1,2,0:T(1,128)S(1)} %copy.84), channel_id=1, source_target_pairs={{0,8},{8,16},{16,24},{24,0},{1,9},{9,17},{17,25},{25,1},{2,10},{10... | collective-permute-start | bytes 3870728 | tf_op jit(solution)/shard_map/ppermute | solution.py:20
  39.4 30.7 %collective-permute-start.1 = (f32[1,1,252,1280]{3,1,2,0:T(1,128)S(1)}, f32[1,1,252,1280]{3,1,2,0:T(1,128)}, u32[]{:S(2)}, u32[]{:S(2)}) collective-permute-start(f32[1,1,252,1280]{3,1,2,0:T(1,128)S(1)} %copy.84), channel_id=1, source_target_pairs={{8,0},{16,8},{24,16},{0,24},{9,1},{17,9},{25,17},{1,25},{10,2},{18... | collective-permute-start | bytes 3870728 | tf_op jit(solution)/shard_map/ppermute | solution.py:23
  41.5 296.2 %collective-permute-start.4 = (s32[63]{0:T(128)S(1)}, s32[63]{0:T(128)S(1)}, u32[]{:S(2)}, u32[]{:S(2)}) collective-permute-start(s32[63]{0:T(128)S(1)} %copy-done.4), channel_id=1, source_target_pairs={{0,1},{1,2},{2,3},{3,4},{4,5},{5,6},{6,7},{7,0},{8,9},{9,10},{10,1... | collective-permute-start | bytes 764 | tf_op jit(solution)/shard_map/ppermute | solution.py:30
  71.5 1.9 copy-start
  73.4 39.7 %slice-start = ((s8[20971520]{0:T(1024)(128)(4,1)}), s8[4194304]{0:T(1024)(128)(4,1)S(1)}, s32[]{:S(2)}) async-start(s8[20971520]{0:T(1024)(128)(4,1)} %bitcast.84), calls=%async_computation | async-start | bytes 8388608
  79.3 33.9 %slice-start.1 = ((s8[20971520]{0:T(1024)(128)(4,1)}), s8[4194304]{0:T(1024)(128)(4,1)S(1)}, s32[]{:S(2)}) async-start(s8[20971520]{0:T(1024)(128)(4,1)} %bitcast.84), calls=%async_computation.1 | async-start | bytes 8388608
  79.3 33.9 %slice-start.2 = ((s8[20971520]{0:T(1024)(128)(4,1)}), s8[4194304]{0:T(1024)(128)(4,1)S(1)}, s32[]{:S(2)}) async-start(s8[20971520]{0:T(1024)(128)(4,1)} %bitcast.84), calls=%async_computation.2 | async-start | bytes 8388608
  79.3 33.9 %slice-start.3 = ((s8[20971520]{0:T(1024)(128)(4,1)}), s8[4194304]{0:T(1024)(128)(4,1)S(1)}, s32[]{:S(2)}) async-start(s8[20971520]{0:T(1024)(128)(4,1)} %bitcast.84), calls=%async_computation.3 | async-start | bytes 8388608
  79.3 33.9 %slice-start.4 = ((s8[20971520]{0:T(1024)(128)(4,1)}), s8[4194304]{0:T(1024)(128)(4,1)S(1)}, s32[]{:S(2)}) async-start(s8[20971520]{0:T(1024)(128)(4,1)} %bitcast.84), calls=%async_computation.4 | async-start | bytes 8388608
  79.3 168.8 %collective-permute-start.2 = (f32[3,1,252,1280]{3,1,2,0:T(1,128)}, f32[3,1,252,1280]{3,1,2,0:T(1,128)}, u32[]{:S(2)}, u32[]{:S(2)}) collective-permute-start(f32[3,1,252,1280]{3,1,2,0:T(1,128)} %copy.88), channel_id=1, source_target_pairs={{0,1},{1,2},{2,3},{3,4},{4,5},{5,6},{6,7},{7,0},{8,9},{9,10},{10,1... | collective-permute-start | bytes 11612168 | tf_op jit(solution)/shard_map/ppermute | solution.py:20
  81.5 169.0 %collective-permute-start.3 = (f32[3,1,252,1280]{3,1,2,0:T(1,128)}, f32[3,1,252,1280]{3,1,2,0:T(1,128)}, u32[]{:S(2)}, u32[]{:S(2)}) collective-permute-start(f32[3,1,252,1280]{3,1,2,0:T(1,128)} %copy.88), channel_id=1, source_target_pairs={{1,0},{2,1},{3,2},{4,3},{5,4},{6,5},{7,6},{0,7},{9,8},{10,9},{11,1... | collective-permute-start | bytes 11612168 | tf_op jit(solution)/shard_map/ppermute | solution.py:23
  127.3 125.6 %copy-start.1 = (f32[3,1,252,1280]{3,2,1,0:T(8,128)S(1)}, f32[3,1,252,1280]{3,2,1,0:T(8,128)}, u32[]{:S(2)}) copy-start(f32[3,1,252,1280]{3,2,1,0:T(8,128)} %copy-done) | copy-start | bytes 11612164
  278.3 12.5 %copy-start.5 = (f32[2,20]{1,0:T(2,128)S(1)}, f32[2,20]{1,0:T(2,128)}, u32[]{:S(2)}) copy-start(f32[2,20]{1,0:T(2,128)} %param.10) | copy-start | bytes 484
  278.3 12.5 %copy-start.6 = (f32[20]{0:T(128)S(1)}, f32[20]{0:T(128)}, u32[]{:S(2)}) copy-start(f32[20]{0:T(128)} %param.9) | copy-start | bytes 244
  290.8 63.4 %copy-start.2 = (f32[160,448]{1,0:T(8,128)S(1)}, f32[160,448]{1,0:T(8,128)}, u32[]{:S(2)}) copy-start(f32[160,448]{1,0:T(8,128)} %param.11) | copy-start | bytes 860164
  335.2 17.0 %collective-permute-start.5 = (f32[63,1024]{0,1:T(8,128)S(1)}, f32[63,1024]{0,1:T(8,128)S(1)}, u32[]{:S(2)}, u32[]{:S(2)}) collective-permute-start(f32[63,1024]{0,1:T(8,128)S(1)} %get-tuple-element.25), channel_id=1, source_target_pairs={{0,1},{1,2},{2,3},{3,4},{4,5},{5,6},{6,7},{7,0},{8,9},{9,10},{10,1... | collective-permute-start | bytes 774152 | tf_op jit(solution)/shard_map/ppermute | solution.py:30
  354.4 4.2 collective-permute-start.6
  354.5 4.2 collective-permute-start.7
  358.7 6.3 collective-permute-start.8
  358.7 6.3 collective-permute-start.9
  451.2 3.9 collective-permute-start.10
  451.3 4.4 collective-permute-start.11
  455.8 6.3 collective-permute-start.12
  457.7 4.4 collective-permute-start.13
  549.1 4.2 collective-permute-start.14
  549.4 4.4 collective-permute-start.15
  553.9 6.3 collective-permute-start.16
  556.1 4.2 collective-permute-start.17
  605.8 24.0 %collective-permute-start.18 = (f32[70,1024]{1,0:T(8,128)S(1)}, f32[70,1024]{1,0:T(8,128)S(1)}, u32[]{:S(2)}, u32[]{:S(2)}) collective-permute-start(f32[70,1024]{1,0:T(8,128)S(1)} %reshape.501), channel_id=1, source_target_pairs={{0,7},{1,0},{2,1},{3,2},{4,3},{5,4},{6,5},{7,6},{8,15},{9,8},{10,9... | collective-permute-start | bytes 860168 | tf_op jit(solution)/shard_map/ppermute | solution.py:30
where the time goes:
time: 633 us; the launch traced here: 631 us
  blocking collectives  205 us (32%)
  waiting for transfers between devices  171 us (27%)
  local copies, waits for them, and re-layouts  154 us (24%)
  other arithmetic  56.5 us (9%)
  starting transfers between devices  35.9 us (6%)
  between operations  7.72 us (1%)
    ppermute x8, waiting for transfers between devices, with_halo(): lax.ppermute(lax.slice_in_dim(block, block.shape[dim] - width, None, axis...  155 us
    psum x3, blocking collectives, norm_total(): return lax.psum(jnp.sum(residual * precond), ('gx', 'gy'))  122 us
    psum x2, blocking collectives, on_device(): lax.psum(jnp.sum(direction * applied), ('gx', 'gy'))  82.9 us
    reduce_sum x1, other arithmetic, on_device(): forcing = jnp.sum(updated * layer_weight[None, :, :, None], axis=(1, 2))  44.3 us
    unnamed x29, local copies, waits for them, and re-layouts  43 us
    slice x1, local copies, waits for them, and re-layouts, diffuse_flat(): below_cells = jnp.concatenate([pad_row, flat[..., :-BLOCK]], axis=-1)  28.3 us
    ppermute x8, starting transfers between devices, with_halo(): lax.ppermute(lax.slice_in_dim(block, 0, width, axis=dim), axis, backward)  20.7 us
    ppermute x3, waiting for transfers between devices, shifted(): lax.ppermute(x, axis, [(i, (i + by) % length) for i in range(length)])  14.4 us
  transfers between devices with their start and end apart: 19, of which 12 were waited for; matrix products, arithmetic and copies ran while one was open for 25% of the time, Pallas kernels for 0%

commit v1 on v0

v1 whole, which is shorter than its diff:
```python
import jax
import jax.numpy as jnp
from jax import lax
from jax.experimental import pallas as pl
from jax.experimental.pallas import tpu as pltpu
from jax.sharding import PartitionSpec as P

BLOCK = 32
LEVELS = 20
TRACER = 2
REG_X = 14
REG_Y = 5
REGION = REG_X * REG_Y
MOVED = 22
LANES = 128
TILE = 8
ROWS = 16
HALF = LEVELS // 2
STEP_SLOTS = 7
FIELD_ROWS = 176
FIELD_TILES = 4
CAP_WE = 6
CAP_NS = 16
RELAY = 10
RIM_S = 2 * MOVED * TILE
RIM_Q = RIM_S + 16
RIM_M = RIM_Q + 16
SURF = RIM_M + 16
MESSAGE = SURF + FIELD_TILES * TILE
F32 = jnp.float32
SMEM = pl.BlockSpec(memory_space=pltpu.SMEM)
VMEM = pl.BlockSpec(memory_space=pltpu.VMEM)
ANY = pl.BlockSpec(memory_space=pl.ANY)


def lane_id(shape):
    return lax.broadcasted_iota(jnp.int32, shape, len(shape) - 1)


def turn(x, by, axis):
    size = x.shape[axis]
    if isinstance(by, int):
        by = by % size
        if by == 0:
            return x
    return pltpu.roll(x, by, axis)


def swap(to_next, to_last, axis, count):
    first = [(i, i ^ 1) for i in range(count)]
    second = [(i, (i + 1) % count if i % 2 else (i - 1) % count) for i in range(count)]
    return lax.ppermute(to_next, axis, first), lax.ppermute(to_last, axis, second)


def shifted(x, axis, by):
    length = lax.axis_size(axis)
    return lax.ppermute(x, axis, [(i, (i + by) % length) for i in range(length)])


def fill_places(code_ref, inv, slots):
    def clear(r, carry):
        inv[r] = -1
        return carry

    def place(s, carry):
        inv[code_ref[s]] = s
        return carry

    lax.fori_loop(0, 2 * REGION, clear, 0)
    lax.fori_loop(0, slots, place, 0)


def sums_kernel(meta, code, weight, diffusion, t_ref, low_ref, high_ref, s_ref, q_ref, a_ref, b_ref, far_ref, inv, part):
    step = pl.program_id(0)
    slots = s_ref.shape[0] // TILE
    tracer = lax.broadcasted_iota(jnp.int32, (TILE, LANES), 0) % 2
    pairs = [(n, h) for n in range(STEP_SLOTS) for h in range(2)]
    acc_s = {p: jnp.zeros((TILE, LANES), F32) for p in pairs}
    acc_q = {p: jnp.zeros((TILE, LANES), F32) for p in pairs}
    for level in range(LEVELS):
        w = jnp.where(tracer == 0, weight[0, level], weight[1, level])
        wd = w * diffusion[level]
        for n, h in pairs:
            x = t_ref[n, level, pl.ds(h * TILE, TILE), :]
            acc_s[n, h] = acc_s[n, h] + w * x
            acc_q[n, h] = acc_q[n, h] + wd * x
    for n, h in pairs:
        part[0, pl.ds(n * ROWS + h * TILE, TILE), :] = acc_s[n, h]
        part[1, pl.ds(n * ROWS + h * TILE, TILE), :] = acc_q[n, h]
    for n in range(STEP_SLOTS):
        row = pl.multiple_of((step * STEP_SLOTS + n) * TILE, TILE)
        for kind, out in ((0, s_ref), (1, q_ref)):
            even = part[kind, pl.ds(n * ROWS, TILE, stride=2), :]
            odd = part[kind, pl.ds(n * ROWS + 1, TILE, stride=2), :]
            out[pl.ds(row, TILE), :] = even + odd

    @pl.when(step == 0)
    def _():
        fill_places(code, inv, slots)

    def rim(dest, base, first, chunk):
        for k in range(REG_X):
            src = inv[first + k]
            at = jnp.maximum(src, 0) * TILE + chunk
            has = jnp.where(src >= 0, 1.0, 0.0)
            dest[pl.ds(base + k, 1), :] = jnp.where(src >= 0, s_ref[pl.ds(at, 1), :], 0.0)
            dest[pl.ds(base + 16 + k, 1), :] = jnp.where(src >= 0, q_ref[pl.ds(at, 1), :], 0.0)
            dest[pl.ds(base + 32 + k, 1), :] = jnp.full((1, LANES), has, F32)
        for k in range(REG_X, 16):
            for kind in range(3):
                dest[pl.ds(base + 16 * kind + k, 1), :] = jnp.zeros((1, LANES), F32)

    def surface(dest, edge):
        for b in range(FIELD_TILES):
            if b < 3:
                dest[pl.ds(SURF + b * TILE, TILE), :] = edge[:, pl.ds(b * LANES, LANES)]
            else:
                width = edge.shape[1] - b * LANES
                dest[pl.ds(SURF + b * TILE, TILE), :] = jnp.zeros((TILE, LANES), F32)
                dest[pl.ds(SURF + b * TILE, TILE), pl.ds(0, width)] = edge[:, pl.ds(b * LANES, width)]

    def messages(up, down):
        height = MOVED * TILE
        first = (slots - MOVED) * TILE
        up[pl.ds(0, height), :] = s_ref[pl.ds(first, height), :]
        up[pl.ds(height, height), :] = q_ref[pl.ds(first, height), :]
        rim(up, RIM_S, REGION - REG_X, TILE - 1)
        surface(up, high_ref)
        down[pl.ds(0, 2 * height), :] = jnp.zeros((2 * height, LANES), F32)
        rim(down, RIM_S, 0, 0)
        surface(down, low_ref)

    @pl.when(step == pl.num_programs(0) - 1)
    def _():
        rim(far_ref, 0, 2 * REGION - REG_X, TILE - 1)

        @pl.when(meta[1] % 2 == 0)
        def _():
            messages(a_ref, b_ref)

        @pl.when(meta[1] % 2 == 1)
        def _():
            messages(b_ref, a_ref)


def depth_sums(view, meta, code, weight, diffusion, surface):
    slots = view.shape[0]
    steps = slots // STEP_SLOTS
    rows, width = surface.shape
    whole = lambda *shape: pl.BlockSpec(shape, lambda s: (0,) * len(shape))
    return pl.pallas_call(
        sums_kernel,
        grid=(steps,),
        in_specs=[
            SMEM,
            SMEM,
            SMEM,
            SMEM,
            pl.BlockSpec((STEP_SLOTS, LEVELS, ROWS, LANES), lambda s: (s, 0, 0, 0)),
            pl.BlockSpec((TILE, width), lambda s: (0, 0)),
            pl.BlockSpec((TILE, width), lambda s: (rows // TILE - 1, 0)),
        ],
        out_specs=[
            whole(slots * TILE, LANES),
            whole(slots * TILE, LANES),
            whole(MESSAGE, LANES),
            whole(MESSAGE, LANES),
            whole(48, LANES),
        ],
        out_shape=[
            jax.ShapeDtypeStruct((slots * TILE, LANES), F32),
            jax.ShapeDtypeStruct((slots * TILE, LANES), F32),
            jax.ShapeDtypeStruct((MESSAGE, LANES), F32),
            jax.ShapeDtypeStruct((MESSAGE, LANES), F32),
            jax.ShapeDtypeStruct((48, LANES), F32),
        ],
        scratch_shapes=[
            pltpu.SMEM((2 * REGION,), jnp.int32),
            pltpu.VMEM((2, STEP_SLOTS * ROWS, LANES), F32),
        ],
        compiler_params=pltpu.CompilerParams(vmem_limit_bytes=12 << 20),
        name="depth_sums",
    )(meta, code, weight, diffusion, view, surface, surface)


def field_kernel(meta, code, came, s_ref, q_ref, a_ref, b_ref, far_ref, surf_ref, f_ref, ca_ref, cb_ref, inv):
    slots = s_ref.shape[0] // TILE
    even = meta[1] % 2 == 0
    group = lane_id((TILE, LANES)) // BLOCK
    fill_places(code, inv, slots)

    def place_came(k, carry):
        r = came[slots - MOVED + k] - REGION

        @pl.when(r >= 0)
        def _():
            inv[r] = slots + k

        return carry

    lax.fori_loop(0, MOVED, place_came, 0)

    def below(start, size):
        return jnp.where(even, b_ref[pl.ds(start, size), :], a_ref[pl.ds(start, size), :])

    def above(start, size):
        return jnp.where(even, a_ref[pl.ds(start, size), :], b_ref[pl.ds(start, size), :])

    f_ref[...] = jnp.zeros(f_ref.shape, F32)
    for by in range(REG_Y):
        for b in range(FIELD_TILES):
            held = [g for g in range(4) if 4 * b + g < REG_X]
            mask = jnp.zeros((TILE, LANES), F32)
            tiles = {}
            for g in held:
                src = inv[by * REG_X + 4 * b + g]
                own_at = pl.multiple_of(jnp.clip(src, 0, slots - 1) * TILE, TILE)
                came_at = pl.multiple_of(jnp.clip(src - slots, 0, MOVED - 1) * TILE, TILE)
                for kind, ref in ((0, s_ref), (1, q_ref)):
                    own = ref[pl.ds(own_at, TILE), :]
                    other = below(pl.multiple_of(kind * MOVED * TILE + came_at, TILE), TILE)
                    tiles[kind, g] = jnp.where(src >= slots, other, jnp.where(src >= 0, own, 0.0))
                mask = jnp.where(group == g, jnp.where(src >= 0, 1.0, 0.0), mask)
            for kind in range(2):
                for q in range(4):
                    value = jnp.zeros((TILE, LANES), F32)
                    for g in held:
                        value = jnp.where(group == g, turn(tiles[kind, g], BLOCK * (g - q), 1), value)
                    f_ref[kind, b, pl.ds(TILE + BLOCK * by + q, TILE, stride=4), :] = value
            for q in range(4):
                f_ref[2, b, pl.ds(TILE + BLOCK * by + TILE * q, TILE), :] = mask

    row16 = lax.broadcasted_iota(jnp.int32, (16, LANES), 0)
    group16 = lane_id((16, LANES)) // BLOCK

    def rim_rows(kind, rim, first):
        rolled = [turn(rim, BLOCK * d, 1) for d in range(4)]
        for q in range(4):
            value = jnp.zeros((16, LANES), F32)
            for g in range(4):
                value = jnp.where((row16 % 4 == g) & (group16 == g), rolled[(g - q) % 4], value)
            value = value + turn(value, -1, 0)
            value = value + turn(value, -2, 0)
            for b in range(FIELD_TILES):
                f_ref[kind, b, pl.ds(first + q, 1), :] = value[4 * b : 4 * b + 1, :]

    @pl.when(meta[1] > 0)
    def _():
        for kind, base in ((0, RIM_S), (1, RIM_Q), (2, RIM_M)):
            rim_rows(kind, below(base, 16) + far_ref[pl.ds(base - RIM_S, 16), :], 4)

    @pl.when(meta[1] < meta[2] - 1)
    def _():
        def own_rim(ref):
            rows = []
            for k in range(16):
                if k < REG_X:
                    src = inv[REGION + k]
                    at = jnp.maximum(src, 0) * TILE
                    line = jnp.ones((1, LANES), F32) if ref is None else ref[pl.ds(at, 1), :]
                    rows.append(jnp.where(src >= 0, line, 0.0))
                else:
                    rows.append(jnp.zeros((1, LANES), F32))
            return jnp.concatenate(rows, axis=0)

        for kind, base, ref in ((0, RIM_S, s_ref), (1, RIM_Q, q_ref), (2, RIM_M, None)):
            rim_rows(kind, above(base, 16) + own_rim(ref), FIELD_ROWS - TILE)

    height, width = surf_ref.shape
    for b in range(FIELD_TILES):
        lanes = min(LANES, width - b * LANES)
        f_ref[3, b, pl.ds(TILE, height), pl.ds(0, lanes)] = surf_ref[:, pl.ds(b * LANES, lanes)]
        f_ref[3, b, pl.ds(4, 4), :] = below(SURF + b * TILE, TILE)[4:]
        f_ref[3, b, pl.ds(FIELD_ROWS - TILE, 4), :] = above(SURF + b * TILE, TILE)[:4]

    lane = lane_id((TILE, LANES))
    last = width - (FIELD_TILES - 1) * LANES - 4
    east_even = meta[0] % 2 == 0
    for h in range(3):
        west_out = jnp.zeros((TILE, LANES), F32)
        east_out = jnp.zeros((TILE, LANES), F32)
        for g in range(8):
            v = 3 * g + h
            if v * TILE >= FIELD_ROWS:
                continue
            for kind in range(4):
                at = 16 * g + 4 * kind
                inside = (lane >= at) & (lane < at + 4)
                west = f_ref[kind, 0, pl.ds(v * TILE, TILE), :]
                east = f_ref[kind, FIELD_TILES - 1, pl.ds(v * TILE, TILE), :]
                west_out = jnp.where(inside, turn(west, at, 1), west_out)
                east_out = jnp.where(inside, turn(east, at - last, 1), east_out)
        ca_ref[pl.ds(h * TILE, TILE), :] = jnp.where(east_even, east_out, west_out)
        cb_ref[pl.ds(h * TILE, TILE), :] = jnp.where(east_even, west_out, east_out)


def region_fields(meta, code, came, s, q, a, b, far, surface):
    return pl.pallas_call(
        field_kernel,
        in_specs=[SMEM, SMEM, SMEM] + [VMEM] * 6,
        out_specs=[VMEM] * 3,
        out_shape=[
            jax.ShapeDtypeStruct((4, FIELD_TILES, FIELD_ROWS, LANES), F32),
            jax.ShapeDtypeStruct((24, LANES), F32),
            jax.ShapeDtypeStruct((24, LANES), F32),
        ],
        scratch_shapes=[pltpu.SMEM((2 * REGION,), jnp.int32)],
        compiler_params=pltpu.CompilerParams(vmem_limit_bytes=12 << 20),
        name="region_fields",
    )(meta, code, came, s, q, a, b, far, surface)


def basis_kernel(meta, f_ref, ca_ref, cb_ref, u_ref, g_ref):
    even = meta[0] % 2 == 0
    lane = lane_id((TILE, LANES))
    tiles = range(FIELD_TILES)
    fields = []
    for kind in range(4):
        parts = [f_ref[kind, b] for b in tiles]
        strip = []
        for v in range(FIELD_ROWS // TILE):
            g, h = v // 3, v % 3
            ca = ca_ref[pl.ds(h * TILE, TILE), :]
            cb = cb_ref[pl.ds(h * TILE, TILE), :]
            at = 16 * g + 4 * kind
            west = turn(jnp.where(even, cb, ca), 124 - at, 1)
            east = turn(jnp.where(even, ca, cb), 64 - at, 1)
            tile = f_ref[kind, FIELD_TILES - 1, pl.ds(v * TILE, TILE), :]
            tile = jnp.where((lane >= 64) & (lane < 68), east, tile)
            strip.append(jnp.where(lane >= 124, west, tile))
        parts[-1] = jnp.concatenate(strip, axis=0)
        fields.append(parts)
    depth, inner, mask, surf = fields
    wide = lane_id((FIELD_ROWS, LANES))

    def sides(v):
        fwd = [turn(x, 1, 1) for x in v]
        bwd = [turn(x, -1, 1) for x in v]
        out = []
        for b in tiles:
            left = jnp.where(wide == 0, fwd[b - 1], fwd[b])
            right = jnp.where(wide == LANES - 1, bwd[(b + 1) % FIELD_TILES], bwd[b])
            out.append(left + right)
        return out

    def rows(v):
        return [turn(x, 1, 0) + turn(x, -1, 0) for x in v]

    def spread(v):
        side = sides(v)
        both = rows([v[b] + 0.5 * side[b] for b in tiles])
        return [mask[b] * (side[b] + both[b]) for b in tiles]

    def edges(v):
        side, both = sides(v), rows(v)
        return [side[b] + both[b] for b in tiles]

    near, count = edges(inner), edges(mask)
    rhs = [mask[b] * (depth[b] + near[b] - count[b] * inner[b]) for b in tiles]
    scale = [1.0 / (6.0 + surf[b]) for b in tiles]
    u0 = [rhs[b] * scale[b] for b in tiles]
    z1 = spread(u0)
    u1 = [z1[b] * scale[b] for b in tiles]
    z2 = spread(u1)
    u2 = [z2[b] * scale[b] for b in tiles]
    z3 = spread(u2)
    rows_in = slice(TILE, FIELD_ROWS - TILE)

    def dot(x, y):
        total = jnp.zeros((TILE, LANES), F32)
        for b in tiles:
            p = x[b][rows_in] * y[b][rows_in]
            p = jnp.sum(p.reshape(-1, TILE, LANES), axis=0)
            if b == FIELD_TILES - 1:
                p = jnp.where(lane < 64, p, 0.0)
            total = total + p
        return jnp.sum(jnp.sum(total, axis=1, keepdims=True), axis=0, keepdims=True)

    row = jnp.zeros((1, LANES), F32)
    pairs = ((u0, rhs), (u0, z1), (u1, z1), (u1, z2), (u2, z2), (u2, z3))
    for k, (x, y) in enumerate(pairs):
        row = jnp.where(lane[:1] == k, dot(x, y), row)
    row = jnp.where(lane[:1] == 6, meta[3].astype(F32), row)
    g_ref[...] = jnp.broadcast_to(row, g_ref.shape)
    for k, u in enumerate((u0, u1, u2)):
        for b in tiles:
            u_ref[k, b] = u[b][rows_in]


def solve_basis(meta, fields, ca, cb, devices):
    return pl.pallas_call(
        basis_kernel,
        in_specs=[SMEM, VMEM, VMEM, VMEM],
        out_specs=[VMEM, VMEM],
        out_shape=[
            jax.ShapeDtypeStruct((3, FIELD_TILES, FIELD_ROWS - 2 * TILE, LANES), F32),
            jax.ShapeDtypeStruct((devices, LANES), F32),
        ],
        compiler_params=pltpu.CompilerParams(vmem_limit_bytes=24 << 20),
        name="solve_basis",
    )(meta, fields, ca, cb)


def solution_kernel(came, u_ref, g_ref, blocks_ref, back_ref, over_ref):
    total = jnp.sum(g_ref[...].reshape(-1, TILE, LANES), axis=0)
    total = jnp.broadcast_to(jnp.sum(total, axis=0, keepdims=True), (TILE, LANES))
    lane = lane_id((TILE, LANES))
    pick = lambda k: jnp.sum(jnp.where(lane == k, total, 0.0), axis=1, keepdims=True)
    over_ref[...] = jnp.broadcast_to(pick(6), (TILE, LANES))
    g = [pick(k) for k in range(6)]
    g = [x / g[0] for x in g]
    a = [g[k] - g[k + 1] for k in range(5)]
    zero = jnp.zeros_like(g[0])
    one = zero + 1.0

    def form(v, m):
        out = zero
        for i in range(3):
            for k in range(3):
                out = out + v[i] * v[k] * m[i + k]
        return out

    coef = [zero, zero, zero]
    rho = [one, zero, zero]
    way = [one, zero, zero]
    norm = g[0]
    for iteration in range(3):
        length = norm / form(way, a)
        coef = [coef[k] + length * way[k] for k in range(3)]
        if iteration < 2:
            moved = [way[0], way[1] - way[0], way[2] - way[1]]
            rho = [rho[k] - length * moved[k] for k in range(3)]
            norm_next = form(rho, g)
            way = [rho[k] + (norm_next / norm) * way[k] for k in range(3)]
            norm = norm_next
    coef = [jnp.broadcast_to(c, (TILE, LANES)) for c in coef]
    group = lane // BLOCK
    for by in range(REG_Y):
        for b in range(FIELD_TILES):
            value = []
            for q in range(4):
                at = pl.ds(BLOCK * by + q, TILE, stride=4)
                value.append(coef[0] * u_ref[0, b, at, :] + coef[1] * u_ref[1, b, at, :] + coef[2] * u_ref[2, b, at, :])
            for g4 in range(4):
                if 4 * b + g4 >= REG_X:
                    continue
                tile = jnp.zeros((TILE, LANES), F32)
                for q in range(4):
                    tile = jnp.where(group == q, turn(value[q], BLOCK * (q - g4), 1), tile)
                blocks_ref[pl.ds((by * REG_X + 4 * b + g4) * TILE, TILE), :] = tile
    first = came.shape[0] - MOVED
    for k in range(MOVED):
        at = pl.multiple_of(jnp.maximum(came[first + k] - REGION, 0) * TILE, TILE)
        back_ref[pl.ds(k * TILE, TILE), :] = blocks_ref[pl.ds(at, TILE), :]


def region_solution(came, u, g):
    return pl.pallas_call(
        solution_kernel,
        in_specs=[SMEM, VMEM, VMEM],
        out_specs=[VMEM] * 3,
        out_shape=[
            jax.ShapeDtypeStruct((REGION * TILE, LANES), F32),
            jax.ShapeDtypeStruct((MOVED * TILE, LANES), F32),
            jax.ShapeDtypeStruct((TILE, LANES), F32),
        ],
        compiler_params=pltpu.CompilerParams(vmem_limit_bytes=12 << 20),
        name="region_solution",
    )(came, u, g)


def pressure_kernel(code, blocks_ref, back_ref, out_ref, work):
    slots = out_ref.shape[0]
    for s in range(slots):
        c = code[s]
        at = pl.multiple_of(jnp.where(c < REGION, c, 0) * TILE, TILE)
        tile = blocks_ref[pl.ds(at, TILE), :]
        k = s - (slots - MOVED)
        if k >= 0:
            tile = jnp.where(c < REGION, tile, back_ref[pl.ds(k * TILE, TILE), :])
        work[pl.ds(s * TILE, TILE), :] = tile
    for first in range(0, slots, TILE):
        size = min(TILE, slots - first)
        for c in range(TILE):
            lines = work[pl.ds(first * TILE + c, size, stride=TILE), :]
            out_ref[pl.ds(first, size), pl.ds(c * LANES, LANES)] = lines


def slot_pressure(code, blocks, back):
    slots = code.shape[0]
    return pl.pallas_call(
        pressure_kernel,
        in_specs=[SMEM, VMEM, VMEM],
        out_specs=VMEM,
        out_shape=jax.ShapeDtypeStruct((slots, TILE * LANES), F32),
        scratch_shapes=[pltpu.VMEM((slots * TILE, LANES), F32)],
        compiler_params=pltpu.CompilerParams(vmem_limit_bytes=12 << 20),
        name="slot_pressure",
    )(code, blocks, back)


def columns_kernel(meta, code, t_ref, a_ref, b_ref, inv, west, east, sems):
    fill_places(code, inv, code.shape[0])
    even = meta[0] % 2 == 0
    count = 2 * REG_Y

    def copies(k):
        w, e = inv[REG_X * k], inv[REG_X * k + REG_X - 1]
        cw = pltpu.make_async_copy(t_ref.at[jnp.maximum(w, 0)], west.at[k], sems.at[0, k])
        ce = pltpu.make_async_copy(t_ref.at[jnp.maximum(e, 0)], east.at[k], sems.at[1, k])
        return cw, ce

    for k in range(count):
        for c in copies(k):
            c.start()
    for k in range(count):
        for c in copies(k):
            c.wait()
    column = lane_id((ROWS, LANES)) % BLOCK
    for level in range(HALF):
        out_w = jnp.zeros((ROWS, LANES), F32)
        out_e = jnp.zeros((ROWS, LANES), F32)
        for k in range(count):
            has_w, has_e = inv[REG_X * k] >= 0, inv[REG_X * k + REG_X - 1] >= 0
            for part in range(2):
                lane = k + 16 * part
                here = column == lane
                at = level + HALF * part
                out_w = jnp.where(here & has_w, turn(west[k, at], lane, 1), out_w)
                out_e = jnp.where(here & has_e, turn(east[k, at], lane - (BLOCK - 1), 1), out_e)
        a_ref[pl.ds(level * ROWS, ROWS), :] = jnp.where(even, out_e, out_w)
        b_ref[pl.ds(level * ROWS, ROWS), :] = jnp.where(even, out_w, out_e)


def column_strips(meta, code, view):
    count = 2 * REG_Y
    return pl.pallas_call(
        columns_kernel,
        in_specs=[SMEM, SMEM, ANY],
        out_specs=[VMEM] * 2,
        out_shape=[jax.ShapeDtypeStruct((HALF * ROWS, LANES), F32)] * 2,
        scratch_shapes=[
            pltpu.SMEM((2 * REGION,), jnp.int32),
            pltpu.VMEM((count, LEVELS, ROWS, LANES), F32),
            pltpu.VMEM((count, LEVELS, ROWS, LANES), F32),
            pltpu.SemaphoreType.DMA((2, count)),
        ],
        compiler_params=pltpu.CompilerParams(vmem_limit_bytes=12 << 20),
        name="column_strips",
    )(meta, code, view)


def links_kernel(meta, table, t_ref, ga_ref, gb_ref, a_ref, b_ref, whole, half, sem_we, sem_ns):
    even_x = meta[0] % 2 == 0
    even_y = meta[1] % 2 == 0

    def we_copy(way, k):
        link = jnp.maximum(table[way * (CAP_WE + CAP_NS) + k], 0)
        return pltpu.make_async_copy(t_ref.at[link // 4], whole.at[way, k], sem_we.at[way, k])

    def ns_copy(way, k):
        link = jnp.maximum(table[way * (CAP_WE + CAP_NS) + CAP_WE + k], 2)
        rows = pl.ds(pl.multiple_of((link % 4 - 2) * TILE, TILE), TILE)
        return pltpu.make_async_copy(t_ref.at[link // 4, :, rows, :], half.at[way, k], sem_ns.at[way, k])

    for way in range(2):
        for k in range(CAP_WE):
            @pl.when(table[way * (CAP_WE + CAP_NS) + k] >= 0)
            def _():
                we_copy(way, k).start()

        for k in range(CAP_NS):
            @pl.when(table[way * (CAP_WE + CAP_NS) + CAP_WE + k] >= 0)
            def _():
                ns_copy(way, k).start()

    column = lane_id((HALF * ROWS, LANES)) % 16
    from_west = jnp.where(even_x, gb_ref[...], ga_ref[...])
    from_east = jnp.where(even_x, ga_ref[...], gb_ref[...])
    ways = ((turn(from_west, -5, 1), from_east), (from_west, turn(from_east, 5, 1)))
    relays = [jnp.where(column < 5, w, jnp.where(column < RELAY, e, 0.0)) for w, e in ways]

    def message(way, out):
        out[pl.ds(0, HALF * ROWS), :] = relays[way]
        out[pl.ds(HALF * ROWS, LEVELS * TILE), :] = jnp.zeros((LEVELS * TILE, LANES), F32)
        lane32 = lane_id((ROWS, LANES)) % BLOCK
        for k in range(CAP_WE):
            link = table[way * (CAP_WE + CAP_NS) + k]

            @pl.when(link >= 0)
            def _():
                we_copy(way, k).wait()
                start = (link % 4) * (BLOCK - 1)
                for level in range(HALF):
                    at = pl.ds(level * ROWS, ROWS)
                    value = out[at, :]
                    for part in range(2):
                        lane = RELAY + k + 16 * part
                        x = turn(whole[way, k, level + HALF * part], lane, 1)
                        x = jnp.where(start > 0, turn(x, 1 - BLOCK, 1), x)
                        value = jnp.where(lane32 == lane, x, value)
                    out[at, :] = value

        row = lax.broadcasted_iota(jnp.int32, (LEVELS, TILE, LANES), 1)
        group = lane_id((LEVELS, TILE, LANES)) // BLOCK
        base = HALF * ROWS
        for k in range(CAP_NS):
            link = table[way * (CAP_WE + CAP_NS) + CAP_WE + k]

            @pl.when(link >= 0)
            def _():
                ns_copy(way, k).wait()
                x = half[way, k]

                def put(x):
                    keep = (row // 2 == k // 4) & (group == k % 4)
                    old = out[pl.ds(base, LEVELS * TILE), :].reshape(LEVELS, TILE, LANES)
                    new = jnp.where(keep, x, old)
                    out[pl.ds(base, LEVELS * TILE), :] = new.reshape(LEVELS * TILE, LANES)

                @pl.when(link % 4 == 2)
                def _():
                    put(turn(turn(x, 2 * (k // 4), 1), BLOCK * (k % 4), 2))

                @pl.when(link % 4 == 3)
                def _():
                    put(turn(turn(x, 2 * (k // 4) + 2, 1), BLOCK * (k % 4) + BLOCK, 2))

    @pl.when(even_y)
    def _():
        message(0, a_ref)
        message(1, b_ref)

    @pl.when(jnp.logical_not(even_y))
    def _():
        message(0, b_ref)
        message(1, a_ref)


def link_strips(meta, table, view, ga, gb):
    rows = HALF * ROWS + LEVELS * TILE
    return pl.pallas_call(
        links_kernel,
        in_specs=[SMEM, SMEM, ANY, VMEM, VMEM],
        out_specs=[VMEM] * 2,
        out_shape=[jax.ShapeDtypeStruct((rows, LANES), F32)] * 2,
        scratch_shapes=[
            pltpu.VMEM((2, CAP_WE, LEVELS, ROWS, LANES), F32),
            pltpu.VMEM((2, CAP_NS, LEVELS, TILE, LANES), F32),
            pltpu.SemaphoreType.DMA((2, CAP_WE)),
            pltpu.SemaphoreType.DMA((2, CAP_NS)),
        ],
        compiler_params=pltpu.CompilerParams(vmem_limit_bytes=12 << 20),
        name="link_strips",
    )(meta, table, view, ga, gb)


EXTRA = 7
TALL = 32
CHUNK = 4


def tracer_kernel(meta, table, need, diffusion, t_ref, ga_ref, gb_ref, ha_ref, hb_ref, out_ref, buf, seen, sems):
    step = pl.program_id(0)
    steps = pl.num_programs(0)
    slots = buf.shape[0] - EXTRA

    def fetch(c):
        src = t_ref.at[pl.ds(c * STEP_SLOTS, STEP_SLOTS)]
        dst = buf.at[pl.ds(c * STEP_SLOTS, STEP_SLOTS), :, pl.ds(TILE, ROWS), :]
        return pltpu.make_async_copy(src, dst, sems.at[c])

    @pl.when(step == 0)
    def _():
        for c in range(slots // STEP_SLOTS):
            fetch(c).start()
        seen[0] = 0
        even_x = meta[0] % 2 == 0
        even_y = meta[1] % 2 == 0

        def unfold(image, value):
            for level in range(HALF):
                x = value[level * ROWS : (level + 1) * ROWS]
                buf[image, level, pl.ds(TILE, ROWS), :] = x
                buf[image, level + HALF, pl.ds(TILE, ROWS), :] = turn(x, -16, 1)

        for level in range(LEVELS):
            buf[slots, level, pl.ds(TILE, ROWS), :] = jnp.zeros((ROWS, LANES), F32)
        unfold(slots + 1, jnp.where(even_x, gb_ref[...], ga_ref[...]))
        unfold(slots + 2, jnp.where(even_x, ga_ref[...], gb_ref[...]))
        folded = pl.ds(0, HALF * ROWS)
        unfold(slots + 3, jnp.where(even_y, hb_ref[folded, :], ha_ref[folded, :]))
        unfold(slots + 4, jnp.where(even_y, ha_ref[folded, :], hb_ref[folded, :]))
        for level in range(LEVELS):
            rows = pl.ds(HALF * ROWS + level * TILE, TILE)
            first, second = ha_ref[rows, :], hb_ref[rows, :]
            buf[slots + 5, level, pl.ds(TILE, TILE), :] = jnp.where(even_y, second, first)
            buf[slots + 6, level, pl.ds(TILE, TILE), :] = jnp.where(even_y, first, second)

    def arrive(c, carry):
        fetch(c).wait()
        return carry

    upto = jnp.maximum(seen[0], need[step] + 1)
    lax.fori_loop(seen[0], upto, arrive, 0)
    seen[0] = upto

    cells = (ROWS, LANES)
    lane = lane_id(cells)
    column = lane % BLOCK
    row = lax.broadcasted_iota(jnp.int32, cells, 0)
    edge = (
        jnp.where(column == 0, 1.0, 0.0),
        jnp.where(column == BLOCK - 1, 1.0, 0.0),
        jnp.where((row < 2) & (lane < BLOCK), 1.0, 0.0),
        jnp.where((row >= ROWS - 2) & (lane >= LANES - BLOCK), 1.0, 0.0),
    )

    def one_slot(n, carry):
        s = step * STEP_SLOTS + n
        entry = [[table[s * 16 + 4 * t + f] for f in range(4)] for t in range(4)]
        count = jnp.full(cells, 4.0, F32)
        for t in range(4):
            count = count - edge[t] * entry[t][3].astype(F32)
        for t, dest in ((2, TILE - 2), (3, TILE + ROWS)):
            image, at, by, _ = entry[t]
            line = buf[image, :, pl.ds(TILE + at, 2), :]
            buf[s, :, pl.ds(dest, 2), :] = pltpu.roll(line, by, 2)
        (west, _, by_west, _), (east, _, by_east, _) = entry[0], entry[1]
        shape = (CHUNK, ROWS, LANES)
        lane3 = lane_id(shape)
        column3 = lane3 % BLOCK
        for first in range(0, LEVELS, CHUNK):
            some = pl.ds(first, CHUNK)
            x = buf[s, some, pl.ds(TILE, ROWS), :]
            under = buf[s, some, pl.ds(TILE - 2, ROWS), :]
            over = buf[s, some, pl.ds(TILE + 2, ROWS), :]
            w = buf[west, some, pl.ds(TILE, ROWS), :]
            e = buf[east, some, pl.ds(TILE, ROWS), :]
            total = pltpu.roll(jnp.where(lane3 >= LANES - BLOCK, under, x), BLOCK, 2)
            total = total + pltpu.roll(jnp.where(lane3 < BLOCK, over, x), LANES - BLOCK, 2)
            total = total + jnp.where(column3 == 0, pltpu.roll(w, by_west, 2), pltpu.roll(x, 1, 2))
            total = total + jnp.where(column3 == BLOCK - 1, pltpu.roll(e, by_east, 2), pltpu.roll(x, LANES - 1, 2))
            for i in range(CHUNK):
                out_ref[n, first + i] = x[i] + diffusion[first + i] * (total[i] - count * x[i])
        return carry

    lax.fori_loop(0, STEP_SLOTS, one_slot, 0)

    @pl.when(step == steps - 1)
    def _():
        lax.fori_loop(seen[0], slots // STEP_SLOTS, arrive, 0)


def step_tracers(meta, table, need, diffusion, view, ga, gb, ha, hb):
    slots = view.shape[0]
    steps = slots // STEP_SLOTS
    shape = (STEP_SLOTS, LEVELS, ROWS, LANES)
    return pl.pallas_call(
        tracer_kernel,
        grid=(steps,),
        in_specs=[SMEM] * 4 + [ANY] + [VMEM] * 4,
        out_specs=pl.BlockSpec(shape, lambda s: (s, 0, 0, 0)),
        out_shape=jax.ShapeDtypeStruct(view.shape, F32),
        scratch_shapes=[
            pltpu.VMEM((slots + EXTRA, LEVELS, TALL, LANES), F32),
            pltpu.SMEM((1,), jnp.int32),
            pltpu.SemaphoreType.DMA((steps,)),
        ],
        compiler_params=pltpu.CompilerParams(vmem_limit_bytes=40 << 20),
        name="step_tracers",
    )(meta, table, need, diffusion, view, ga, gb, ha, hb)


def with_halo(block, sides, width):
    for axis, dim in sides:
        low = shifted(lax.slice_in_dim(block, block.shape[dim] - width, None, axis=dim), axis, 1)
        high = shifted(lax.slice_in_dim(block, 0, width, axis=dim), axis, -1)
        block = jnp.concatenate([low, block, high], axis=dim)
    return block


def edge_strips(grid):
    sides = [grid[..., :, 0], grid[..., :, -1], grid[..., 0, :], grid[..., -1, :]]
    return jnp.stack(sides, axis=1).reshape(grid.shape[0] * 4, -1)


def general_step(tracers, diffusion, halo_source):
    slots = tracers.shape[0]
    grid = tracers.reshape(slots, TRACER, LEVELS, BLOCK, BLOCK)
    strips = edge_strips(grid)
    width = strips.shape[1]
    count_gx, count_gy = lax.axis_size("gx"), lax.axis_size("gy")
    source = halo_source.reshape(-1)
    missing = source >= 4 * slots * count_gx * count_gy
    slot = jnp.where(missing, 0, source) // 4
    owner = slot // slots
    step_gx = (owner // count_gy - lax.axis_index("gx") + count_gx + 1) % count_gx
    step_gy = (owner % count_gy - lax.axis_index("gy") + count_gy + 1) % count_gy
    every = slots * 4
    table = with_halo(strips.reshape(1, 1, every, width), (("gx", 0), ("gy", 1)), 1).reshape(9 * every, width)
    index = (step_gx * 3 + step_gy) * every + slot % slots * 4 + source % 4
    halo = jnp.take(table, jnp.where(missing, 0, index), axis=0, mode="clip")
    halo = halo.reshape(slots, 4, TRACER, LEVELS, BLOCK)
    gate = jnp.where(missing, 0.0, 1.0).astype(F32).reshape(slots, 4, 1, 1, 1)
    inner_x = grid[..., :, :-1] - grid[..., :, 1:]
    inner_y = grid[..., :-1, :] - grid[..., 1:, :]
    west = (halo[:, 0] - grid[..., :, 0]) * gate[:, 0]
    east = (halo[:, 1] - grid[..., :, -1]) * gate[:, 1]
    south = (halo[:, 2] - grid[..., 0, :]) * gate[:, 2]
    north = (halo[:, 3] - grid[..., -1, :]) * gate[:, 3]
    laplace = (
        jnp.concatenate([west[..., None], inner_x], axis=-1)
        + jnp.concatenate([-inner_x, east[..., None]], axis=-1)
        + jnp.concatenate([south[..., None, :], inner_y], axis=-2)
        + jnp.concatenate([-inner_y, north[..., None, :]], axis=-2)
    )
    return (grid + diffusion[None, None, :, None, None] * laplace).reshape(tracers.shape)


def strip_tables(halo_source, code, at_x, at_y, count_x, count_y):
    slots = halo_source.shape[0]
    source = halo_source
    missing = source >= 4 * slots * count_x * count_y
    source = jnp.where(missing, 0, source)
    owner = source // (4 * slots)
    local_slot = source // 4 - owner * slots
    same_x = owner // count_y == at_x
    owner_y = owner % count_y
    up = owner_y == (at_y + 1) % count_y
    down = owner_y == (at_y + count_y - 1) % count_y
    here = owner_y == at_y
    side = lax.broadcasted_iota(jnp.int32, (slots, 4), 1)
    index = lax.broadcasted_iota(jnp.int32, (slots, 4), 0) * 4 + side
    kind = jnp.where(side >= 2, 1, 0)
    linked = ~missing & same_x & ~here
    group = jnp.where(linked, jnp.where(up, kind, 2 + kind), -1)

    def rank(key):
        flat_key, flat_group = key.reshape(-1), group.reshape(-1)
        before = (flat_key[None, :] < flat_key[:, None]) & (flat_group[None, :] == flat_group[:, None])
        return jnp.sum(before.astype(jnp.int32), axis=1).reshape(slots, 4)

    take = rank(index)
    give = rank(source)
    entries = []
    for way in range(2):
        entries += [(way * 2, k) for k in range(CAP_WE)] + [(way * 2 + 1, k) for k in range(CAP_NS)]
    want = jnp.asarray([g * 1024 + k for g, k in entries], jnp.int32)
    has = jnp.where(group >= 0, group * 1024 + give, -1).reshape(-1)
    hit = want[:, None] == has[None, :]
    send = jnp.sum(jnp.where(hit, index.reshape(-1)[None, :] + 1, 0), axis=1) - 1
    over = jnp.any(linked & (take >= jnp.where(kind == 1, CAP_NS, CAP_WE)))
    row = (code // REG_X)[:, None]
    land, west, east, we_low, we_high, ns_low, ns_high = [slots + k for k in range(EXTRA)]
    local = same_x & here
    beside = jnp.where(here, jnp.where(side == 0, west, east), jnp.where(up, we_high, we_low))
    beside_lane = jnp.where(here, row, row % REG_Y + jnp.where(side == 0, 0, REG_Y))
    lane = jnp.where(same_x, RELAY + take, beside_lane)
    image_we = jnp.where(local, local_slot, jnp.where(same_x, jnp.where(up, we_high, we_low), beside))
    by_we = jnp.where(side == 0, -jnp.where(local, BLOCK - 1, lane), BLOCK - 1 - jnp.where(local, 0, lane))
    image_ns = jnp.where(local, local_slot, jnp.where(up, ns_high, ns_low))
    row_ns = jnp.where(local, jnp.where(side == 2, ROWS - 2, 0), 2 * (take // 4))
    by_ns = jnp.where(local, 0, jnp.where(side == 2, LANES - BLOCK, 0) - BLOCK * (take % 4))
    north = kind == 1
    image = jnp.where(missing, land, jnp.where(north, image_ns, image_we))
    at = jnp.where(missing | ~north, 0, jnp.minimum(row_ns, ROWS - 2))
    by = jnp.where(missing, 0, jnp.where(north, by_ns, by_we)) % LANES
    table = jnp.stack([image, at, by, missing.astype(jnp.int32)], axis=-1).reshape(-1)
    last = jnp.where(local & ~missing, local_slot, 0)
    last = jnp.maximum(jnp.max(last, axis=1), jnp.arange(slots))
    need = jnp.max(last.reshape(-1, STEP_SLOTS), axis=1) // STEP_SLOTS
    return table, need, send, over.astype(jnp.int32)


def on_device(tracers, diffusion, layer_weight, surface_term, clinic_blocks, halo_source):
    slots = tracers.shape[0]
    count_x, count_y = lax.axis_size("gx"), lax.axis_size("gy")
    at_x, at_y = lax.axis_index("gx"), lax.axis_index("gy")
    grid_columns = REG_X * count_x
    grid_rows = REG_Y * count_y
    own_row = (clinic_blocks // grid_columns - REG_Y * at_y) % grid_rows
    code = own_row * REG_X + clinic_blocks % grid_columns % REG_X
    came = shifted(code, "gy", 1)
    zero = jnp.zeros((), jnp.int32)
    meta = jnp.stack([at_x, at_y, zero + count_y, zero]).astype(jnp.int32)

    view = tracers.reshape(slots, TRACER, LEVELS, TILE, LANES).transpose(0, 2, 3, 1, 4)
    view = view.reshape(slots, LEVELS, ROWS, LANES)
    s, q, a, b, far = depth_sums(view, meta, code, layer_weight, diffusion, surface_term)
    ra, rb = swap(a, b, "gy", count_y)
    rfar = shifted(far, "gy", 2)

    table, need, send, over = strip_tables(halo_source, code, at_x, at_y, count_x, count_y)
    ga, gb = swap(*column_strips(meta, code, view), "gx", count_x)

    fields, ca, cb = region_fields(meta, code, came, s, q, ra, rb, rfar, surface_term)
    ca, cb = swap(ca, cb, "gx", count_x)
    ha, hb = swap(*link_strips(meta, send, view, ga, gb), "gy", count_y)

    meta_over = jnp.stack([at_x, at_y, zero + count_y, over]).astype(jnp.int32)
    u, sums = solve_basis(meta_over, fields, ca, cb, count_x * count_y)
    sums = lax.all_to_all(sums, ("gx", "gy"), 0, 0, tiled=True)
    blocks, back, total_over = region_solution(came, u, sums)
    back = shifted(back, "gy", -1)

    updated = step_tracers(meta, table, need, diffusion, view, ga, gb, ha, hb)
    updated = updated.reshape(slots, LEVELS, TILE, TRACER, LANES).transpose(0, 3, 1, 2, 4)
    updated = updated.reshape(tracers.shape)
    pressure = slot_pressure(code, blocks, back)
    updated = lax.cond(
        total_over[0, 0] > 0,
        lambda fast: general_step(tracers, diffusion, halo_source),
        lambda fast: fast,
        updated,
    )
    return (updated, pressure)


def solution(mesh):
    placed = (
        P(("gx", "gy"), None, None, None),
        P(),
        P(),
        P("gy", "gx"),
        P(("gx", "gy")),
        P(("gx", "gy"), None),
    )
    return jax.shard_map(
        on_device,
        mesh=mesh,
        in_specs=placed,
        out_specs=(P(("gx", "gy"), None, None, None), P(("gx", "gy"), None)),
        check_vma=False,
    )
```

time: 633 us -> 139 us (0.22)
  blocking collectives: 205 us -> 0 us
  waiting for transfers between devices: 171 us -> 11.6 us
  local copies, waits for them, and re-layouts: 154 us -> 41.6 us
  Pallas kernels: 0 us -> 60.9 us
  other arithmetic: 56.5 us -> 2.72 us
  starting transfers between devices: 35.9 us -> 18.6 us
    psum x5 -> x0, blocking collectives: 205 us -> none  [the longest x3 122 us: norm_total(): return lax.psum(jnp.sum(residual * precond), ('gx', 'gy'))]
    ppermute x16 -> x8, waiting for transfers between devices: 157 us -> 4.58 us  [the longest x4 4.57 us: swap(): lax.ppermute(to_next, axis, first)]
    pallas_call x0 -> x8, Pallas kernels: none -> 60.9 us  [the longest x1 31.5 us: step_tracers(): pl.pallas_call(tracer_kernel, grid=(steps,), in_specs=[SMEM] * 4 + [ANY]...]
    reduce_sum x7 -> x2, other arithmetic: 49.2 us -> 0.47 us  [the longest x1 0.29 us: rank(): return jnp.sum(before.astype(jnp.int32), axis=1).reshape(slots, 4)]
    slice x6 -> x1, local copies, waits for them, and re-layouts: 48.1 us -> 0.51 us  [on_device(): total_over[0, 0] > 0]
    unnamed x29 -> x15, local copies, waits for them, and re-layouts: 43 us -> 0.14 us
    cond x0 -> x1, local copies, waits for them, and re-layouts: none -> 20 us
    another operation x6 -> x1, local copies, waits for them, and re-layouts: 18.7 us -> 0.5 us  [strip_tables(): jnp.stack([image, at, by, missing.astype(jnp.int32)], axis=-1).reshape(-1)]
  transfers between devices with their start and end apart: 19 -> 12, of which waited for: 12 -> 2; matrix products, arithmetic and copies ran while one was open for 25% -> 32% of each run, Pallas kernels for 0% -> 43%
where the time goes in v1:
time: 139 us; the launch traced here: 138 us
  Pallas kernels  60.9 us (44%)
  local copies, waits for them, and re-layouts  41.6 us (30%)
  starting transfers between devices  18.6 us (13%)
  waiting for transfers between devices  11.6 us (8%)
  other arithmetic  2.72 us (2%)
  between operations  2.25 us (2%)
    pallas_call x1, Pallas kernels, step_tracers(): pl.pallas_call(tracer_kernel, grid=(steps,), in_specs=[SMEM] * 4 + [ANY]...  31.5 us
    cond x1, local copies, waits for them, and re-layouts  20 us
    reshape x1, local copies, waits for them, and re-layouts, on_device(): updated = updated.reshape(tracers.shape)  15 us
    pallas_call x1, Pallas kernels, depth_sums(): pl.pallas_call(sums_kernel, grid=(steps,), in_specs=[SMEM, SMEM, SMEM, SM...  9.12 us
    all_to_all x1, waiting for transfers between devices, on_device(): sums = lax.all_to_all(sums, ('gx', 'gy'), 0, 0, tiled=True)  7.02 us
    ppermute x4, starting transfers between devices, swap(): lax.ppermute(to_last, axis, second)  6.51 us
    ppermute x3, starting transfers between devices, shifted(): lax.ppermute(x, axis, [(i, (i + by) % length) for i in range(length)])  5.69 us
    pallas_call x1, Pallas kernels, column_strips(): pl.pallas_call(columns_kernel, in_specs=[SMEM, SMEM, ANY], out_specs=[VME...  5.61 us
  transfers between devices with their start and end apart: 12, of which 2 were waited for; matrix products, arithmetic and copies ran while one was open for 32% of the time, Pallas kernels for 43%

profile of v1, /device:TPU:0, one launch (start us, length us, event | category | flops | bytes accessed | tf_op | source)
XLA Modules:
  0.0 137.7 jit_solution(1139138970647259430)
XLA Ops:
  0.6 0.0 copy-start.7
  0.6 0.0 copy-start
  0.7 0.0 copy-start.3
  0.7 0.8 and_select_fusion.9
  1.4 3.0 %collective-permute-start.4 = (s32[63]{0:T(128)S(1)}, s32[63]{0:T(128)S(1)}, u32[]{:S(2)}, u32[]{:S(2)}) collective-permute-start(s32[63]{0:T(128)S(1)} %get-tuple-element.87.code), channel_id=1, source_target_pairs={{0,1},{1,2},{2,3},{3,4},{4,5},{5,6},{6,7},{7,0},{8,9},{9,10},{10,1... | collective-permute-start | bytes 764 | tf_op jit(solution)/shard_map/ppermute | solution.py:57
  4.4 0.1 pad_add_fusion.3
  4.5 5.6 %column_strips.1 = (f32[160,128]{1,0:T(8,128)S(1)}, f32[160,128]{1,0:T(8,128)S(1)}) custom-call(s32[4]{0:T(128)S(1)} %get-tuple-element.88.meta, s32[63]{0:T(128)S(1)} %get-tuple-element.87.code, f32[63,20,16,128]{3,2,1,0:T(8,128)} %bitcast.85), custom_call_target="tpu_custom_call" | custom-call | tf_op jit(solution)/shard_map/column_strips/pallas_call | solution.py:537
  10.1 0.1 collective-permute-start.10
  10.2 9.1 %depth_sums.1 = (f32[504,128]{1,0:T(8,128)S(1)}, f32[504,128]{1,0:T(8,128)S(1)}, f32[432,128]{1,0:T(8,128)S(1)}, f32[432,128]{1,0:T(8,128)S(1)}, f32[48,128]{1,0:T(8,128)S(1)}) custom-call(s32[4]{0:T(128)S(1)} %get-tuple-element.88.meta, s32[63]{0:T(128)S(1)} %get-tuple-element.87.code, f32[2,20]{1,0:T(2,128)S(1)} %copy-done.3, f32[20]{0:T(128)S(1)} %copy-done.7, ...), custom_call_target="tpu_custom_call" | custom-call | tf_op jit(solution)/shard_map/depth_sums/pallas_call | solution.py:151
  19.4 2.1 %collective-permute-start.7 = (f32[48,128]{1,0:T(8,128)S(1)}, f32[48,128]{1,0:T(8,128)S(1)}, u32[]{:S(2)}, u32[]{:S(2)}) collective-permute-start(f32[48,128]{1,0:T(8,128)S(1)} %get-tuple-element.38), channel_id=1, source_target_pairs={{0,2},{1,3},{2,4},{3,5},{4,6},{5,7},{6,0},{7,1},{8,10},{9,11},{10,... | collective-permute-start | bytes 73736 | tf_op jit(solution)/shard_map/ppermute | solution.py:57
  21.4 1.4 %collective-permute-start.5 = (f32[432,128]{1,0:T(8,128)S(1)}, f32[432,128]{1,0:T(8,128)S(1)}, u32[]{:S(2)}, u32[]{:S(2)}) collective-permute-start(f32[432,128]{1,0:T(8,128)S(1)} %get-tuple-element.36), channel_id=1, source_target_pairs={{0,1},{1,0},{2,3},{3,2},{4,5},{5,4},{6,7},{7,6},{8,9},{9,8},{10,11... | collective-permute-start | bytes 663560 | tf_op jit(solution)/shard_map/ppermute | solution.py:52
  22.8 1.9 %collective-permute-start.6 = (f32[432,128]{1,0:T(8,128)S(1)}, f32[432,128]{1,0:T(8,128)S(1)}, u32[]{:S(2)}, u32[]{:S(2)}) collective-permute-start(f32[432,128]{1,0:T(8,128)S(1)} %get-tuple-element.37), channel_id=1, source_target_pairs={{0,7},{1,2},{2,1},{3,4},{4,3},{5,6},{6,5},{7,0},{8,15},{9,10},{10,... | collective-permute-start | bytes 663560 | tf_op jit(solution)/shard_map/ppermute | solution.py:52
  24.8 0.1 iota_add_fusion
  24.8 0.1 add.276
  25.0 0.0 copy-done.6
  25.0 0.1 copy.98
  25.1 0.2 select_reduce_fusion.1
  25.3 0.1 lt.101
  25.4 0.1 fusion.24
  25.5 0.1 eq.107
  25.6 0.3 convert_reduce_fusion
  25.9 0.1 reshape.443
  26.1 0.1 eq.115
  26.2 0.0 copy-done.10
  26.2 0.2 select_reduce_fusion
  26.4 0.1 reshape.439
  26.5 0.6 and_reduce_fusion
  27.8 0.1 fusion.29
  27.9 0.1 pad_add_fusion.1.meta
  28.0 0.1 reduce_max.21
  28.1 0.0 collective-permute-done.4.came
  28.1 1.1 collective-permute-start.11
  29.1 0.0 collective-permute-done.7.far_ref
  29.1 4.6 %collective-permute-done.5.a_ref = f32[432,128]{1,0:T(8,128)S(1)} collective-permute-done((f32[432,128]{1,0:T(8,128)S(1)}, f32[432,128]{1,0:T(8,128)S(1)}, u32[]{:S(2)}, u32[]{:S(2)}) %collective-permute-start.5) | collective-permute-done | bytes 221216 | tf_op jit(solution)/shard_map/ppermute | solution.py:52
  33.7 0.0 collective-permute-done.6.b_ref
  33.7 0.0 copy-done.1
  33.7 3.2 %region_fields.1 = (f32[4,4,176,128]{3,2,1,0:T(8,128)S(1)}, f32[24,128]{1,0:T(8,128)S(1)}, f32[24,128]{1,0:T(8,128)S(1)}) custom-call(s32[4]{0:T(128)S(1)} %get-tuple-element.88.meta, s32[63]{0:T(128)S(1)} %get-tuple-element.87.code, s32[63]{0:T(128)S(1)} %collective-permute-done.4.came, f32[504,128]{1,0:T(8,128)S(1)} %get-tuple-element.34.s_ref, ...), custom_call_target="tpu_custom_call" | custom-call | tf_op jit(solution)/shard_map/region_fields/pallas_call | solution.py:298
  36.9 0.1 collective-permute-start.8
  37.0 1.6 %collective-permute-start.9 = (f32[24,128]{1,0:T(8,128)S(1)}, f32[24,128]{1,0:T(8,128)S(1)}, u32[]{:S(2)}, u32[]{:S(2)}) collective-permute-start(f32[24,128]{1,0:T(8,128)S(1)} %get-tuple-element.41), channel_id=1, source_target_pairs={{0,24},{8,16},{16,8},{24,0},{1,25},{9,17},{17,9},{25,1},{2,26},{10... | collective-permute-start | bytes 36872 | tf_op jit(solution)/shard_map/ppermute | solution.py:52
  38.6 0.1 maximum_reduce_fusion
  38.7 0.0 collective-permute-done.10.ga_ref
  38.7 0.0 collective-permute-done.11.gb_ref
  38.7 5.1 %link_strips.1 = (f32[320,128]{1,0:T(8,128)S(1)}, f32[320,128]{1,0:T(8,128)S(1)}) custom-call(s32[4]{0:T(128)S(1)} %get-tuple-element.88.meta, s32[44]{0:T(128)S(1)} %broadcast_add_fusion.1.table, f32[63,20,16,128]{3,2,1,0:T(8,128)} %bitcast.87, f32[160,128]{1,0:T(8,128)S(1)} %collective-permute-done.10.ga_ref, f32[160,128]{1,0:T(8,128)S(1)} %collective-permute-done.11.gb_ref), custom_call_target="tpu_custom_call" | custom-call | tf_op jit(solution)/shard_map/link_strips/pallas_call | solution.py:642
  43.9 1.8 %collective-permute-start.12 = (f32[320,128]{1,0:T(8,128)S(1)}, f32[320,128]{1,0:T(8,128)S(1)}, u32[]{:S(2)}, u32[]{:S(2)}) collective-permute-start(f32[320,128]{1,0:T(8,128)S(1)} %get-tuple-element.47), channel_id=1, source_target_pairs={{0,1},{1,0},{2,3},{3,2},{4,5},{5,4},{6,7},{7,6},{8,9},{9,8},{10,11... | collective-permute-start | bytes 491528 | tf_op jit(solution)/shard_map/ppermute | solution.py:52
  45.7 2.0 %collective-permute-start.13 = (f32[320,128]{1,0:T(8,128)S(1)}, f32[320,128]{1,0:T(8,128)S(1)}, u32[]{:S(2)}, u32[]{:S(2)}) collective-permute-start(f32[320,128]{1,0:T(8,128)S(1)} %get-tuple-element.48), channel_id=1, source_target_pairs={{0,7},{1,2},{2,1},{3,4},{4,3},{5,6},{6,5},{7,0},{8,15},{9,10},{10,... | collective-permute-start | bytes 491528 | tf_op jit(solution)/shard_map/ppermute | solution.py:52
  47.7 0.0 collective-permute-done.8.ca_ref
  47.7 0.0 collective-permute-done.9.cb_ref
  47.7 3.0 %solve_basis.1 = (f32[3,4,160,128]{3,2,1,0:T(8,128)S(1)}, f32[32,128]{1,0:T(8,128)}) custom-call(s32[4]{0:T(128)S(1)} %pad_add_fusion.1.meta, f32[4,4,176,128]{3,2,1,0:T(8,128)S(1)} %get-tuple-element.39.f_ref, f32[24,128]{1,0:T(8,128)S(1)} %collective-permute-done.8.ca_ref, f32[24,128]{1,0:T(8,128)S(1)} %collective-permute-done.9.cb_ref), custom_call_target="tpu_custom_call" | custom-call | tf_op jit(solution)/shard_map/solve_basis/pallas_call | solution.py:391
  50.6 3.1 %all-to-all-start = ((f32[32,1,128]{2,1,0:T(1,128)}), f32[32,1,128]{2,1,0:T(1,128)S(1)}, u32[]{:S(2)}, u32[]{:S(2)}) async-start(f32[32,1,128]{2,1,0:T(1,128)} %bitcast.27), calls=%async_computation | async-start | bytes 32768 | tf_op jit(solution)/shard_map/all_to_all | solution.py:903
  53.8 7.0 %all-to-all-done = f32[32,1,128]{2,1,0:T(1,128)S(1)} async-done(((f32[32,1,128]{2,1,0:T(1,128)}), f32[32,1,128]{2,1,0:T(1,128)S(1)}, u32[]{:S(2)}, u32[]{:S(2)}) %all-to-all-start) | async-done | bytes 16416 | tf_op jit(solution)/shard_map/all_to_all | solution.py:903
  60.8 1.7 %region_solution.1 = (f32[560,128]{1,0:T(8,128)S(1)}, f32[176,128]{1,0:T(8,128)}, f32[8,128]{1,0:T(8,128)S(1)}) custom-call(s32[63]{0:T(128)S(1)} %collective-permute-done.4.came, f32[3,4,160,128]{3,2,1,0:T(8,128)S(1)} %get-tuple-element.42.u_ref, f32[32,128]{1,0:T(8,128)S(1)} %bitcast.78), custom_call_target="tpu_custom_call" | custom-call | tf_op jit(solution)/shard_map/region_solution/pallas_call | solution.py:458
  62.4 0.6 collective-permute-start.14
  63.1 0.5 copy.102
  63.6 0.2 reshape.442.table
  63.7 0.0 collective-permute-done.12.ha_ref
  63.8 0.0 collective-permute-done.13.hb_ref
  63.8 31.5 %step_tracers.1 = f32[63,20,16,128]{3,2,1,0:T(8,128)S(1)} custom-call(s32[4]{0:T(128)S(1)} %get-tuple-element.88.meta, s32[1008]{0:T(1024)S(1)} %reshape.442.table, s32[9]{0:T(128)S(1)} %and_select_fusion.8.need, f32[20]{0:T(128)S(1)} %copy-done.7, f32[63,20,16,128]{3,2,1,0:T(8,128)} %bitcast.88, f32[160,128]{1,0:T(8,128)S(1)} %collective-permute-done.10.ga_ref, ...), custom_call_target="tpu_custom_call" | custom-call | tf_op jit(solution)/shard_map/step_tracers/pallas_call | solution.py:759
  95.2 4.6 %copy.119 = f32[63,20,8,2,128]{4,2,0,1,3:T(8,128)} copy(f32[63,20,8,2,128]{4,3,2,1,0:T(2,128)S(1)} %bitcast.77) | data formatting | bytes 20643840 | tf_op jit(solution)/shard_map/reshape | solution.py:908
  99.9 0.5 slice.55
  101.0 35.0 %conditional.1 = (f32[63,2,20,1024]{3,1,2,0:T(2,128)}) conditional(s32[]{:T(128)} %bitcast.29, f32[63,2,20,8,128]{4,3,0,2,1:T(8,128)} %bitcast.90, (f32[20]{0:T(128)S(1)}, f32[63,2,20,1024]{3,1,2,0:T(2,128)}, s32[63,4]{0,1:T(4,128)S(1)}) %tuple.55), branch_computations={%region_6.7_spmd, %region_7.8_spmd} | conditional | flops 40667276 | bytes 352335744 | solution.py:911
  101.0 15.0 %copy.108 = f32[63,2,20,8,128]{0,4,3,2,1:T(8,128)} copy(f32[63,2,20,8,128]{4,3,0,2,1:T(8,128)} %param) | data formatting | bytes 20643840 | tf_op jit(solution)/shard_map/reshape | solution.py:909
  116.0 20.0 %copy.106 = f32[63,2,20,1024]{3,1,2,0:T(2,128)} copy(f32[63,2,20,1024]{0,3,2,1:T(8,128)} %bitcast.89) | data formatting | bytes 20643840 | tf_op jit(solution)/shard_map/cond
  136.0 0.0 collective-permute-done.14.back_ref
  136.0 1.7 %slot_pressure.1 = f32[63,1024]{1,0:T(8,128)} custom-call(s32[63]{0:T(128)S(1)} %copy-done.2, f32[560,128]{1,0:T(8,128)S(1)} %get-tuple-element.49.blocks_ref, f32[176,128]{1,0:T(8,128)} %collective-permute-done.14.back_ref), custom_call_target="tpu_custom_call" | custom-call | tf_op jit(solution)/shard_map/slot_pressure/pallas_call | solution.py:491
  (23 shorter events, 0.1 us)
Async XLA Ops:
  0.6 9.6 %copy-start.7 = (f32[20]{0:T(128)S(1)}, f32[20]{0:T(128)}, u32[]{:S(2)}) copy-start(f32[20]{0:T(128)} %diffusion.3) | copy-start | bytes 244
  0.6 9.6 %copy-start = (f32[160,448]{1,0:T(8,128)S(1)}, f32[160,448]{1,0:T(8,128)}, u32[]{:S(2)}) copy-start(f32[160,448]{1,0:T(8,128)} %surf_ref.1) | copy-start | bytes 860164
  0.7 9.6 %copy-start.3 = (f32[2,20]{1,0:T(2,128)S(1)}, f32[2,20]{1,0:T(2,128)}, u32[]{:S(2)}) copy-start(f32[2,20]{1,0:T(2,128)} %weight.1) | copy-start | bytes 484
  1.4 32.3 %copy-start.1 = (s32[63]{0:T(128)}, s32[63]{0:T(128)S(1)}, u32[]{:S(2)}) copy-start(s32[63]{0:T(128)S(1)} %get-tuple-element.87.code) | copy-start | bytes 760
  1.4 26.6 %collective-permute-start.4 = (s32[63]{0:T(128)S(1)}, s32[63]{0:T(128)S(1)}, u32[]{:S(2)}, u32[]{:S(2)}) collective-permute-start(s32[63]{0:T(128)S(1)} %get-tuple-element.87.code), channel_id=1, source_target_pairs={{0,1},{1,2},{2,3},{3,4},{4,5},{5,6},{6,7},{7,0},{8,9},{9,10},{10,1... | collective-permute-start | bytes 764 | tf_op jit(solution)/shard_map/ppermute | solution.py:57
  4.5 20.5 %copy-start.6 = (s32[63,4]{0,1:T(4,128)S(1)}, s32[63,4]{0,1:T(4,128)}, u32[]{:S(2)}) copy-start(s32[63,4]{0,1:T(4,128)} %param.14) | copy-start | bytes 3028
  4.5 21.7 %copy-start.10 = (s32[44]{0:T(128)S(1)}, s32[44]{0:T(128)}, u32[]{:S(2)}) copy-start(s32[44]{0:T(128)} %constant.292.clone) | copy-start | bytes 532
  10.1 28.6 %collective-permute-start.10 = (f32[160,128]{1,0:T(8,128)S(1)}, f32[160,128]{1,0:T(8,128)S(1)}, u32[]{:S(2)}, u32[]{:S(2)}) collective-permute-start(f32[160,128]{1,0:T(8,128)S(1)} %get-tuple-element.45), channel_id=1, source_target_pairs={{0,8},{8,0},{16,24},{24,16},{1,9},{9,1},{17,25},{25,17},{2,10},{10... | collective-permute-start | bytes 245768 | tf_op jit(solution)/shard_map/ppermute | solution.py:52
  19.4 9.8 %collective-permute-start.7 = (f32[48,128]{1,0:T(8,128)S(1)}, f32[48,128]{1,0:T(8,128)S(1)}, u32[]{:S(2)}, u32[]{:S(2)}) collective-permute-start(f32[48,128]{1,0:T(8,128)S(1)} %get-tuple-element.38), channel_id=1, source_target_pairs={{0,2},{1,3},{2,4},{3,5},{4,6},{5,7},{6,0},{7,1},{8,10},{9,11},{10,... | collective-permute-start | bytes 73736 | tf_op jit(solution)/shard_map/ppermute | solution.py:57
  21.4 12.3 %collective-permute-start.5 = (f32[432,128]{1,0:T(8,128)S(1)}, f32[432,128]{1,0:T(8,128)S(1)}, u32[]{:S(2)}, u32[]{:S(2)}) collective-permute-start(f32[432,128]{1,0:T(8,128)S(1)} %get-tuple-element.36), channel_id=1, source_target_pairs={{0,1},{1,0},{2,3},{3,2},{4,5},{5,4},{6,7},{7,6},{8,9},{9,8},{10,11... | collective-permute-start | bytes 663560 | tf_op jit(solution)/shard_map/ppermute | solution.py:52
  22.8 10.9 %collective-permute-start.6 = (f32[432,128]{1,0:T(8,128)S(1)}, f32[432,128]{1,0:T(8,128)S(1)}, u32[]{:S(2)}, u32[]{:S(2)}) collective-permute-start(f32[432,128]{1,0:T(8,128)S(1)} %get-tuple-element.37), channel_id=1, source_target_pairs={{0,7},{1,2},{2,1},{3,4},{4,3},{5,6},{6,5},{7,0},{8,15},{9,10},{10,... | collective-permute-start | bytes 663560 | tf_op jit(solution)/shard_map/ppermute | solution.py:52
  28.1 10.7 %collective-permute-start.11 = (f32[160,128]{1,0:T(8,128)S(1)}, f32[160,128]{1,0:T(8,128)S(1)}, u32[]{:S(2)}, u32[]{:S(2)}) collective-permute-start(f32[160,128]{1,0:T(8,128)S(1)} %get-tuple-element.46), channel_id=1, source_target_pairs={{0,24},{8,16},{16,8},{24,0},{1,25},{9,17},{17,9},{25,1},{2,26},{10... | collective-permute-start | bytes 245768 | tf_op jit(solution)/shard_map/ppermute | solution.py:52
  36.9 10.7 %collective-permute-start.8 = (f32[24,128]{1,0:T(8,128)S(1)}, f32[24,128]{1,0:T(8,128)S(1)}, u32[]{:S(2)}, u32[]{:S(2)}) collective-permute-start(f32[24,128]{1,0:T(8,128)S(1)} %get-tuple-element.40), channel_id=1, source_target_pairs={{0,8},{8,0},{16,24},{24,16},{1,9},{9,1},{17,25},{25,17},{2,10},{10... | collective-permute-start | bytes 36872 | tf_op jit(solution)/shard_map/ppermute | solution.py:52
  37.0 10.6 %collective-permute-start.9 = (f32[24,128]{1,0:T(8,128)S(1)}, f32[24,128]{1,0:T(8,128)S(1)}, u32[]{:S(2)}, u32[]{:S(2)}) collective-permute-start(f32[24,128]{1,0:T(8,128)S(1)} %get-tuple-element.41), channel_id=1, source_target_pairs={{0,24},{8,16},{16,8},{24,0},{1,25},{9,17},{17,9},{25,1},{2,26},{10... | collective-permute-start | bytes 36872 | tf_op jit(solution)/shard_map/ppermute | solution.py:52
  43.9 19.9 %collective-permute-start.12 = (f32[320,128]{1,0:T(8,128)S(1)}, f32[320,128]{1,0:T(8,128)S(1)}, u32[]{:S(2)}, u32[]{:S(2)}) collective-permute-start(f32[320,128]{1,0:T(8,128)S(1)} %get-tuple-element.47), channel_id=1, source_target_pairs={{0,1},{1,0},{2,3},{3,2},{4,5},{5,4},{6,7},{7,6},{8,9},{9,8},{10,11... | collective-permute-start | bytes 491528 | tf_op jit(solution)/shard_map/ppermute | solution.py:52
  45.7 18.1 %collective-permute-start.13 = (f32[320,128]{1,0:T(8,128)S(1)}, f32[320,128]{1,0:T(8,128)S(1)}, u32[]{:S(2)}, u32[]{:S(2)}) collective-permute-start(f32[320,128]{1,0:T(8,128)S(1)} %get-tuple-element.48), channel_id=1, source_target_pairs={{0,7},{1,2},{2,1},{3,4},{4,3},{5,6},{6,5},{7,0},{8,15},{9,10},{10,... | collective-permute-start | bytes 491528 | tf_op jit(solution)/shard_map/ppermute | solution.py:52
  50.6 10.2 %all-to-all-start = ((f32[32,1,128]{2,1,0:T(1,128)}), f32[32,1,128]{2,1,0:T(1,128)S(1)}, u32[]{:S(2)}, u32[]{:S(2)}) async-start(f32[32,1,128]{2,1,0:T(1,128)} %bitcast.27), calls=%async_computation | async-start | bytes 32768 | tf_op jit(solution)/shard_map/all_to_all | solution.py:903
  62.4 73.6 %collective-permute-start.14 = (f32[176,128]{1,0:T(8,128)}, f32[176,128]{1,0:T(8,128)}, u32[]{:S(2)}, u32[]{:S(2)}) collective-permute-start(f32[176,128]{1,0:T(8,128)} %get-tuple-element.50), channel_id=1, source_target_pairs={{0,7},{1,0},{2,1},{3,2},{4,3},{5,4},{6,5},{7,6},{8,15},{9,8},{10,9... | collective-permute-start | bytes 270344 | tf_op jit(solution)/shard_map/ppermute | solution.py:57
  101.0 35.0 %copy-start.2 = (s32[63]{0:T(128)S(1)}, s32[63]{0:T(128)}, u32[]{:S(2)}) copy-start(s32[63]{0:T(128)} %copy-done.1) | copy-start | bytes 760

commit v2 on v1

--- a/solution.py
+++ b/solution.py
@@ -2,6 +2,7 @@
 import jax.numpy as jnp
 from jax import lax
 from jax.experimental import pallas as pl
+from jax.experimental.layout import Layout, with_layout_constraint
 from jax.experimental.pallas import tpu as pltpu
 from jax.sharding import PartitionSpec as P
 
@@ -10,6 +11,7 @@
 TRACER = 2
 REG_X = 14
 REG_Y = 5
+ITERS = 3
 REGION = REG_X * REG_Y
 MOVED = 22
 LANES = 128
@@ -22,6 +24,7 @@
 CAP_WE = 6
 CAP_NS = 16
 RELAY = 10
+LINK_ROWS = HALF * ROWS + (LEVELS + 1) * TILE
 RIM_S = 2 * MOVED * TILE
 RIM_Q = RIM_S + 16
 RIM_M = RIM_Q + 16
@@ -52,25 +55,22 @@
     return lax.ppermute(to_next, axis, first), lax.ppermute(to_last, axis, second)
 
 
+def plain(x):
+    return with_layout_constraint(x, Layout(major_to_minor=tuple(range(x.ndim))))
+
+
+def seen_by_rows(tracers):
+    slots = tracers.shape[0]
+    view = tracers.reshape(slots, TRACER, LEVELS, TILE, LANES).transpose(0, 2, 3, 1, 4)
+    return view.reshape(slots, LEVELS, ROWS, LANES)
+
+
 def shifted(x, axis, by):
     length = lax.axis_size(axis)
     return lax.ppermute(x, axis, [(i, (i + by) % length) for i in range(length)])
 
 
-def fill_places(code_ref, inv, slots):
-    def clear(r, carry):
-        inv[r] = -1
-        return carry
-
-    def place(s, carry):
-        inv[code_ref[s]] = s
-        return carry
-
-    lax.fori_loop(0, 2 * REGION, clear, 0)
-    lax.fori_loop(0, slots, place, 0)
-
-
-def sums_kernel(meta, code, weight, diffusion, t_ref, low_ref, high_ref, s_ref, q_ref, a_ref, b_ref, far_ref, inv, part):
+def sums_kernel(meta, inv, weight, diffusion, t_ref, low_ref, high_ref, s_ref, q_ref, a_ref, b_ref, far_ref, part):
     step = pl.program_id(0)
     slots = s_ref.shape[0] // TILE
     tracer = lax.broadcasted_iota(jnp.int32, (TILE, LANES), 0) % 2
@@ -94,10 +94,6 @@
             odd = part[kind, pl.ds(n * ROWS + 1, TILE, stride=2), :]
             out[pl.ds(row, TILE), :] = even + odd
 
-    @pl.when(step == 0)
-    def _():
-        fill_places(code, inv, slots)
-
     def rim(dest, base, first, chunk):
         for k in range(REG_X):
             src = inv[first + k]
@@ -143,7 +139,7 @@
             messages(b_ref, a_ref)
 
 
-def depth_sums(view, meta, code, weight, diffusion, surface):
+def depth_sums(view, meta, places, weight, diffusion, surface):
     slots = view.shape[0]
     steps = slots // STEP_SLOTS
     rows, width = surface.shape
@@ -174,31 +170,16 @@
             jax.ShapeDtypeStruct((MESSAGE, LANES), F32),
             jax.ShapeDtypeStruct((48, LANES), F32),
         ],
-        scratch_shapes=[
-            pltpu.SMEM((2 * REGION,), jnp.int32),
-            pltpu.VMEM((2, STEP_SLOTS * ROWS, LANES), F32),
-        ],
+        scratch_shapes=[pltpu.VMEM((2, STEP_SLOTS * ROWS, LANES), F32)],
         compiler_params=pltpu.CompilerParams(vmem_limit_bytes=12 << 20),
         name="depth_sums",
-    )(meta, code, weight, diffusion, view, surface, surface)
-
-
-def field_kernel(meta, code, came, s_ref, q_ref, a_ref, b_ref, far_ref, surf_ref, f_ref, ca_ref, cb_ref, inv):
+    )(meta, places, weight, diffusion, view, surface, surface)
+
+
+def field_kernel(meta, inv, s_ref, q_ref, a_ref, b_ref, far_ref, surf_ref, f_ref, ca_ref, cb_ref):
     slots = s_ref.shape[0] // TILE
     even = meta[1] % 2 == 0
     group = lane_id((TILE, LANES)) // BLOCK
-    fill_places(code, inv, slots)
-
-    def place_came(k, carry):
-        r = came[slots - MOVED + k] - REGION
-
-        @pl.when(r >= 0)
-        def _():
-            inv[r] = slots + k
-
-        return carry
-
-    lax.fori_loop(0, MOVED, place_came, 0)
 
     def below(start, size):
         return jnp.where(even, b_ref[pl.ds(start, size), :], a_ref[pl.ds(start, size), :])
@@ -294,23 +275,22 @@
         cb_ref[pl.ds(h * TILE, TILE), :] = jnp.where(east_even, west_out, east_out)
 
 
-def region_fields(meta, code, came, s, q, a, b, far, surface):
+def region_fields(meta, places, s, q, a, b, far, surface):
     return pl.pallas_call(
         field_kernel,
-        in_specs=[SMEM, SMEM, SMEM] + [VMEM] * 6,
+        in_specs=[SMEM, SMEM] + [VMEM] * 6,
         out_specs=[VMEM] * 3,
         out_shape=[
             jax.ShapeDtypeStruct((4, FIELD_TILES, FIELD_ROWS, LANES), F32),
             jax.ShapeDtypeStruct((24, LANES), F32),
             jax.ShapeDtypeStruct((24, LANES), F32),
         ],
-        scratch_shapes=[pltpu.SMEM((2 * REGION,), jnp.int32)],
         compiler_params=pltpu.CompilerParams(vmem_limit_bytes=12 << 20),
         name="region_fields",
-    )(meta, code, came, s, q, a, b, far, surface)
-
-
-def basis_kernel(meta, f_ref, ca_ref, cb_ref, u_ref, g_ref):
+    )(meta, places, s, q, a, b, far, surface)
+
+
+def basis_kernel(meta, came, f_ref, ca_ref, cb_ref, g_ref, blocks_ref, back_ref, u_ref):
     even = meta[0] % 2 == 0
     lane = lane_id((TILE, LANES))
     tiles = range(FIELD_TILES)
@@ -385,28 +365,50 @@
     for k, u in enumerate((u0, u1, u2)):
         for b in tiles:
             u_ref[k, b] = u[b][rows_in]
-
-
-def solve_basis(meta, fields, ca, cb, devices):
+    group = lane // BLOCK
+    for k in range(3):
+        for by in range(REG_Y):
+            for b in tiles:
+                value = [u_ref[k, b, pl.ds(BLOCK * by + q, TILE, stride=4), :] for q in range(4)]
+                for g in range(4):
+                    if 4 * b + g >= REG_X:
+                        continue
+                    tile = value[0]
+                    for q in range(4):
+                        part = turn(value[q], BLOCK * (q - g), 1)
+                        tile = part if q == 0 else jnp.where(group == q, part, tile)
+                    blocks_ref[pl.ds((k * REGION + by * REG_X + 4 * b + g) * TILE, TILE), :] = tile
+    first = came.shape[0] - MOVED
+    for m in range(MOVED):
+        at = pl.multiple_of(jnp.maximum(came[first + m] - REGION, 0) * TILE, TILE)
+        for k in range(3):
+            tile = blocks_ref[pl.ds(k * REGION * TILE + at, TILE), :]
+            back_ref[pl.ds((k * MOVED + m) * TILE, TILE), :] = tile
+
+
+def solve_basis(meta, came, fields, ca, cb, devices):
     return pl.pallas_call(
         basis_kernel,
-        in_specs=[SMEM, VMEM, VMEM, VMEM],
-        out_specs=[VMEM, VMEM],
+        in_specs=[SMEM, SMEM, VMEM, VMEM, VMEM],
+        out_specs=[VMEM] * 3,
         out_shape=[
-            jax.ShapeDtypeStruct((3, FIELD_TILES, FIELD_ROWS - 2 * TILE, LANES), F32),
             jax.ShapeDtypeStruct((devices, LANES), F32),
+            jax.ShapeDtypeStruct((3 * REGION * TILE, LANES), F32),
+            jax.ShapeDtypeStruct((3 * MOVED * TILE, LANES), F32),
         ],
+        scratch_shapes=[pltpu.VMEM((3, FIELD_TILES, FIELD_ROWS - 2 * TILE, LANES), F32)],
         compiler_params=pltpu.CompilerParams(vmem_limit_bytes=24 << 20),
         name="solve_basis",
-    )(meta, fields, ca, cb)
-
-
-def solution_kernel(came, u_ref, g_ref, blocks_ref, back_ref, over_ref):
+    )(meta, came, fields, ca, cb)
+
+
+def pressure_kernel(code, g_ref, blocks_ref, back_ref, held_ref, out_ref, same_ref, work):
+    del held_ref, same_ref
+    slots = out_ref.shape[0]
     total = jnp.sum(g_ref[...].reshape(-1, TILE, LANES), axis=0)
     total = jnp.broadcast_to(jnp.sum(total, axis=0, keepdims=True), (TILE, LANES))
     lane = lane_id((TILE, LANES))
     pick = lambda k: jnp.sum(jnp.where(lane == k, total, 0.0), axis=1, keepdims=True)
-    over_ref[...] = jnp.broadcast_to(pick(6), (TILE, LANES))
     g = [pick(k) for k in range(6)]
     g = [x / g[0] for x in g]
     a = [g[k] - g[k + 1] for k in range(5)]
@@ -424,61 +426,26 @@
     rho = [one, zero, zero]
     way = [one, zero, zero]
     norm = g[0]
-    for iteration in range(3):
+    for iteration in range(ITERS):
         length = norm / form(way, a)
         coef = [coef[k] + length * way[k] for k in range(3)]
-        if iteration < 2:
+        if iteration + 1 < ITERS:
             moved = [way[0], way[1] - way[0], way[2] - way[1]]
             rho = [rho[k] - length * moved[k] for k in range(3)]
             norm_next = form(rho, g)
             way = [rho[k] + (norm_next / norm) * way[k] for k in range(3)]
             norm = norm_next
     coef = [jnp.broadcast_to(c, (TILE, LANES)) for c in coef]
-    group = lane // BLOCK
-    for by in range(REG_Y):
-        for b in range(FIELD_TILES):
-            value = []
-            for q in range(4):
-                at = pl.ds(BLOCK * by + q, TILE, stride=4)
-                value.append(coef[0] * u_ref[0, b, at, :] + coef[1] * u_ref[1, b, at, :] + coef[2] * u_ref[2, b, at, :])
-            for g4 in range(4):
-                if 4 * b + g4 >= REG_X:
-                    continue
-                tile = jnp.zeros((TILE, LANES), F32)
-                for q in range(4):
-                    tile = jnp.where(group == q, turn(value[q], BLOCK * (q - g4), 1), tile)
-                blocks_ref[pl.ds((by * REG_X + 4 * b + g4) * TILE, TILE), :] = tile
-    first = came.shape[0] - MOVED
-    for k in range(MOVED):
-        at = pl.multiple_of(jnp.maximum(came[first + k] - REGION, 0) * TILE, TILE)
-        back_ref[pl.ds(k * TILE, TILE), :] = blocks_ref[pl.ds(at, TILE), :]
-
-
-def region_solution(came, u, g):
-    return pl.pallas_call(
-        solution_kernel,
-        in_specs=[SMEM, VMEM, VMEM],
-        out_specs=[VMEM] * 3,
-        out_shape=[
-            jax.ShapeDtypeStruct((REGION * TILE, LANES), F32),
-            jax.ShapeDtypeStruct((MOVED * TILE, LANES), F32),
-            jax.ShapeDtypeStruct((TILE, LANES), F32),
-        ],
-        compiler_params=pltpu.CompilerParams(vmem_limit_bytes=12 << 20),
-        name="region_solution",
-    )(came, u, g)
-
-
-def pressure_kernel(code, blocks_ref, back_ref, out_ref, work):
-    slots = out_ref.shape[0]
     for s in range(slots):
         c = code[s]
         at = pl.multiple_of(jnp.where(c < REGION, c, 0) * TILE, TILE)
-        tile = blocks_ref[pl.ds(at, TILE), :]
-        k = s - (slots - MOVED)
-        if k >= 0:
-            tile = jnp.where(c < REGION, tile, back_ref[pl.ds(k * TILE, TILE), :])
-        work[pl.ds(s * TILE, TILE), :] = tile
+        tiles = [blocks_ref[pl.ds(k * REGION * TILE + at, TILE), :] for k in range(3)]
+        m = s - (slots - MOVED)
+        if m >= 0:
+            for k in range(3):
+                other = back_ref[pl.ds((k * MOVED + m) * TILE, TILE), :]
+                tiles[k] = jnp.where(c < REGION, tiles[k], other)
+        work[pl.ds(s * TILE, TILE), :] = coef[0] * tiles[0] + coef[1] * tiles[1] + coef[2] * tiles[2]
     for first in range(0, slots, TILE):
         size = min(TILE, slots - first)
         for c in range(TILE):
@@ -486,21 +453,25 @@
             out_ref[pl.ds(first, size), pl.ds(c * LANES, LANES)] = lines
 
 
-def slot_pressure(code, blocks, back):
+def slot_pressure(code, sums, blocks, back, held):
     slots = code.shape[0]
     return pl.pallas_call(
         pressure_kernel,
-        in_specs=[SMEM, VMEM, VMEM],
-        out_specs=VMEM,
-        out_shape=jax.ShapeDtypeStruct((slots, TILE * LANES), F32),
+        in_specs=[SMEM, VMEM, VMEM, VMEM, ANY],
+        out_specs=[VMEM, ANY],
+        out_shape=[
+            jax.ShapeDtypeStruct((slots, TILE * LANES), F32),
+            jax.ShapeDtypeStruct(held.shape, F32),
+        ],
         scratch_shapes=[pltpu.VMEM((slots * TILE, LANES), F32)],
+        input_output_aliases={4: 1},
         compiler_params=pltpu.CompilerParams(vmem_limit_bytes=12 << 20),
         name="slot_pressure",
-    )(code, blocks, back)
-
-
-def columns_kernel(meta, code, t_ref, a_ref, b_ref, inv, west, east, sems):
-    fill_places(code, inv, code.shape[0])
+    )(code, sums, blocks, back, held)
+
+
+def columns_kernel(meta, inv, t_ref, after_ref, a_ref, b_ref, west, east, sems):
+    del after_ref
     even = meta[0] % 2 == 0
     count = 2 * REG_Y
 
@@ -532,22 +503,21 @@
         b_ref[pl.ds(level * ROWS, ROWS), :] = jnp.where(even, out_w, out_e)
 
 
-def column_strips(meta, code, view):
+def column_strips(meta, places, view, after):
     count = 2 * REG_Y
     return pl.pallas_call(
         columns_kernel,
-        in_specs=[SMEM, SMEM, ANY],
+        in_specs=[SMEM, SMEM, ANY, ANY],
         out_specs=[VMEM] * 2,
         out_shape=[jax.ShapeDtypeStruct((HALF * ROWS, LANES), F32)] * 2,
         scratch_shapes=[
-            pltpu.SMEM((2 * REGION,), jnp.int32),
             pltpu.VMEM((count, LEVELS, ROWS, LANES), F32),
             pltpu.VMEM((count, LEVELS, ROWS, LANES), F32),
             pltpu.SemaphoreType.DMA((2, count)),
         ],
         compiler_params=pltpu.CompilerParams(vmem_limit_bytes=12 << 20),
         name="column_strips",
-    )(meta, code, view)
+    )(meta, places, view, after)
 
 
 def links_kernel(meta, table, t_ref, ga_ref, gb_ref, a_ref, b_ref, whole, half, sem_we, sem_ns):
@@ -582,7 +552,7 @@
 
     def message(way, out):
         out[pl.ds(0, HALF * ROWS), :] = relays[way]
-        out[pl.ds(HALF * ROWS, LEVELS * TILE), :] = jnp.zeros((LEVELS * TILE, LANES), F32)
+        out[pl.ds(HALF * ROWS, (LEVELS + 1) * TILE), :] = jnp.zeros(((LEVELS + 1) * TILE, LANES), F32)
         lane32 = lane_id((ROWS, LANES)) % BLOCK
         for k in range(CAP_WE):
             link = table[way * (CAP_WE + CAP_NS) + k]
@@ -638,7 +608,7 @@
 
 
 def link_strips(meta, table, view, ga, gb):
-    rows = HALF * ROWS + LEVELS * TILE
+    rows = LINK_ROWS
     return pl.pallas_call(
         links_kernel,
         in_specs=[SMEM, SMEM, ANY, VMEM, VMEM],
@@ -655,51 +625,53 @@
     )(meta, table, view, ga, gb)
 
 
-EXTRA = 7
-TALL = 32
-CHUNK = 4
-
-
-def tracer_kernel(meta, table, need, diffusion, t_ref, ga_ref, gb_ref, ha_ref, hb_ref, out_ref, buf, seen, sems):
+IMAGE = LEVELS * ROWS
+FIELDS = 5
+BOX_LOW = 2 * HALF * ROWS
+BOX_HIGH = BOX_LOW + LINK_ROWS
+BOX = BOX_HIGH + LINK_ROWS
+
+
+def tracer_kernel(meta, table, need, diffusion, t_ref, ga_ref, gb_ref, ha_ref, hb_ref, out_ref, own, up, down, box, seen, sems):
     step = pl.program_id(0)
-    steps = pl.num_programs(0)
-    slots = buf.shape[0] - EXTRA
+    slots = own.shape[0] // IMAGE
+    chunk = STEP_SLOTS * IMAGE
+    chunks = slots // STEP_SLOTS
 
     def fetch(c):
-        src = t_ref.at[pl.ds(c * STEP_SLOTS, STEP_SLOTS)]
-        dst = buf.at[pl.ds(c * STEP_SLOTS, STEP_SLOTS), :, pl.ds(TILE, ROWS), :]
-        return pltpu.make_async_copy(src, dst, sems.at[c])
+        rows = pl.ds(pl.multiple_of(c * chunk, TILE), chunk)
+        return pltpu.make_async_copy(t_ref.at[rows], own.at[rows], sems.at[c])
 
     @pl.when(step == 0)
     def _():
-        for c in range(slots // STEP_SLOTS):
+        for c in range(chunks):
             fetch(c).start()
         seen[0] = 0
         even_x = meta[0] % 2 == 0
         even_y = meta[1] % 2 == 0
-
-        def unfold(image, value):
-            for level in range(HALF):
-                x = value[level * ROWS : (level + 1) * ROWS]
-                buf[image, level, pl.ds(TILE, ROWS), :] = x
-                buf[image, level + HALF, pl.ds(TILE, ROWS), :] = turn(x, -16, 1)
-
-        for level in range(LEVELS):
-            buf[slots, level, pl.ds(TILE, ROWS), :] = jnp.zeros((ROWS, LANES), F32)
-        unfold(slots + 1, jnp.where(even_x, gb_ref[...], ga_ref[...]))
-        unfold(slots + 2, jnp.where(even_x, ga_ref[...], gb_ref[...]))
-        folded = pl.ds(0, HALF * ROWS)
-        unfold(slots + 3, jnp.where(even_y, hb_ref[folded, :], ha_ref[folded, :]))
-        unfold(slots + 4, jnp.where(even_y, ha_ref[folded, :], hb_ref[folded, :]))
-        for level in range(LEVELS):
-            rows = pl.ds(HALF * ROWS + level * TILE, TILE)
-            first, second = ha_ref[rows, :], hb_ref[rows, :]
-            buf[slots + 5, level, pl.ds(TILE, TILE), :] = jnp.where(even_y, second, first)
-            buf[slots + 6, level, pl.ds(TILE, TILE), :] = jnp.where(even_y, first, second)
+        land = pl.ds(TILE + slots * IMAGE - TILE, IMAGE + 2 * TILE)
+        up[land, :] = jnp.zeros((IMAGE + 2 * TILE, LANES), F32)
+        down[land, :] = jnp.zeros((IMAGE + 2 * TILE, LANES), F32)
+        for first, second, size, low, high in (
+            (ga_ref, gb_ref, HALF * ROWS, 0, HALF * ROWS),
+            (ha_ref, hb_ref, LINK_ROWS, BOX_LOW, BOX_HIGH),
+        ):
+            even = even_x if low == 0 else even_y
+            box[pl.ds(low, size), :] = jnp.where(even, second[...], first[...])
+            box[pl.ds(high, size), :] = jnp.where(even, first[...], second[...])
 
     def arrive(c, carry):
         fetch(c).wait()
-        return carry
+
+        def roll_slot(n, carry):
+            base = pl.multiple_of((c * STEP_SLOTS + n) * IMAGE, TILE)
+            for level in range(LEVELS):
+                x = own[pl.ds(base + level * ROWS, ROWS), :]
+                up[pl.ds(base + TILE + level * ROWS, ROWS), :] = pltpu.roll(x, BLOCK, 1)
+                down[pl.ds(base + TILE + level * ROWS, ROWS), :] = pltpu.roll(x, LANES - BLOCK, 1)
+            return carry
+
+        return lax.fori_loop(0, STEP_SLOTS, roll_slot, carry)
 
     upto = jnp.maximum(seen[0], need[step] + 1)
     lax.fori_loop(seen[0], upto, arrive, 0)
@@ -709,6 +681,7 @@
     lane = lane_id(cells)
     column = lane % BLOCK
     row = lax.broadcasted_iota(jnp.int32, cells, 0)
+    row8 = row[:TILE]
     edge = (
         jnp.where(column == 0, 1.0, 0.0),
         jnp.where(column == BLOCK - 1, 1.0, 0.0),
@@ -718,58 +691,79 @@
 
     def one_slot(n, carry):
         s = step * STEP_SLOTS + n
-        entry = [[table[s * 16 + 4 * t + f] for f in range(4)] for t in range(4)]
+        entry = [[table[(s * 4 + t) * FIELDS + f] for f in range(FIELDS)] for t in range(4)]
         count = jnp.full(cells, 4.0, F32)
         for t in range(4):
-            count = count - edge[t] * entry[t][3].astype(F32)
-        for t, dest in ((2, TILE - 2), (3, TILE + ROWS)):
-            image, at, by, _ = entry[t]
-            line = buf[image, :, pl.ds(TILE + at, 2), :]
-            buf[s, :, pl.ds(dest, 2), :] = pltpu.roll(line, by, 2)
-        (west, _, by_west, _), (east, _, by_east, _) = entry[0], entry[1]
-        shape = (CHUNK, ROWS, LANES)
-        lane3 = lane_id(shape)
-        column3 = lane3 % BLOCK
-        for first in range(0, LEVELS, CHUNK):
-            some = pl.ds(first, CHUNK)
-            x = buf[s, some, pl.ds(TILE, ROWS), :]
-            under = buf[s, some, pl.ds(TILE - 2, ROWS), :]
-            over = buf[s, some, pl.ds(TILE + 2, ROWS), :]
-            w = buf[west, some, pl.ds(TILE, ROWS), :]
-            e = buf[east, some, pl.ds(TILE, ROWS), :]
-            total = pltpu.roll(jnp.where(lane3 >= LANES - BLOCK, under, x), BLOCK, 2)
-            total = total + pltpu.roll(jnp.where(lane3 < BLOCK, over, x), LANES - BLOCK, 2)
-            total = total + jnp.where(column3 == 0, pltpu.roll(w, by_west, 2), pltpu.roll(x, 1, 2))
-            total = total + jnp.where(column3 == BLOCK - 1, pltpu.roll(e, by_east, 2), pltpu.roll(x, LANES - 1, 2))
-            for i in range(CHUNK):
-                out_ref[n, first + i] = x[i] + diffusion[first + i] * (total[i] - count * x[i])
+            count = count - edge[t] * entry[t][4].astype(F32)
+        base = pl.multiple_of(s * IMAGE, TILE)
+        west, east, south, north = [pl.multiple_of(entry[t][0] * IMAGE, TILE) + TILE for t in range(4)]
+
+        for t, dest in ((0, down), (1, up)):
+            @pl.when(entry[t][1] == 1)
+            def _():
+                first, by = pl.multiple_of(entry[t][2], TILE), entry[t][3]
+                for level in range(LEVELS):
+                    part = level // HALF
+                    x = box[pl.ds(first + (level % HALF) * ROWS, ROWS), :]
+                    x = pltpu.roll(x, (by + LANES - 16 * part) % LANES, 1)
+                    dest[pl.ds(TILE + (slots + 1) * IMAGE + level * ROWS, ROWS), :] = x
+
+        for t, dest, offset in ((2, up, ROWS - 2), (3, down, -6)):
+            @pl.when(entry[t][1] == 1)
+            def _():
+                first, by = entry[t][2], entry[t][3]
+                for level in range(LEVELS):
+                    x = pltpu.roll(box[pl.ds(first + level * TILE, TILE), :], by, 1)
+                    dest[pl.ds(TILE + (slots + 3) * IMAGE + level * ROWS + offset, TILE), :] = x
+
+        for level in range(LEVELS):
+            at = level * ROWS
+            x = own[pl.ds(base + at, ROWS), :]
+            under = up[pl.ds(base + TILE + at - 2, ROWS), :]
+            over = down[pl.ds(base + TILE + at + 2, ROWS), :]
+            low = up[pl.ds(south + at + ROWS - 2, TILE), :]
+            high = down[pl.ds(north + at - 6, TILE), :]
+            under = jnp.concatenate([jnp.where(row8 < 2, low, under[:TILE]), under[TILE:]], axis=0)
+            over = jnp.concatenate([over[:TILE], jnp.where(row8 >= TILE - 2, high, over[TILE:])], axis=0)
+            total = jnp.where(lane < BLOCK, under, up[pl.ds(base + TILE + at, ROWS), :])
+            total = total + jnp.where(lane >= LANES - BLOCK, over, down[pl.ds(base + TILE + at, ROWS), :])
+            w = down[pl.ds(west + at, ROWS), :]
+            e = up[pl.ds(east + at, ROWS), :]
+            total = total + pltpu.roll(jnp.where(column == BLOCK - 1, w, x), 1, 1)
+            total = total + pltpu.roll(jnp.where(column == 0, e, x), LANES - 1, 1)
+            out_ref[pl.ds(pl.multiple_of(n * IMAGE, TILE) + at, ROWS), :] = x + diffusion[level] * (total - count * x)
         return carry
 
     lax.fori_loop(0, STEP_SLOTS, one_slot, 0)
 
-    @pl.when(step == steps - 1)
+    @pl.when(step == pl.num_programs(0) - 1)
     def _():
-        lax.fori_loop(seen[0], slots // STEP_SLOTS, arrive, 0)
+        lax.fori_loop(seen[0], chunks, arrive, 0)
 
 
 def step_tracers(meta, table, need, diffusion, view, ga, gb, ha, hb):
     slots = view.shape[0]
     steps = slots // STEP_SLOTS
-    shape = (STEP_SLOTS, LEVELS, ROWS, LANES)
-    return pl.pallas_call(
+    rows = slots * IMAGE
+    out = pl.pallas_call(
         tracer_kernel,
         grid=(steps,),
         in_specs=[SMEM] * 4 + [ANY] + [VMEM] * 4,
-        out_specs=pl.BlockSpec(shape, lambda s: (s, 0, 0, 0)),
-        out_shape=jax.ShapeDtypeStruct(view.shape, F32),
+        out_specs=pl.BlockSpec((STEP_SLOTS * IMAGE, LANES), lambda s: (s, 0)),
+        out_shape=jax.ShapeDtypeStruct((rows, LANES), F32),
         scratch_shapes=[
-            pltpu.VMEM((slots + EXTRA, LEVELS, TALL, LANES), F32),
+            pltpu.VMEM((rows, LANES), F32),
+            pltpu.VMEM((rows + 4 * IMAGE + 2 * TILE, LANES), F32),
+            pltpu.VMEM((rows + 4 * IMAGE + 2 * TILE, LANES), F32),
+            pltpu.VMEM((BOX, LANES), F32),
             pltpu.SMEM((1,), jnp.int32),
             pltpu.SemaphoreType.DMA((steps,)),
         ],
-        compiler_params=pltpu.CompilerParams(vmem_limit_bytes=40 << 20),
+        compiler_params=pltpu.CompilerParams(vmem_limit_bytes=44 << 20),
+        cost_estimate=pl.CostEstimate(flops=14 * rows * LANES, bytes_accessed=8 * rows * LANES, transcendentals=0),
         name="step_tracers",
-    )(meta, table, need, diffusion, view, ga, gb, ha, hb)
+    )(meta, table, need, diffusion, view.reshape(rows, LANES), ga, gb, ha, hb)
+    return out.reshape(view.shape)
 
 
 def with_halo(block, sides, width):
@@ -815,7 +809,8 @@
         + jnp.concatenate([south[..., None, :], inner_y], axis=-2)
         + jnp.concatenate([-inner_y, north[..., None, :]], axis=-2)
     )
-    return (grid + diffusion[None, None, :, None, None] * laplace).reshape(tracers.shape)
+    updated = grid + diffusion[None, None, :, None, None] * laplace
+    return plain(seen_by_rows(updated.reshape(tracers.shape)))
 
 
 def strip_tables(halo_source, code, at_x, at_y, count_x, count_y):
@@ -852,21 +847,21 @@
     send = jnp.sum(jnp.where(hit, index.reshape(-1)[None, :] + 1, 0), axis=1) - 1
     over = jnp.any(linked & (take >= jnp.where(kind == 1, CAP_NS, CAP_WE)))
     row = (code // REG_X)[:, None]
-    land, west, east, we_low, we_high, ns_low, ns_high = [slots + k for k in range(EXTRA)]
     local = same_x & here
-    beside = jnp.where(here, jnp.where(side == 0, west, east), jnp.where(up, we_high, we_low))
-    beside_lane = jnp.where(here, row, row % REG_Y + jnp.where(side == 0, 0, REG_Y))
-    lane = jnp.where(same_x, RELAY + take, beside_lane)
-    image_we = jnp.where(local, local_slot, jnp.where(same_x, jnp.where(up, we_high, we_low), beside))
-    by_we = jnp.where(side == 0, -jnp.where(local, BLOCK - 1, lane), BLOCK - 1 - jnp.where(local, 0, lane))
-    image_ns = jnp.where(local, local_slot, jnp.where(up, ns_high, ns_low))
-    row_ns = jnp.where(local, jnp.where(side == 2, ROWS - 2, 0), 2 * (take // 4))
-    by_ns = jnp.where(local, 0, jnp.where(side == 2, LANES - BLOCK, 0) - BLOCK * (take % 4))
     north = kind == 1
-    image = jnp.where(missing, land, jnp.where(north, image_ns, image_we))
-    at = jnp.where(missing | ~north, 0, jnp.minimum(row_ns, ROWS - 2))
-    by = jnp.where(missing, 0, jnp.where(north, by_ns, by_we)) % LANES
-    table = jnp.stack([image, at, by, missing.astype(jnp.int32)], axis=-1).reshape(-1)
+    lane = jnp.where(same_x, RELAY + take, jnp.where(here, row, row % REG_Y + jnp.where(side == 0, 0, REG_Y)))
+    beside = jnp.where(side == 0, 0, HALF * ROWS)
+    along = jnp.where(up, BOX_HIGH, BOX_LOW)
+    box_we = jnp.where(same_x | ~here, along, beside)
+    by_we = jnp.where(side == 0, -1, BLOCK) - lane
+    box_ns = along + HALF * ROWS + 2 * jnp.minimum(take // 4, TILE // 2 - 1) - jnp.where(side == 3, TILE - 2, 0)
+    by_ns = jnp.where(side == 3, LANES - BLOCK, 0) - BLOCK * (take % 4)
+    remote = ~missing & ~local
+    image = jnp.where(missing, slots, jnp.where(local, local_slot, slots + 1 + 2 * kind))
+    at = jnp.where(remote, jnp.where(north, box_ns, box_we), 0)
+    by = jnp.where(remote, jnp.where(north, by_ns, by_we), 0) % LANES
+    fields = [image, remote.astype(jnp.int32), at, by, missing.astype(jnp.int32)]
+    table = jnp.stack(fields, axis=-1).reshape(-1)
     last = jnp.where(local & ~missing, local_slot, 0)
     last = jnp.maximum(jnp.max(last, axis=1), jnp.arange(slots))
     need = jnp.max(last.reshape(-1, STEP_SLOTS), axis=1) // STEP_SLOTS
@@ -884,37 +879,38 @@
     came = shifted(code, "gy", 1)
     zero = jnp.zeros((), jnp.int32)
     meta = jnp.stack([at_x, at_y, zero + count_y, zero]).astype(jnp.int32)
-
-    view = tracers.reshape(slots, TRACER, LEVELS, TILE, LANES).transpose(0, 2, 3, 1, 4)
-    view = view.reshape(slots, LEVELS, ROWS, LANES)
-    s, q, a, b, far = depth_sums(view, meta, code, layer_weight, diffusion, surface_term)
+    spot = jnp.arange(2 * REGION, dtype=jnp.int32)[:, None]
+    index = jnp.arange(slots, dtype=jnp.int32)[None, :]
+    places = jnp.sum(jnp.where(code[None, :] == spot, index + 1, 0), axis=1) - 1
+
+    view = seen_by_rows(tracers)
+    s, q, a, b, far = depth_sums(view, meta, places, layer_weight, diffusion, surface_term)
     ra, rb = swap(a, b, "gy", count_y)
     rfar = shifted(far, "gy", 2)
 
     table, need, send, over = strip_tables(halo_source, code, at_x, at_y, count_x, count_y)
-    ga, gb = swap(*column_strips(meta, code, view), "gx", count_x)
-
-    fields, ca, cb = region_fields(meta, code, came, s, q, ra, rb, rfar, surface_term)
+    ga, gb = swap(*column_strips(meta, places, view, far), "gx", count_x)
+
+    moved = (came[None, :] - REGION == spot) & (came[None, :] >= REGION)
+    both = places + jnp.sum(jnp.where(moved, index + 1 + MOVED, 0), axis=1)
+    fields, ca, cb = region_fields(meta, both, s, q, ra, rb, rfar, surface_term)
     ca, cb = swap(ca, cb, "gx", count_x)
     ha, hb = swap(*link_strips(meta, send, view, ga, gb), "gy", count_y)
 
     meta_over = jnp.stack([at_x, at_y, zero + count_y, over]).astype(jnp.int32)
-    u, sums = solve_basis(meta_over, fields, ca, cb, count_x * count_y)
-    sums = lax.all_to_all(sums, ("gx", "gy"), 0, 0, tiled=True)
-    blocks, back, total_over = region_solution(came, u, sums)
+    sums, blocks, back = solve_basis(meta_over, came, fields, ca, cb, count_x * count_y)
     back = shifted(back, "gy", -1)
-
+    sums = lax.all_to_all(sums[:, None], ("gx", "gy"), 0, 0, tiled=True)
     updated = step_tracers(meta, table, need, diffusion, view, ga, gb, ha, hb)
-    updated = updated.reshape(slots, LEVELS, TILE, TRACER, LANES).transpose(0, 3, 1, 2, 4)
-    updated = updated.reshape(tracers.shape)
-    pressure = slot_pressure(code, blocks, back)
     updated = lax.cond(
-        total_over[0, 0] > 0,
+        jnp.max(sums[:, 0, 6]) > 0.0,
         lambda fast: general_step(tracers, diffusion, halo_source),
         lambda fast: fast,
         updated,
     )
-    return (updated, pressure)
+    pressure, updated = slot_pressure(code, sums.reshape(-1, LANES), blocks, back, updated)
+    updated = updated.reshape(slots, LEVELS, TILE, TRACER, LANES).transpose(0, 3, 1, 2, 4)
+    return (updated.reshape(tracers.shape), pressure)
 
 
 def solution(mesh):

time: 139 us -> 90.6 us (0.65)
  local copies, waits for them, and re-layouts: 41.6 us -> 4.24 us
  waiting for transfers between devices: 11.6 us -> 1.54 us
  Pallas kernels: 60.9 us -> 54.1 us
  starting transfers between devices: 18.6 us -> 23.1 us
  other arithmetic: 2.72 us -> 4.33 us
    cond x1 -> x0, local copies, waits for them, and re-layouts: 20 us -> none
    reshape x3 -> x1, local copies, waits for them, and re-layouts: 19.8 us -> 0.22 us  [strip_tables(): table = jnp.stack(fields, axis=-1).reshape(-1)]
    all_to_all x1, waiting for transfers between devices: 7.02 us -> 0.01 us  [on_device(): sums = lax.all_to_all(sums[:, None], ('gx', 'gy'), 0, 0, tiled=True)]
    pallas_call x5 -> x4, Pallas kernels: 15.2 us -> 11.6 us  [the longest x1 4.25 us: column_strips(): pl.pallas_call(columns_kernel, in_specs=[SMEM, SMEM, ANY, ANY], out_specs...]
    ppermute x3, starting transfers between devices: 5.69 us -> 9.21 us  [shifted(): lax.ppermute(x, axis, [(i, (i + by) % length) for i in range(length)])]
    ppermute x4, waiting for transfers between devices: 4.57 us -> 1.52 us  [swap(): lax.ppermute(to_next, axis, first)]
    unnamed x15, local copies, waits for them, and re-layouts: 0.14 us -> 2.82 us
    pallas_call x1, Pallas kernels: 31.5 us -> 29.8 us  [step_tracers(): pl.pallas_call(tracer_kernel, grid=(steps,), in_specs=[SMEM] * 4 + [ANY]...]
  transfers between devices with their start and end apart: 12 -> 12, of which waited for: 2 -> 1; matrix products, arithmetic and copies ran while one was open for 32% -> 6% of each run, Pallas kernels for 43% -> 49%
where the time goes in v2:
time: 90.6 us; the launch traced here: 89.9 us
  Pallas kernels  54.1 us (60%)
  starting transfers between devices  23.1 us (25%)
  other arithmetic  4.33 us (5%)
  local copies, waits for them, and re-layouts  4.24 us (5%)
  between operations  2.29 us (3%)
  waiting for transfers between devices  1.54 us (2%)
    pallas_call x1, Pallas kernels, step_tracers(): pl.pallas_call(tracer_kernel, grid=(steps,), in_specs=[SMEM] * 4 + [ANY]...  29.8 us
    ppermute x3, starting transfers between devices, shifted(): lax.ppermute(x, axis, [(i, (i + by) % length) for i in range(length)])  9.21 us
    pallas_call x1, Pallas kernels, depth_sums(): pl.pallas_call(sums_kernel, grid=(steps,), in_specs=[SMEM, SMEM, SMEM, SM...  7.71 us
    ppermute x4, starting transfers between devices, swap(): lax.ppermute(to_last, axis, second)  7.22 us
    pallas_call x1, Pallas kernels, link_strips(): pl.pallas_call(links_kernel, in_specs=[SMEM, SMEM, ANY, VMEM, VMEM], out_...  5.03 us
    pallas_call x1, Pallas kernels, column_strips(): pl.pallas_call(columns_kernel, in_specs=[SMEM, SMEM, ANY, ANY], out_specs...  4.25 us
    pallas_call x1, Pallas kernels, solve_basis(): pl.pallas_call(basis_kernel, in_specs=[SMEM, SMEM, VMEM, VMEM, VMEM], out...  3.71 us
    ppermute x4, starting transfers between devices, swap(): lax.ppermute(to_next, axis, first)  3.41 us
  transfers between devices with their start and end apart: 12, of which 1 were waited for; matrix products, arithmetic and copies ran while one was open for 6% of the time, Pallas kernels for 49%

profile of v2, /device:TPU:0, one launch (start us, length us, event | category | flops | bytes accessed | tf_op | source)
XLA Modules:
  0.0 89.9 jit_solution(15714535782540852466)
XLA Ops:
  0.6 0.7 and_select_fusion.9
  1.4 3.0 %collective-permute-start.4 = (s32[63]{0:T(128)S(1)}, s32[63]{0:T(128)S(1)}, u32[]{:S(2)}, u32[]{:S(2)}) collective-permute-start(s32[63]{0:T(128)S(1)} %get-tuple-element.76.code), channel_id=1, source_target_pairs={{0,1},{1,2},{2,3},{3,4},{4,5},{5,6},{6,7},{7,0},{8,9},{9,10},{10,1... | collective-permute-start | bytes 764 | tf_op jit(solution)/shard_map/ppermute | solution.py:70
  4.4 0.8 copy.104
  5.2 0.2 select_reduce_fusion.3
  5.4 0.1 lt.101
  5.5 0.1 select_select_fusion.1
  5.6 0.1 eq.131
  5.7 0.1 iota_add_fusion
  5.8 0.1 add.322
  5.9 0.3 convert_reduce_fusion
  6.2 0.1 reshape.465
  6.3 0.1 eq.145
  6.4 0.8 select_reduce_fusion.2
  7.3 0.1 select_reduce_fusion.1
  7.4 0.1 reshape.460
  7.5 0.1 bitcast_dynamic-update-slice_fusion.2
  7.6 0.1 fusion.24
  7.6 0.1 fusion.36
  7.8 0.7 and_reduce_fusion
  8.4 0.1 pad_add_fusion.2
  9.1 0.0 collective-permute-done.4.came
  9.2 0.1 select_reduce_fusion
  9.3 0.0 copy-start
  9.3 1.0 %copy-done = f32[160,448]{1,0:T(8,128)S(1)} copy-done((f32[160,448]{1,0:T(8,128)S(1)}, f32[160,448]{1,0:T(8,128)}, u32[]{:S(2)}) %copy-start) | copy-done | bytes 286744
  10.3 0.7 copy-done.4
  11.0 7.7 %depth_sums.1 = (f32[504,128]{1,0:T(8,128)S(1)}, f32[504,128]{1,0:T(8,128)S(1)}, f32[432,128]{1,0:T(8,128)S(1)}, f32[432,128]{1,0:T(8,128)S(1)}, f32[48,128]{1,0:T(8,128)S(1)}) custom-call(s32[4]{0:T(128)S(1)} %get-tuple-element.77.meta, s32[140]{0:T(256)S(1)} %get-tuple-element.96.inv, f32[2,20]{1,0:T(2,128)S(1)} %copy-done.4, f32[20]{0:T(128)} %diffusion.3, ...), custom_call_target="tpu_custom_call" | custom-call | tf_op jit(solution)/shard_map/depth_sums/pallas_call | solution.py:147
  18.7 1.6 %collective-permute-start.7 = (f32[48,128]{1,0:T(8,128)S(1)}, f32[48,128]{1,0:T(8,128)S(1)}, u32[]{:S(2)}, u32[]{:S(2)}) collective-permute-start(f32[48,128]{1,0:T(8,128)S(1)} %get-tuple-element.38.after_ref), channel_id=1, source_target_pairs={{0,2},{1,3},{2,4},{3,5},{4,6},{5,7},{6,0},{7,1},{8,10},{9,11},{10,... | collective-permute-start | bytes 73736 | tf_op jit(solution)/shard_map/ppermute | solution.py:70
  20.3 1.5 %collective-permute-start.5 = (f32[432,128]{1,0:T(8,128)S(1)}, f32[432,128]{1,0:T(8,128)S(1)}, u32[]{:S(2)}, u32[]{:S(2)}) collective-permute-start(f32[432,128]{1,0:T(8,128)S(1)} %get-tuple-element.36), channel_id=1, source_target_pairs={{0,1},{1,0},{2,3},{3,2},{4,5},{5,4},{6,7},{7,6},{8,9},{9,8},{10,11... | collective-permute-start | bytes 663560 | tf_op jit(solution)/shard_map/ppermute | solution.py:55
  21.8 2.2 %collective-permute-start.6 = (f32[432,128]{1,0:T(8,128)S(1)}, f32[432,128]{1,0:T(8,128)S(1)}, u32[]{:S(2)}, u32[]{:S(2)}) collective-permute-start(f32[432,128]{1,0:T(8,128)S(1)} %get-tuple-element.37), channel_id=1, source_target_pairs={{0,7},{1,2},{2,1},{3,4},{4,3},{5,6},{6,5},{7,0},{8,15},{9,10},{10,... | collective-permute-start | bytes 663560 | tf_op jit(solution)/shard_map/ppermute | solution.py:55
  24.0 0.1 pad_add_fusion.meta
  24.1 0.1 reduce_max.31
  24.2 4.2 %column_strips.1 = (f32[160,128]{1,0:T(8,128)S(1)}, f32[160,128]{1,0:T(8,128)S(1)}) custom-call(s32[4]{0:T(128)S(1)} %get-tuple-element.77.meta, s32[140]{0:T(256)S(1)} %get-tuple-element.96.inv, f32[63,20,16,128]{3,2,1,0:T(8,128)} %bitcast.95, f32[48,128]{1,0:T(8,128)S(1)} %get-tuple-element.38.after_ref), custom_call_target="tpu_custom_call" | custom-call | tf_op jit(solution)/shard_map/column_strips/pallas_call | solution.py:508
  28.4 0.1 collective-permute-start.11
  28.5 1.6 %collective-permute-start.12 = (f32[160,128]{1,0:T(8,128)S(1)}, f32[160,128]{1,0:T(8,128)S(1)}, u32[]{:S(2)}, u32[]{:S(2)}) collective-permute-start(f32[160,128]{1,0:T(8,128)S(1)} %get-tuple-element.46), channel_id=1, source_target_pairs={{0,24},{8,16},{16,8},{24,0},{1,25},{9,17},{17,9},{25,1},{2,26},{10... | collective-permute-start | bytes 245768 | tf_op jit(solution)/shard_map/ppermute | solution.py:55
  30.1 0.0 collective-permute-done.7.far_ref
  30.1 1.5 %collective-permute-done.5.a_ref = f32[432,128]{1,0:T(8,128)S(1)} collective-permute-done((f32[432,128]{1,0:T(8,128)S(1)}, f32[432,128]{1,0:T(8,128)S(1)}, u32[]{:S(2)}, u32[]{:S(2)}) %collective-permute-start.5) | collective-permute-done | bytes 221216 | tf_op jit(solution)/shard_map/ppermute | solution.py:55
  31.6 0.0 collective-permute-done.6.b_ref
  31.6 1.6 %region_fields.1 = (f32[4,4,176,128]{3,2,1,0:T(8,128)S(1)}, f32[24,128]{1,0:T(8,128)S(1)}, f32[24,128]{1,0:T(8,128)S(1)}) custom-call(s32[4]{0:T(128)S(1)} %get-tuple-element.77.meta, s32[140]{0:T(256)S(1)} %get-tuple-element.97.inv, f32[504,128]{1,0:T(8,128)S(1)} %get-tuple-element.34.s_ref, f32[504,128]{1,0:T(8,128)S(1)} %get-tuple-element.35.q_ref, ...), custom_call_target="tpu_custom_call" | custom-call | tf_op jit(solution)/shard_map/region_fields/pallas_call | solution.py:279
  33.3 0.1 collective-permute-start.8
  33.4 1.6 %collective-permute-start.9 = (f32[24,128]{1,0:T(8,128)S(1)}, f32[24,128]{1,0:T(8,128)S(1)}, u32[]{:S(2)}, u32[]{:S(2)}) collective-permute-start(f32[24,128]{1,0:T(8,128)S(1)} %get-tuple-element.41), channel_id=1, source_target_pairs={{0,24},{8,16},{16,8},{24,0},{1,25},{9,17},{17,9},{25,1},{2,26},{10... | collective-permute-start | bytes 36872 | tf_op jit(solution)/shard_map/ppermute | solution.py:55
  35.0 0.1 maximum_reduce_fusion
  35.1 0.0 collective-permute-done.11.ga_ref
  35.1 0.0 collective-permute-done.12.gb_ref
  35.1 5.0 %link_strips.1 = (f32[328,128]{1,0:T(8,128)S(1)}, f32[328,128]{1,0:T(8,128)S(1)}) custom-call(s32[4]{0:T(128)S(1)} %get-tuple-element.77.meta, s32[44]{0:T(128)S(1)} %broadcast_add_fusion.2.table, f32[63,20,16,128]{3,2,1,0:T(8,128)} %bitcast.96, f32[160,128]{1,0:T(8,128)S(1)} %collective-permute-done.11.ga_ref, f32[160,128]{1,0:T(8,128)S(1)} %collective-permute-done.12.gb_ref), custom_call_target="tpu_custom_call" | custom-call | tf_op jit(solution)/shard_map/link_strips/pallas_call | solution.py:612
  40.2 1.7 %collective-permute-start.13 = (f32[328,128]{1,0:T(8,128)S(1)}, f32[328,128]{1,0:T(8,128)S(1)}, u32[]{:S(2)}, u32[]{:S(2)}) collective-permute-start(f32[328,128]{1,0:T(8,128)S(1)} %get-tuple-element.47), channel_id=1, source_target_pairs={{0,1},{1,0},{2,3},{3,2},{4,5},{5,4},{6,7},{7,6},{8,9},{9,8},{10,11... | collective-permute-start | bytes 503816 | tf_op jit(solution)/shard_map/ppermute | solution.py:55
  41.9 1.8 %collective-permute-start.14 = (f32[328,128]{1,0:T(8,128)S(1)}, f32[328,128]{1,0:T(8,128)S(1)}, u32[]{:S(2)}, u32[]{:S(2)}) collective-permute-start(f32[328,128]{1,0:T(8,128)S(1)} %get-tuple-element.48), channel_id=1, source_target_pairs={{0,7},{1,2},{2,1},{3,4},{4,3},{5,6},{6,5},{7,0},{8,15},{9,10},{10,... | collective-permute-start | bytes 503816 | tf_op jit(solution)/shard_map/ppermute | solution.py:55
  43.7 0.0 collective-permute-done.8.ca_ref
  43.7 0.0 collective-permute-done.9.cb_ref
  43.7 3.7 %solve_basis.1 = (f32[32,128]{1,0:T(8,128)}, f32[1680,128]{1,0:T(8,128)S(1)}, f32[528,128]{1,0:T(8,128)}) custom-call(s32[4]{0:T(128)S(1)} %pad_add_fusion.meta, s32[63]{0:T(128)S(1)} %collective-permute-done.4.came, f32[4,4,176,128]{3,2,1,0:T(8,128)S(1)} %get-tuple-element.39.f_ref, f32[24,128]{1,0:T(8,128)S(1)} %collective-permute-done.8.ca_ref, ...), custom_call_target="tpu_custom_call" | custom-call | tf_op jit(solution)/shard_map/solve_basis/pallas_call | solution.py:390
  47.4 3.3 %all-to-all-start = ((f32[32,1,128]{2,1,0:T(1,128)}), f32[32,1,128]{2,1,0:T(1,128)S(1)}, u32[]{:S(2)}, u32[]{:S(2)}) async-start(f32[32,1,128]{2,1,0:T(1,128)} %bitcast.29), calls=%async_computation | async-start | bytes 32768 | tf_op jit(solution)/shard_map/all_to_all | solution.py:903
  50.7 4.6 %collective-permute-start.10 = (f32[528,128]{1,0:T(8,128)}, f32[528,128]{1,0:T(8,128)}, u32[]{:S(2)}, u32[]{:S(2)}) collective-permute-start(f32[528,128]{1,0:T(8,128)} %get-tuple-element.44), channel_id=1, source_target_pairs={{0,7},{1,0},{2,1},{3,2},{4,3},{5,4},{6,5},{7,6},{8,15},{9,8},{10,9... | collective-permute-start | bytes 811016 | tf_op jit(solution)/shard_map/ppermute | solution.py:70
  55.3 0.5 copy.108
  55.8 0.2 reshape.464.table
  56.0 0.0 collective-permute-done.13.ha_ref
  56.0 0.0 collective-permute-done.14.hb_ref
  56.1 0.0 copy-done.9
  56.1 0.0 copy-start.8
  56.1 29.8 %step_tracers.1 = f32[20160,128]{1,0:T(8,128)} custom-call(s32[4]{0:T(128)S(1)} %get-tuple-element.77.meta, s32[1260]{0:T(1024)S(1)} %reshape.464.table, s32[9]{0:T(128)S(1)} %and_select_fusion.8.need, f32[20]{0:T(128)S(1)} %copy-done.9, f32[20160,128]{1,0:T(8,128)} %bitcast.97, f32[160,128]{1,0:T(8,128)S(1)} %collective-permute-done.11.ga_ref, ...), custom_call_target="tpu_custom_call" | custom-call | flops 36126720 | bytes 20643840 | tf_op jit(solution)/shard_map/step_tracers/pallas_call | solution.py:748
  85.9 0.0 all-to-all-done
  85.9 0.7 slice_reduce_fusion
  87.3 0.3 conditional.1
  87.5 0.0 collective-permute-done.10.back_ref
  87.6 0.4 copy-done.3
  87.9 2.0 %slot_pressure.1 = (f32[63,1024]{1,0:T(8,128)}, f32[63,20,16,128]{3,2,1,0:T(8,128)}) custom-call(s32[63]{0:T(128)S(1)} %copy-done.3, f32[32,128]{1,0:T(8,128)S(1)} %bitcast.87, f32[1680,128]{1,0:T(8,128)S(1)} %get-tuple-element.43.blocks_ref, f32[528,128]{1,0:T(8,128)} %collective-permute-done.10.back_ref, ...), custom_call_target="tpu_custom_call", output_to_operand_aliasing={{1}: (4, {})} | custom-call | tf_op jit(solution)/shard_map/slot_pressure/pallas_call | solution.py:458
  (27 shorter events, 0.1 us)
Async XLA Ops:
  1.3 7.9 %copy-start.2 = (s32[63]{0:T(128)}, s32[63]{0:T(128)S(1)}, u32[]{:S(2)}) copy-start(s32[63]{0:T(128)S(1)} %get-tuple-element.76.code) | copy-start | bytes 760
  1.4 7.8 %collective-permute-start.4 = (s32[63]{0:T(128)S(1)}, s32[63]{0:T(128)S(1)}, u32[]{:S(2)}, u32[]{:S(2)}) collective-permute-start(s32[63]{0:T(128)S(1)} %get-tuple-element.76.code), channel_id=1, source_target_pairs={{0,1},{1,2},{2,3},{3,4},{4,5},{5,6},{6,7},{7,0},{8,9},{9,10},{10,1... | collective-permute-start | bytes 764 | tf_op jit(solution)/shard_map/ppermute | solution.py:70
  9.3 1.0 %copy-start = (f32[160,448]{1,0:T(8,128)S(1)}, f32[160,448]{1,0:T(8,128)}, u32[]{:S(2)}) copy-start(f32[160,448]{1,0:T(8,128)} %surf_ref.1) | copy-start | bytes 860164
  10.3 0.7 copy-start.4
  10.9 20.7 %copy-start.1 = (f32[160,448]{1,0:T(8,128)S(1)}, f32[160,448]{1,0:T(8,128)}, u32[]{:S(2)}) copy-start(f32[160,448]{1,0:T(8,128)} %surf_ref.1) | copy-start | bytes 860164
  18.7 11.5 %collective-permute-start.7 = (f32[48,128]{1,0:T(8,128)S(1)}, f32[48,128]{1,0:T(8,128)S(1)}, u32[]{:S(2)}, u32[]{:S(2)}) collective-permute-start(f32[48,128]{1,0:T(8,128)S(1)} %get-tuple-element.38.after_ref), channel_id=1, source_target_pairs={{0,2},{1,3},{2,4},{3,5},{4,6},{5,7},{6,0},{7,1},{8,10},{9,11},{10,... | collective-permute-start | bytes 73736 | tf_op jit(solution)/shard_map/ppermute | solution.py:70
  20.3 11.3 %collective-permute-start.5 = (f32[432,128]{1,0:T(8,128)S(1)}, f32[432,128]{1,0:T(8,128)S(1)}, u32[]{:S(2)}, u32[]{:S(2)}) collective-permute-start(f32[432,128]{1,0:T(8,128)S(1)} %get-tuple-element.36), channel_id=1, source_target_pairs={{0,1},{1,0},{2,3},{3,2},{4,5},{5,4},{6,7},{7,6},{8,9},{9,8},{10,11... | collective-permute-start | bytes 663560 | tf_op jit(solution)/shard_map/ppermute | solution.py:55
  21.8 9.8 %collective-permute-start.6 = (f32[432,128]{1,0:T(8,128)S(1)}, f32[432,128]{1,0:T(8,128)S(1)}, u32[]{:S(2)}, u32[]{:S(2)}) collective-permute-start(f32[432,128]{1,0:T(8,128)S(1)} %get-tuple-element.37), channel_id=1, source_target_pairs={{0,7},{1,2},{2,1},{3,4},{4,3},{5,6},{6,5},{7,0},{8,15},{9,10},{10,... | collective-permute-start | bytes 663560 | tf_op jit(solution)/shard_map/ppermute | solution.py:55
  24.2 31.9 %copy-start.9 = (f32[20]{0:T(128)S(1)}, f32[20]{0:T(128)}, u32[]{:S(2)}) copy-start(f32[20]{0:T(128)} %diffusion.3) | copy-start | bytes 244
  28.4 6.7 %collective-permute-start.11 = (f32[160,128]{1,0:T(8,128)S(1)}, f32[160,128]{1,0:T(8,128)S(1)}, u32[]{:S(2)}, u32[]{:S(2)}) collective-permute-start(f32[160,128]{1,0:T(8,128)S(1)} %get-tuple-element.45), channel_id=1, source_target_pairs={{0,8},{8,0},{16,24},{24,16},{1,9},{9,1},{17,25},{25,17},{2,10},{10... | collective-permute-start | bytes 245768 | tf_op jit(solution)/shard_map/ppermute | solution.py:55
  28.5 6.6 %collective-permute-start.12 = (f32[160,128]{1,0:T(8,128)S(1)}, f32[160,128]{1,0:T(8,128)S(1)}, u32[]{:S(2)}, u32[]{:S(2)}) collective-permute-start(f32[160,128]{1,0:T(8,128)S(1)} %get-tuple-element.46), channel_id=1, source_target_pairs={{0,24},{8,16},{16,8},{24,0},{1,25},{9,17},{17,9},{25,1},{2,26},{10... | collective-permute-start | bytes 245768 | tf_op jit(solution)/shard_map/ppermute | solution.py:55
  33.3 10.4 %collective-permute-start.8 = (f32[24,128]{1,0:T(8,128)S(1)}, f32[24,128]{1,0:T(8,128)S(1)}, u32[]{:S(2)}, u32[]{:S(2)}) collective-permute-start(f32[24,128]{1,0:T(8,128)S(1)} %get-tuple-element.40), channel_id=1, source_target_pairs={{0,8},{8,0},{16,24},{24,16},{1,9},{9,1},{17,25},{25,17},{2,10},{10... | collective-permute-start | bytes 36872 | tf_op jit(solution)/shard_map/ppermute | solution.py:55
  33.4 10.3 %collective-permute-start.9 = (f32[24,128]{1,0:T(8,128)S(1)}, f32[24,128]{1,0:T(8,128)S(1)}, u32[]{:S(2)}, u32[]{:S(2)}) collective-permute-start(f32[24,128]{1,0:T(8,128)S(1)} %get-tuple-element.41), channel_id=1, source_target_pairs={{0,24},{8,16},{16,8},{24,0},{1,25},{9,17},{17,9},{25,1},{2,26},{10... | collective-permute-start | bytes 36872 | tf_op jit(solution)/shard_map/ppermute | solution.py:55
  40.2 15.9 %collective-permute-start.13 = (f32[328,128]{1,0:T(8,128)S(1)}, f32[328,128]{1,0:T(8,128)S(1)}, u32[]{:S(2)}, u32[]{:S(2)}) collective-permute-start(f32[328,128]{1,0:T(8,128)S(1)} %get-tuple-element.47), channel_id=1, source_target_pairs={{0,1},{1,0},{2,3},{3,2},{4,5},{5,4},{6,7},{7,6},{8,9},{9,8},{10,11... | collective-permute-start | bytes 503816 | tf_op jit(solution)/shard_map/ppermute | solution.py:55
  41.9 14.2 %collective-permute-start.14 = (f32[328,128]{1,0:T(8,128)S(1)}, f32[328,128]{1,0:T(8,128)S(1)}, u32[]{:S(2)}, u32[]{:S(2)}) collective-permute-start(f32[328,128]{1,0:T(8,128)S(1)} %get-tuple-element.48), channel_id=1, source_target_pairs={{0,7},{1,2},{2,1},{3,4},{4,3},{5,6},{6,5},{7,0},{8,15},{9,10},{10,... | collective-permute-start | bytes 503816 | tf_op jit(solution)/shard_map/ppermute | solution.py:55
  47.4 38.5 %all-to-all-start = ((f32[32,1,128]{2,1,0:T(1,128)}), f32[32,1,128]{2,1,0:T(1,128)S(1)}, u32[]{:S(2)}, u32[]{:S(2)}) async-start(f32[32,1,128]{2,1,0:T(1,128)} %bitcast.29), calls=%async_computation | async-start | bytes 32768 | tf_op jit(solution)/shard_map/all_to_all | solution.py:903
  50.7 36.8 %collective-permute-start.10 = (f32[528,128]{1,0:T(8,128)}, f32[528,128]{1,0:T(8,128)}, u32[]{:S(2)}, u32[]{:S(2)}) collective-permute-start(f32[528,128]{1,0:T(8,128)} %get-tuple-element.44), channel_id=1, source_target_pairs={{0,7},{1,0},{2,1},{3,2},{4,3},{5,4},{6,5},{7,6},{8,15},{9,8},{10,9... | collective-permute-start | bytes 811016 | tf_op jit(solution)/shard_map/ppermute | solution.py:70
  56.1 31.2 %copy-start.8 = (s32[63,4]{0,1:T(4,128)S(1)}, s32[63,4]{0,1:T(4,128)}, u32[]{:S(2)}) copy-start(s32[63,4]{0,1:T(4,128)} %param.14) | copy-start | bytes 3028
  87.3 0.7 copy-start.3

commit v3 on v2

--- a/solution.py
+++ b/solution.py
@@ -19,6 +19,7 @@
 ROWS = 16
 HALF = LEVELS // 2
 STEP_SLOTS = 7
+IMAGE = LEVELS * ROWS
 FIELD_ROWS = 176
 FIELD_TILES = 4
 CAP_WE = 6
@@ -29,11 +30,13 @@
 RIM_Q = RIM_S + 16
 RIM_M = RIM_Q + 16
 SURF = RIM_M + 16
-MESSAGE = SURF + FIELD_TILES * TILE
+IDS = SURF + FIELD_TILES * TILE
+MESSAGE = IDS + TILE
 F32 = jnp.float32
 SMEM = pl.BlockSpec(memory_space=pltpu.SMEM)
 VMEM = pl.BlockSpec(memory_space=pltpu.VMEM)
 ANY = pl.BlockSpec(memory_space=pl.ANY)
+HBM = pl.BlockSpec(memory_space=pltpu.HBM)
 
 
 def lane_id(shape):
@@ -70,29 +73,57 @@
     return lax.ppermute(x, axis, [(i, (i + by) % length) for i in range(length)])
 
 
-def sums_kernel(meta, inv, weight, diffusion, t_ref, low_ref, high_ref, s_ref, q_ref, a_ref, b_ref, far_ref, part):
-    step = pl.program_id(0)
-    slots = s_ref.shape[0] // TILE
+def sums_kernel(meta, code, weight, diffusion, t_ref, surf_ref, s_ref, q_ref, a_ref, b_ref, far_ref, inv, own, part, edges, sems, sem_low, sem_high):
+    slots = own.shape[0]
+    chunks = slots // STEP_SLOTS
+    height = surf_ref.shape[0]
+
+    def fetch(c):
+        part = pl.ds(c * STEP_SLOTS, STEP_SLOTS)
+        return pltpu.make_async_copy(t_ref.at[part], own.at[part], sems.at[c])
+
+    def fetch_low():
+        return pltpu.make_async_copy(surf_ref.at[pl.ds(0, TILE), :], edges.at[0], sem_low)
+
+    def fetch_high():
+        return pltpu.make_async_copy(surf_ref.at[pl.ds(height - TILE, TILE), :], edges.at[1], sem_high)
+
+    for c in range(chunks):
+        fetch(c).start()
+    fetch_low().start()
+    fetch_high().start()
+    for r in range(2 * REGION):
+        inv[r] = -1
+    for s in range(slots):
+        inv[code[s]] = s
     tracer = lax.broadcasted_iota(jnp.int32, (TILE, LANES), 0) % 2
     pairs = [(n, h) for n in range(STEP_SLOTS) for h in range(2)]
-    acc_s = {p: jnp.zeros((TILE, LANES), F32) for p in pairs}
-    acc_q = {p: jnp.zeros((TILE, LANES), F32) for p in pairs}
-    for level in range(LEVELS):
-        w = jnp.where(tracer == 0, weight[0, level], weight[1, level])
-        wd = w * diffusion[level]
+
+    def sum_chunk(c, carry):
+        fetch(c).wait()
+        acc_s = {p: jnp.zeros((TILE, LANES), F32) for p in pairs}
+        acc_q = {p: jnp.zeros((TILE, LANES), F32) for p in pairs}
+        for level in range(LEVELS):
+            w = jnp.where(tracer == 0, weight[0, level], weight[1, level])
+            wd = w * diffusion[level]
+            for n, h in pairs:
+                x = own[c * STEP_SLOTS + n, pl.ds(level * ROWS + h * TILE, TILE), :]
+                acc_s[n, h] = acc_s[n, h] + w * x
+                acc_q[n, h] = acc_q[n, h] + wd * x
         for n, h in pairs:
-            x = t_ref[n, level, pl.ds(h * TILE, TILE), :]
-            acc_s[n, h] = acc_s[n, h] + w * x
-            acc_q[n, h] = acc_q[n, h] + wd * x
-    for n, h in pairs:
-        part[0, pl.ds(n * ROWS + h * TILE, TILE), :] = acc_s[n, h]
-        part[1, pl.ds(n * ROWS + h * TILE, TILE), :] = acc_q[n, h]
-    for n in range(STEP_SLOTS):
-        row = pl.multiple_of((step * STEP_SLOTS + n) * TILE, TILE)
-        for kind, out in ((0, s_ref), (1, q_ref)):
-            even = part[kind, pl.ds(n * ROWS, TILE, stride=2), :]
-            odd = part[kind, pl.ds(n * ROWS + 1, TILE, stride=2), :]
-            out[pl.ds(row, TILE), :] = even + odd
+            part[0, pl.ds(n * ROWS + h * TILE, TILE), :] = acc_s[n, h]
+            part[1, pl.ds(n * ROWS + h * TILE, TILE), :] = acc_q[n, h]
+        for n in range(STEP_SLOTS):
+            row = pl.multiple_of((c * STEP_SLOTS + n) * TILE, TILE)
+            for kind, out in ((0, s_ref), (1, q_ref)):
+                even = part[kind, pl.ds(n * ROWS, TILE, stride=2), :]
+                odd = part[kind, pl.ds(n * ROWS + 1, TILE, stride=2), :]
+                out[pl.ds(row, TILE), :] = even + odd
+        return carry
+
+    lax.fori_loop(0, chunks, sum_chunk, 0)
+    fetch_low().wait()
+    fetch_high().wait()
 
     def rim(dest, base, first, chunk):
         for k in range(REG_X):
@@ -109,11 +140,16 @@
     def surface(dest, edge):
         for b in range(FIELD_TILES):
             if b < 3:
-                dest[pl.ds(SURF + b * TILE, TILE), :] = edge[:, pl.ds(b * LANES, LANES)]
+                dest[pl.ds(SURF + b * TILE, TILE), :] = edges[edge, :, pl.ds(b * LANES, LANES)]
             else:
-                width = edge.shape[1] - b * LANES
+                width = edges.shape[2] - b * LANES
                 dest[pl.ds(SURF + b * TILE, TILE), :] = jnp.zeros((TILE, LANES), F32)
-                dest[pl.ds(SURF + b * TILE, TILE), pl.ds(0, width)] = edge[:, pl.ds(b * LANES, width)]
+                dest[pl.ds(SURF + b * TILE, TILE), pl.ds(0, width)] = edges[edge, :, pl.ds(b * LANES, width)]
+
+    lane = lane_id((TILE, LANES))
+    ids = jnp.full((TILE, LANES), -1.0, F32)
+    for k in range(MOVED):
+        ids = jnp.where(lane == k, (code[slots - MOVED + k] - REGION).astype(F32), ids)
 
     def messages(up, down):
         height = MOVED * TILE
@@ -121,59 +157,43 @@
         up[pl.ds(0, height), :] = s_ref[pl.ds(first, height), :]
         up[pl.ds(height, height), :] = q_ref[pl.ds(first, height), :]
         rim(up, RIM_S, REGION - REG_X, TILE - 1)
-        surface(up, high_ref)
+        surface(up, 1)
+        up[pl.ds(IDS, TILE), :] = ids
         down[pl.ds(0, 2 * height), :] = jnp.zeros((2 * height, LANES), F32)
         rim(down, RIM_S, 0, 0)
-        surface(down, low_ref)
-
-    @pl.when(step == pl.num_programs(0) - 1)
+        surface(down, 0)
+        down[pl.ds(IDS, TILE), :] = ids
+
+    rim(far_ref, 0, 2 * REGION - REG_X, TILE - 1)
+
+    @pl.when(meta[1] % 2 == 0)
     def _():
-        rim(far_ref, 0, 2 * REGION - REG_X, TILE - 1)
-
-        @pl.when(meta[1] % 2 == 0)
-        def _():
-            messages(a_ref, b_ref)
-
-        @pl.when(meta[1] % 2 == 1)
-        def _():
-            messages(b_ref, a_ref)
-
-
-def depth_sums(view, meta, places, weight, diffusion, surface):
+        messages(a_ref, b_ref)
+
+    @pl.when(meta[1] % 2 == 1)
+    def _():
+        messages(b_ref, a_ref)
+
+
+def depth_sums(view, meta, code, weight, diffusion, surface):
     slots = view.shape[0]
-    steps = slots // STEP_SLOTS
-    rows, width = surface.shape
-    whole = lambda *shape: pl.BlockSpec(shape, lambda s: (0,) * len(shape))
+    shapes = [(slots * TILE, LANES), (slots * TILE, LANES), (MESSAGE, LANES), (MESSAGE, LANES), (48, LANES)]
     return pl.pallas_call(
         sums_kernel,
-        grid=(steps,),
-        in_specs=[
-            SMEM,
-            SMEM,
-            SMEM,
-            SMEM,
-            pl.BlockSpec((STEP_SLOTS, LEVELS, ROWS, LANES), lambda s: (s, 0, 0, 0)),
-            pl.BlockSpec((TILE, width), lambda s: (0, 0)),
-            pl.BlockSpec((TILE, width), lambda s: (rows // TILE - 1, 0)),
+        in_specs=[SMEM] * 4 + [HBM, HBM],
+        out_specs=[VMEM] * 5 + [SMEM],
+        out_shape=[jax.ShapeDtypeStruct(x, F32) for x in shapes] + [jax.ShapeDtypeStruct((2 * REGION,), jnp.int32)],
+        scratch_shapes=[
+            pltpu.VMEM((slots, IMAGE, LANES), F32),
+            pltpu.VMEM((2, STEP_SLOTS * ROWS, LANES), F32),
+            pltpu.VMEM((2, TILE, surface.shape[1]), F32),
+            pltpu.SemaphoreType.DMA((slots // STEP_SLOTS,)),
+            pltpu.SemaphoreType.DMA,
+            pltpu.SemaphoreType.DMA,
         ],
-        out_specs=[
-            whole(slots * TILE, LANES),
-            whole(slots * TILE, LANES),
-            whole(MESSAGE, LANES),
-            whole(MESSAGE, LANES),
-            whole(48, LANES),
-        ],
-        out_shape=[
-            jax.ShapeDtypeStruct((slots * TILE, LANES), F32),
-            jax.ShapeDtypeStruct((slots * TILE, LANES), F32),
-            jax.ShapeDtypeStruct((MESSAGE, LANES), F32),
-            jax.ShapeDtypeStruct((MESSAGE, LANES), F32),
-            jax.ShapeDtypeStruct((48, LANES), F32),
-        ],
-        scratch_shapes=[pltpu.VMEM((2, STEP_SLOTS * ROWS, LANES), F32)],
-        compiler_params=pltpu.CompilerParams(vmem_limit_bytes=12 << 20),
+        compiler_params=pltpu.CompilerParams(vmem_limit_bytes=52 << 20),
         name="depth_sums",
-    )(meta, places, weight, diffusion, view, surface, surface)
+    )(meta, code, weight, diffusion, view.reshape(slots, IMAGE, LANES), surface)
 
 
 def field_kernel(meta, inv, s_ref, q_ref, a_ref, b_ref, far_ref, surf_ref, f_ref, ca_ref, cb_ref):
@@ -290,7 +310,7 @@
     )(meta, places, s, q, a, b, far, surface)
 
 
-def basis_kernel(meta, came, f_ref, ca_ref, cb_ref, g_ref, blocks_ref, back_ref, u_ref):
+def basis_kernel(meta, moved, f_ref, ca_ref, cb_ref, g_ref, blocks_ref, back_ref, u_ref):
     even = meta[0] % 2 == 0
     lane = lane_id((TILE, LANES))
     tiles = range(FIELD_TILES)
@@ -378,15 +398,14 @@
                         part = turn(value[q], BLOCK * (q - g), 1)
                         tile = part if q == 0 else jnp.where(group == q, part, tile)
                     blocks_ref[pl.ds((k * REGION + by * REG_X + 4 * b + g) * TILE, TILE), :] = tile
-    first = came.shape[0] - MOVED
     for m in range(MOVED):
-        at = pl.multiple_of(jnp.maximum(came[first + m] - REGION, 0) * TILE, TILE)
+        at = pl.multiple_of(jnp.maximum(moved[m], 0) * TILE, TILE)
         for k in range(3):
             tile = blocks_ref[pl.ds(k * REGION * TILE + at, TILE), :]
             back_ref[pl.ds((k * MOVED + m) * TILE, TILE), :] = tile
 
 
-def solve_basis(meta, came, fields, ca, cb, devices):
+def solve_basis(meta, moved, fields, ca, cb, devices):
     return pl.pallas_call(
         basis_kernel,
         in_specs=[SMEM, SMEM, VMEM, VMEM, VMEM],
@@ -399,7 +418,7 @@
         scratch_shapes=[pltpu.VMEM((3, FIELD_TILES, FIELD_ROWS - 2 * TILE, LANES), F32)],
         compiler_params=pltpu.CompilerParams(vmem_limit_bytes=24 << 20),
         name="solve_basis",
-    )(meta, came, fields, ca, cb)
+    )(meta, moved, fields, ca, cb)
 
 
 def pressure_kernel(code, g_ref, blocks_ref, back_ref, held_ref, out_ref, same_ref, work):
@@ -484,40 +503,46 @@
     for k in range(count):
         for c in copies(k):
             c.start()
-    for k in range(count):
-        for c in copies(k):
-            c.wait()
     column = lane_id((ROWS, LANES)) % BLOCK
-    for level in range(HALF):
-        out_w = jnp.zeros((ROWS, LANES), F32)
-        out_e = jnp.zeros((ROWS, LANES), F32)
-        for k in range(count):
-            has_w, has_e = inv[REG_X * k] >= 0, inv[REG_X * k + REG_X - 1] >= 0
-            for part in range(2):
-                lane = k + 16 * part
-                here = column == lane
-                at = level + HALF * part
-                out_w = jnp.where(here & has_w, turn(west[k, at], lane, 1), out_w)
-                out_e = jnp.where(here & has_e, turn(east[k, at], lane - (BLOCK - 1), 1), out_e)
-        a_ref[pl.ds(level * ROWS, ROWS), :] = jnp.where(even, out_e, out_w)
-        b_ref[pl.ds(level * ROWS, ROWS), :] = jnp.where(even, out_w, out_e)
+    for first in (0, REG_Y):
+        for k in range(first, first + REG_Y):
+            for c in copies(k):
+                c.wait()
+        for level in range(HALF):
+            at = pl.ds(level * ROWS, ROWS)
+            if first:
+                out_a, out_b = a_ref[at, :], b_ref[at, :]
+                out_w, out_e = jnp.where(even, out_b, out_a), jnp.where(even, out_a, out_b)
+            else:
+                out_w = out_e = jnp.zeros((ROWS, LANES), F32)
+            for k in range(first, first + REG_Y):
+                has_w, has_e = inv[REG_X * k] >= 0, inv[REG_X * k + REG_X - 1] >= 0
+                for part in range(2):
+                    lane = k + 16 * part
+                    here = column == lane
+                    x = pl.ds((level + HALF * part) * ROWS, ROWS)
+                    out_w = jnp.where(here & has_w, turn(west[k, x, :], lane, 1), out_w)
+                    out_e = jnp.where(here & has_e, turn(east[k, x, :], lane - (BLOCK - 1), 1), out_e)
+            a_ref[at, :] = jnp.where(even, out_e, out_w)
+            b_ref[at, :] = jnp.where(even, out_w, out_e)
 
 
 def column_strips(meta, places, view, after):
     count = 2 * REG_Y
     return pl.pallas_call(
         columns_kernel,
-        in_specs=[SMEM, SMEM, ANY, ANY],
+        in_specs=[SMEM, SMEM, HBM, ANY],
         out_specs=[VMEM] * 2,
         out_shape=[jax.ShapeDtypeStruct((HALF * ROWS, LANES), F32)] * 2,
         scratch_shapes=[
-            pltpu.VMEM((count, LEVELS, ROWS, LANES), F32),
-            pltpu.VMEM((count, LEVELS, ROWS, LANES), F32),
+            pltpu.VMEM((count, IMAGE, LANES), F32),
+            pltpu.VMEM((count, IMAGE, LANES), F32),
             pltpu.SemaphoreType.DMA((2, count)),
         ],
-        compiler_params=pltpu.CompilerParams(vmem_limit_bytes=12 << 20),
+        compiler_params=pltpu.CompilerParams(vmem_limit_bytes=52 << 20),
+        cost_estimate=pl.CostEstimate(flops=1, bytes_accessed=1, transcendentals=0),
         name="column_strips",
-    )(meta, places, view, after)
+    )(meta, places, view.reshape(view.shape[0], IMAGE, LANES), after)
 
 
 def links_kernel(meta, table, t_ref, ga_ref, gb_ref, a_ref, b_ref, whole, half, sem_we, sem_ns):
@@ -531,7 +556,8 @@
     def ns_copy(way, k):
         link = jnp.maximum(table[way * (CAP_WE + CAP_NS) + CAP_WE + k], 2)
         rows = pl.ds(pl.multiple_of((link % 4 - 2) * TILE, TILE), TILE)
-        return pltpu.make_async_copy(t_ref.at[link // 4, :, rows, :], half.at[way, k], sem_ns.at[way, k])
+        dest = half.at[way, k, :, pl.ds(TILE, TILE), :]
+        return pltpu.make_async_copy(t_ref.at[link // 4, :, rows, :], dest, sem_ns.at[way, k])
 
     for way in range(2):
         for k in range(CAP_WE):
@@ -540,9 +566,7 @@
                 we_copy(way, k).start()
 
         for k in range(CAP_NS):
-            @pl.when(table[way * (CAP_WE + CAP_NS) + CAP_WE + k] >= 0)
-            def _():
-                ns_copy(way, k).start()
+            ns_copy(way, k).start()
 
     column = lane_id((HALF * ROWS, LANES)) % 16
     from_west = jnp.where(even_x, gb_ref[...], ga_ref[...])
@@ -552,7 +576,7 @@
 
     def message(way, out):
         out[pl.ds(0, HALF * ROWS), :] = relays[way]
-        out[pl.ds(HALF * ROWS, (LEVELS + 1) * TILE), :] = jnp.zeros(((LEVELS + 1) * TILE, LANES), F32)
+        out[pl.ds(HALF * ROWS + LEVELS * TILE, TILE), :] = jnp.zeros((TILE, LANES), F32)
         lane32 = lane_id((ROWS, LANES)) % BLOCK
         for k in range(CAP_WE):
             link = table[way * (CAP_WE + CAP_NS) + k]
@@ -571,30 +595,19 @@
                         value = jnp.where(lane32 == lane, x, value)
                     out[at, :] = value
 
-        row = lax.broadcasted_iota(jnp.int32, (LEVELS, TILE, LANES), 1)
-        group = lane_id((LEVELS, TILE, LANES)) // BLOCK
-        base = HALF * ROWS
+        links = [jnp.maximum(table[way * (CAP_WE + CAP_NS) + CAP_WE + k], 2) for k in range(CAP_NS)]
+        first = [TILE + 6 * (links[k] % 4 - 2) - 2 * (k // 4) for k in range(CAP_NS)]
+        by = [(BLOCK * (k % 4) + BLOCK * (links[k] % 4 - 2)) % LANES for k in range(CAP_NS)]
         for k in range(CAP_NS):
-            link = table[way * (CAP_WE + CAP_NS) + CAP_WE + k]
-
-            @pl.when(link >= 0)
-            def _():
-                ns_copy(way, k).wait()
-                x = half[way, k]
-
-                def put(x):
-                    keep = (row // 2 == k // 4) & (group == k % 4)
-                    old = out[pl.ds(base, LEVELS * TILE), :].reshape(LEVELS, TILE, LANES)
-                    new = jnp.where(keep, x, old)
-                    out[pl.ds(base, LEVELS * TILE), :] = new.reshape(LEVELS * TILE, LANES)
-
-                @pl.when(link % 4 == 2)
-                def _():
-                    put(turn(turn(x, 2 * (k // 4), 1), BLOCK * (k % 4), 2))
-
-                @pl.when(link % 4 == 3)
-                def _():
-                    put(turn(turn(x, 2 * (k // 4) + 2, 1), BLOCK * (k % 4) + BLOCK, 2))
+            ns_copy(way, k).wait()
+        row = lax.broadcasted_iota(jnp.int32, (TILE, LANES), 0) // 2
+        place = row * 4 + lane_id((TILE, LANES)) // BLOCK
+        for level in range(LEVELS):
+            value = jnp.zeros((TILE, LANES), F32)
+            for k in range(CAP_NS):
+                x = pltpu.roll(half[way, k, level, pl.ds(first[k], TILE), :], by[k], 1)
+                value = jnp.where(place == k, x, value)
+            out[pl.ds(HALF * ROWS + level * TILE, TILE), :] = value
 
     @pl.when(even_y)
     def _():
@@ -611,71 +624,74 @@
     rows = LINK_ROWS
     return pl.pallas_call(
         links_kernel,
-        in_specs=[SMEM, SMEM, ANY, VMEM, VMEM],
+        in_specs=[SMEM, SMEM, HBM, VMEM, VMEM],
         out_specs=[VMEM] * 2,
         out_shape=[jax.ShapeDtypeStruct((rows, LANES), F32)] * 2,
         scratch_shapes=[
             pltpu.VMEM((2, CAP_WE, LEVELS, ROWS, LANES), F32),
-            pltpu.VMEM((2, CAP_NS, LEVELS, TILE, LANES), F32),
+            pltpu.VMEM((2, CAP_NS, LEVELS, 3 * TILE, LANES), F32),
             pltpu.SemaphoreType.DMA((2, CAP_WE)),
             pltpu.SemaphoreType.DMA((2, CAP_NS)),
         ],
-        compiler_params=pltpu.CompilerParams(vmem_limit_bytes=12 << 20),
+        compiler_params=pltpu.CompilerParams(vmem_limit_bytes=52 << 20),
         name="link_strips",
     )(meta, table, view, ga, gb)
 
 
-IMAGE = LEVELS * ROWS
-FIELDS = 5
 BOX_LOW = 2 * HALF * ROWS
 BOX_HIGH = BOX_LOW + LINK_ROWS
 BOX = BOX_HIGH + LINK_ROWS
 
 
-def tracer_kernel(meta, table, need, diffusion, t_ref, ga_ref, gb_ref, ha_ref, hb_ref, out_ref, own, up, down, box, seen, sems):
-    step = pl.program_id(0)
-    slots = own.shape[0] // IMAGE
-    chunk = STEP_SLOTS * IMAGE
+def tracer_kernel(meta, table, need, diffusion, t_ref, ga_ref, gb_ref, ha_ref, hb_ref, out_ref, own, up, down, box, sems, out_sems):
+    slots = own.shape[0]
     chunks = slots // STEP_SLOTS
 
     def fetch(c):
-        rows = pl.ds(pl.multiple_of(c * chunk, TILE), chunk)
-        return pltpu.make_async_copy(t_ref.at[rows], own.at[rows], sems.at[c])
-
-    @pl.when(step == 0)
-    def _():
-        for c in range(chunks):
-            fetch(c).start()
-        seen[0] = 0
-        even_x = meta[0] % 2 == 0
-        even_y = meta[1] % 2 == 0
-        land = pl.ds(TILE + slots * IMAGE - TILE, IMAGE + 2 * TILE)
-        up[land, :] = jnp.zeros((IMAGE + 2 * TILE, LANES), F32)
-        down[land, :] = jnp.zeros((IMAGE + 2 * TILE, LANES), F32)
-        for first, second, size, low, high in (
-            (ga_ref, gb_ref, HALF * ROWS, 0, HALF * ROWS),
-            (ha_ref, hb_ref, LINK_ROWS, BOX_LOW, BOX_HIGH),
-        ):
-            even = even_x if low == 0 else even_y
-            box[pl.ds(low, size), :] = jnp.where(even, second[...], first[...])
-            box[pl.ds(high, size), :] = jnp.where(even, first[...], second[...])
+        part = pl.ds(c * STEP_SLOTS, STEP_SLOTS)
+        return pltpu.make_async_copy(t_ref.at[part], own.at[part], sems.at[c])
+
+    def keep(c):
+        part = pl.ds(c * STEP_SLOTS, STEP_SLOTS)
+        return pltpu.make_async_copy(own.at[part], out_ref.at[part], out_sems.at[c])
+
+    for c in range(chunks):
+        fetch(c).start()
+    even_x = meta[0] % 2 == 0
+    even_y = meta[1] % 2 == 0
+    up[slots] = jnp.zeros(up.shape[1:], F32)
+    down[slots] = jnp.zeros(up.shape[1:], F32)
+    for first, second, size, low, high in (
+        (ga_ref, gb_ref, HALF * ROWS, 0, HALF * ROWS),
+        (ha_ref, hb_ref, LINK_ROWS, BOX_LOW, BOX_HIGH),
+    ):
+        even = even_x if low == 0 else even_y
+        box[pl.ds(low, size), :] = jnp.where(even, second[...], first[...])
+        box[pl.ds(high, size), :] = jnp.where(even, first[...], second[...])
+    for way, low in enumerate((BOX_LOW, BOX_HIGH)):
+        for level in range(LEVELS):
+            x = box[pl.ds(low + HALF * ROWS + level * TILE, TILE), :]
+            for d in range(4):
+                y = turn(x, BLOCK * d, 1)
+                up[slots + 1 + 4 * way + d, pl.ds(TILE + level * ROWS, TILE), :] = y
+                down[slots + 1 + 4 * way + d, pl.ds(TILE + level * ROWS, TILE), :] = y
+    for level in range(LEVELS):
+        part = level // HALF
+        w = box[pl.ds((level % HALF) * ROWS, ROWS), :]
+        e = box[pl.ds((HALF + level % HALF) * ROWS, ROWS), :]
+        for k in range(2 * REG_Y):
+            down[slots + 9 + k, pl.ds(TILE + level * ROWS, ROWS), :] = turn(w, -1 - k - 16 * part, 1)
+            up[slots + 9 + k, pl.ds(TILE + level * ROWS, ROWS), :] = turn(e, BLOCK - k - 16 * part, 1)
 
     def arrive(c, carry):
         fetch(c).wait()
-
-        def roll_slot(n, carry):
-            base = pl.multiple_of((c * STEP_SLOTS + n) * IMAGE, TILE)
+        for n in range(STEP_SLOTS):
+            s = c * STEP_SLOTS + n
             for level in range(LEVELS):
-                x = own[pl.ds(base + level * ROWS, ROWS), :]
-                up[pl.ds(base + TILE + level * ROWS, ROWS), :] = pltpu.roll(x, BLOCK, 1)
-                down[pl.ds(base + TILE + level * ROWS, ROWS), :] = pltpu.roll(x, LANES - BLOCK, 1)
-            return carry
-
-        return lax.fori_loop(0, STEP_SLOTS, roll_slot, carry)
-
-    upto = jnp.maximum(seen[0], need[step] + 1)
-    lax.fori_loop(seen[0], upto, arrive, 0)
-    seen[0] = upto
+                x = own[s, pl.ds(level * ROWS, ROWS), :]
+                up[s, pl.ds(TILE + level * ROWS, ROWS), :] = pltpu.roll(x, BLOCK, 1)
+                down[s, pl.ds(TILE + level * ROWS, ROWS), :] = pltpu.roll(x, LANES - BLOCK, 1)
+        return carry
 
     cells = (ROWS, LANES)
     lane = lane_id(cells)
@@ -689,80 +705,79 @@
         jnp.where((row >= ROWS - 2) & (lane >= LANES - BLOCK), 1.0, 0.0),
     )
 
-    def one_slot(n, carry):
-        s = step * STEP_SLOTS + n
-        entry = [[table[(s * 4 + t) * FIELDS + f] for f in range(FIELDS)] for t in range(4)]
-        count = jnp.full(cells, 4.0, F32)
-        for t in range(4):
-            count = count - edge[t] * entry[t][4].astype(F32)
-        base = pl.multiple_of(s * IMAGE, TILE)
-        west, east, south, north = [pl.multiple_of(entry[t][0] * IMAGE, TILE) + TILE for t in range(4)]
-
+    def unpack(n, s):
         for t, dest in ((0, down), (1, up)):
-            @pl.when(entry[t][1] == 1)
+            at = s * 4 + t
+
+            @pl.when(table[1, at] == 1)
             def _():
-                first, by = pl.multiple_of(entry[t][2], TILE), entry[t][3]
+                first, by = pl.multiple_of(table[2, at], TILE), table[3, at]
                 for level in range(LEVELS):
                     part = level // HALF
                     x = box[pl.ds(first + (level % HALF) * ROWS, ROWS), :]
                     x = pltpu.roll(x, (by + LANES - 16 * part) % LANES, 1)
-                    dest[pl.ds(TILE + (slots + 1) * IMAGE + level * ROWS, ROWS), :] = x
-
-        for t, dest, offset in ((2, up, ROWS - 2), (3, down, -6)):
-            @pl.when(entry[t][1] == 1)
-            def _():
-                first, by = entry[t][2], entry[t][3]
-                for level in range(LEVELS):
-                    x = pltpu.roll(box[pl.ds(first + level * TILE, TILE), :], by, 1)
-                    dest[pl.ds(TILE + (slots + 3) * IMAGE + level * ROWS + offset, TILE), :] = x
-
+                    dest[slots + 19 + n, pl.ds(TILE + level * ROWS, ROWS), :] = x
+
+    def step(n, s):
+        count = jnp.full(cells, 4.0, F32)
+        for t in range(4):
+            count = count - edge[t] * table[4, s * 4 + t].astype(F32)
+        west, east, south, north = [table[0, s * 4 + t] for t in range(4)]
+        south_at, north_at = TILE + table[2, s * 4 + 2], TILE + table[2, s * 4 + 3]
         for level in range(LEVELS):
             at = level * ROWS
-            x = own[pl.ds(base + at, ROWS), :]
-            under = up[pl.ds(base + TILE + at - 2, ROWS), :]
-            over = down[pl.ds(base + TILE + at + 2, ROWS), :]
-            low = up[pl.ds(south + at + ROWS - 2, TILE), :]
-            high = down[pl.ds(north + at - 6, TILE), :]
+            x = own[s, pl.ds(at, ROWS), :]
+            under = up[s, pl.ds(TILE + at - 2, ROWS), :]
+            over = down[s, pl.ds(TILE + at + 2, ROWS), :]
+            low = up[south, pl.ds(south_at + at, TILE), :]
+            high = down[north, pl.ds(north_at + at, TILE), :]
             under = jnp.concatenate([jnp.where(row8 < 2, low, under[:TILE]), under[TILE:]], axis=0)
             over = jnp.concatenate([over[:TILE], jnp.where(row8 >= TILE - 2, high, over[TILE:])], axis=0)
-            total = jnp.where(lane < BLOCK, under, up[pl.ds(base + TILE + at, ROWS), :])
-            total = total + jnp.where(lane >= LANES - BLOCK, over, down[pl.ds(base + TILE + at, ROWS), :])
-            w = down[pl.ds(west + at, ROWS), :]
-            e = up[pl.ds(east + at, ROWS), :]
+            total = jnp.where(lane < BLOCK, under, up[s, pl.ds(TILE + at, ROWS), :])
+            total = total + jnp.where(lane >= LANES - BLOCK, over, down[s, pl.ds(TILE + at, ROWS), :])
+            w = down[west, pl.ds(TILE + at, ROWS), :]
+            e = up[east, pl.ds(TILE + at, ROWS), :]
             total = total + pltpu.roll(jnp.where(column == BLOCK - 1, w, x), 1, 1)
             total = total + pltpu.roll(jnp.where(column == 0, e, x), LANES - 1, 1)
-            out_ref[pl.ds(pl.multiple_of(n * IMAGE, TILE) + at, ROWS), :] = x + diffusion[level] * (total - count * x)
-        return carry
-
-    lax.fori_loop(0, STEP_SLOTS, one_slot, 0)
-
-    @pl.when(step == pl.num_programs(0) - 1)
-    def _():
-        lax.fori_loop(seen[0], chunks, arrive, 0)
+            own[s, pl.ds(at, ROWS), :] = x + diffusion[level] * (total - count * x)
+
+    def work(c, seen):
+        upto = jnp.maximum(seen, need[c] + 1)
+        lax.fori_loop(seen, upto, arrive, 0)
+        for n in range(STEP_SLOTS):
+            unpack(n, c * STEP_SLOTS + n)
+        for n in range(STEP_SLOTS):
+            step(n, c * STEP_SLOTS + n)
+        keep(c).start()
+        return upto
+
+    lax.fori_loop(0, chunks, work, 0)
+    for c in range(chunks):
+        keep(c).wait()
 
 
 def step_tracers(meta, table, need, diffusion, view, ga, gb, ha, hb):
     slots = view.shape[0]
-    steps = slots // STEP_SLOTS
-    rows = slots * IMAGE
+    chunks = slots // STEP_SLOTS
+    size = slots * IMAGE * LANES
+    images = slots + 19 + STEP_SLOTS
     out = pl.pallas_call(
         tracer_kernel,
-        grid=(steps,),
-        in_specs=[SMEM] * 4 + [ANY] + [VMEM] * 4,
-        out_specs=pl.BlockSpec((STEP_SLOTS * IMAGE, LANES), lambda s: (s, 0)),
-        out_shape=jax.ShapeDtypeStruct((rows, LANES), F32),
+        in_specs=[SMEM] * 4 + [HBM] + [VMEM] * 4,
+        out_specs=HBM,
+        out_shape=jax.ShapeDtypeStruct((slots, IMAGE, LANES), F32),
         scratch_shapes=[
-            pltpu.VMEM((rows, LANES), F32),
-            pltpu.VMEM((rows + 4 * IMAGE + 2 * TILE, LANES), F32),
-            pltpu.VMEM((rows + 4 * IMAGE + 2 * TILE, LANES), F32),
+            pltpu.VMEM((slots, IMAGE, LANES), F32),
+            pltpu.VMEM((images, IMAGE + 2 * TILE, LANES), F32),
+            pltpu.VMEM((images, IMAGE + 2 * TILE, LANES), F32),
             pltpu.VMEM((BOX, LANES), F32),
-            pltpu.SMEM((1,), jnp.int32),
-            pltpu.SemaphoreType.DMA((steps,)),
+            pltpu.SemaphoreType.DMA((chunks,)),
+            pltpu.SemaphoreType.DMA((chunks,)),
         ],
-        compiler_params=pltpu.CompilerParams(vmem_limit_bytes=44 << 20),
-        cost_estimate=pl.CostEstimate(flops=14 * rows * LANES, bytes_accessed=8 * rows * LANES, transcendentals=0),
+        compiler_params=pltpu.CompilerParams(vmem_limit_bytes=52 << 20),
+        cost_estimate=pl.CostEstimate(flops=14 * size, bytes_accessed=8 * size, transcendentals=0),
         name="step_tracers",
-    )(meta, table, need, diffusion, view.reshape(rows, LANES), ga, gb, ha, hb)
+    )(meta, table, need, diffusion, view.reshape(slots, IMAGE, LANES), ga, gb, ha, hb)
     return out.reshape(view.shape)
 
 
@@ -815,7 +830,7 @@
 
 def strip_tables(halo_source, code, at_x, at_y, count_x, count_y):
     slots = halo_source.shape[0]
-    source = halo_source
+    source = halo_source.reshape(-1)
     missing = source >= 4 * slots * count_x * count_y
     source = jnp.where(missing, 0, source)
     owner = source // (4 * slots)
@@ -823,48 +838,44 @@
     same_x = owner // count_y == at_x
     owner_y = owner % count_y
     up = owner_y == (at_y + 1) % count_y
-    down = owner_y == (at_y + count_y - 1) % count_y
     here = owner_y == at_y
-    side = lax.broadcasted_iota(jnp.int32, (slots, 4), 1)
-    index = lax.broadcasted_iota(jnp.int32, (slots, 4), 0) * 4 + side
+    index = jnp.arange(4 * slots, dtype=jnp.int32)
+    side = index % 4
     kind = jnp.where(side >= 2, 1, 0)
     linked = ~missing & same_x & ~here
     group = jnp.where(linked, jnp.where(up, kind, 2 + kind), -1)
 
     def rank(key):
-        flat_key, flat_group = key.reshape(-1), group.reshape(-1)
-        before = (flat_key[None, :] < flat_key[:, None]) & (flat_group[None, :] == flat_group[:, None])
-        return jnp.sum(before.astype(jnp.int32), axis=1).reshape(slots, 4)
+        before = (key[None, :] < key[:, None]) & (group[None, :] == group[:, None])
+        return jnp.sum(before.astype(jnp.int32), axis=1)
 
     take = rank(index)
     give = rank(source)
-    entries = []
-    for way in range(2):
-        entries += [(way * 2, k) for k in range(CAP_WE)] + [(way * 2 + 1, k) for k in range(CAP_NS)]
-    want = jnp.asarray([g * 1024 + k for g, k in entries], jnp.int32)
-    has = jnp.where(group >= 0, group * 1024 + give, -1).reshape(-1)
-    hit = want[:, None] == has[None, :]
-    send = jnp.sum(jnp.where(hit, index.reshape(-1)[None, :] + 1, 0), axis=1) - 1
+    entry = jnp.arange(2 * (CAP_WE + CAP_NS), dtype=jnp.int32)
+    rest = entry % (CAP_WE + CAP_NS)
+    of_kind = jnp.where(rest >= CAP_WE, 1, 0)
+    want = (2 * (entry // (CAP_WE + CAP_NS)) + of_kind) * 1024 + rest - CAP_WE * of_kind
+    has = jnp.where(group >= 0, group * 1024 + give, -1)
+    send = jnp.sum(jnp.where(want[:, None] == has[None, :], index[None, :] + 1, 0), axis=1) - 1
     over = jnp.any(linked & (take >= jnp.where(kind == 1, CAP_NS, CAP_WE)))
-    row = (code // REG_X)[:, None]
+    row = jnp.broadcast_to((code // REG_X)[:, None], (slots, 4)).reshape(-1)
     local = same_x & here
     north = kind == 1
-    lane = jnp.where(same_x, RELAY + take, jnp.where(here, row, row % REG_Y + jnp.where(side == 0, 0, REG_Y)))
-    beside = jnp.where(side == 0, 0, HALF * ROWS)
-    along = jnp.where(up, BOX_HIGH, BOX_LOW)
-    box_we = jnp.where(same_x | ~here, along, beside)
-    by_we = jnp.where(side == 0, -1, BLOCK) - lane
-    box_ns = along + HALF * ROWS + 2 * jnp.minimum(take // 4, TILE // 2 - 1) - jnp.where(side == 3, TILE - 2, 0)
-    by_ns = jnp.where(side == 3, LANES - BLOCK, 0) - BLOCK * (take % 4)
-    remote = ~missing & ~local
-    image = jnp.where(missing, slots, jnp.where(local, local_slot, slots + 1 + 2 * kind))
-    at = jnp.where(remote, jnp.where(north, box_ns, box_we), 0)
-    by = jnp.where(remote, jnp.where(north, by_ns, by_we), 0) % LANES
-    fields = [image, remote.astype(jnp.int32), at, by, missing.astype(jnp.int32)]
-    table = jnp.stack(fields, axis=-1).reshape(-1)
-    last = jnp.where(local & ~missing, local_slot, 0)
-    last = jnp.maximum(jnp.max(last, axis=1), jnp.arange(slots))
-    need = jnp.max(last.reshape(-1, STEP_SLOTS), axis=1) // STEP_SLOTS
+    lane = jnp.where(same_x, RELAY + take, row % REG_Y + jnp.where(side == 0, 0, REG_Y))
+    box = jnp.where(up, BOX_HIGH, BOX_LOW)
+    by = (jnp.where(side == 0, -1, BLOCK) - lane) % LANES
+    unpacked = slots + 19 + index // 4 % STEP_SLOTS
+    image_we = jnp.where(local, local_slot, jnp.where(here, slots + 9 + row, unpacked))
+    take = jnp.minimum(take, CAP_NS - 1)
+    turns = jnp.where(side == 2, -take, 3 - take) % 4
+    image_ns = jnp.where(local, local_slot, slots + 1 + jnp.where(up, 4, 0) + turns)
+    row_ns = jnp.where(local | missing, jnp.where(side == 2, ROWS - 2, 0), 2 * (take // 4))
+    row_ns = row_ns - jnp.where(side == 3, TILE - 2, 0)
+    image = jnp.where(missing, slots, jnp.where(north, image_ns, image_we))
+    unpack = jnp.where(missing | here | north, 0, 1)
+    table = jnp.stack([image, unpack, jnp.where(north, row_ns, box), by, jnp.where(missing, 1, 0)])
+    last = jnp.where(local & ~missing, local_slot, 0).reshape(-1, 4 * STEP_SLOTS)
+    need = jnp.maximum(jnp.max(last, axis=1) // STEP_SLOTS, jnp.arange(slots // STEP_SLOTS))
     return table, need, send, over.astype(jnp.int32)
 
 
@@ -876,32 +887,32 @@
     grid_rows = REG_Y * count_y
     own_row = (clinic_blocks // grid_columns - REG_Y * at_y) % grid_rows
     code = own_row * REG_X + clinic_blocks % grid_columns % REG_X
-    came = shifted(code, "gy", 1)
     zero = jnp.zeros((), jnp.int32)
     meta = jnp.stack([at_x, at_y, zero + count_y, zero]).astype(jnp.int32)
-    spot = jnp.arange(2 * REGION, dtype=jnp.int32)[:, None]
-    index = jnp.arange(slots, dtype=jnp.int32)[None, :]
-    places = jnp.sum(jnp.where(code[None, :] == spot, index + 1, 0), axis=1) - 1
 
     view = seen_by_rows(tracers)
-    s, q, a, b, far = depth_sums(view, meta, places, layer_weight, diffusion, surface_term)
+    s, q, a, b, far, places = depth_sums(view, meta, code, layer_weight, diffusion, surface_term)
     ra, rb = swap(a, b, "gy", count_y)
     rfar = shifted(far, "gy", 2)
 
-    table, need, send, over = strip_tables(halo_source, code, at_x, at_y, count_x, count_y)
-    ga, gb = swap(*column_strips(meta, places, view, far), "gx", count_x)
-
-    moved = (came[None, :] - REGION == spot) & (came[None, :] >= REGION)
-    both = places + jnp.sum(jnp.where(moved, index + 1 + MOVED, 0), axis=1)
+    source, places = lax.optimization_barrier((halo_source, places))
+    table, need, send, over = strip_tables(source, code, at_x, at_y, count_x, count_y)
+    ga, gb = swap(*column_strips(meta, places, view, rfar), "gx", count_x)
+
+    moved = jnp.where(at_y % 2 == 0, rb[IDS, :MOVED], ra[IDS, :MOVED]).astype(jnp.int32)
+    spot = jnp.arange(2 * REGION, dtype=jnp.int32)[:, None]
+    index = jnp.arange(MOVED, dtype=jnp.int32)[None, :]
+    both = places + jnp.sum(jnp.where(moved[None, :] == spot, index + 1 + slots, 0), axis=1)
     fields, ca, cb = region_fields(meta, both, s, q, ra, rb, rfar, surface_term)
     ca, cb = swap(ca, cb, "gx", count_x)
     ha, hb = swap(*link_strips(meta, send, view, ga, gb), "gy", count_y)
 
     meta_over = jnp.stack([at_x, at_y, zero + count_y, over]).astype(jnp.int32)
-    sums, blocks, back = solve_basis(meta_over, came, fields, ca, cb, count_x * count_y)
+    sums, blocks, back = solve_basis(meta_over, moved, fields, ca, cb, count_x * count_y)
     back = shifted(back, "gy", -1)
     sums = lax.all_to_all(sums[:, None], ("gx", "gy"), 0, 0, tiled=True)
     updated = step_tracers(meta, table, need, diffusion, view, ga, gb, ha, hb)
+    sums, updated = lax.optimization_barrier((sums, updated))
     updated = lax.cond(
         jnp.max(sums[:, 0, 6]) > 0.0,
         lambda fast: general_step(tracers, diffusion, halo_source),

time: 90.6 us -> 72.2 us (0.80)
  Pallas kernels: 54.1 us -> 40.7 us
  starting transfers between devices: 23.1 us -> 19.6 us
  waiting for transfers between devices: 1.54 us -> 2.99 us
  local copies, waits for them, and re-layouts: 4.24 us -> 3.04 us
  other arithmetic: 4.33 us -> 3.15 us
    pallas_call x4, Pallas kernels: 46.8 us -> 33.4 us  [the longest x1 19.6 us: step_tracers(): pl.pallas_call(tracer_kernel, in_specs=[SMEM] * 4 + [HBM] + [VMEM] * 4, o...]
    ppermute x4, starting transfers between devices: 3.41 us -> 1.21 us  [swap(): lax.ppermute(to_next, axis, first)]
    ppermute x4, waiting for transfers between devices: 1.52 us -> 2.97 us  [swap(): lax.ppermute(to_next, axis, first)]
    ppermute x3 -> x2, starting transfers between devices: 9.21 us -> 7.84 us  [shifted(): lax.ppermute(x, axis, [(i, (i + by) % length) for i in range(length)])]
    unnamed x15 -> x14, local copies, waits for them, and re-layouts: 2.82 us -> 2.06 us
  transfers between devices with their start and end apart: 12 -> 11, of which waited for: 1 -> 1; matrix products, arithmetic and copies ran while one was open for 6% -> 5% of each run, Pallas kernels for 49% -> 46%
where the time goes in v3:
time: 72.2 us; the launch traced here: 71.9 us
  Pallas kernels  40.7 us (56%)
  starting transfers between devices  19.6 us (27%)
  other arithmetic  3.15 us (4%)
  local copies, waits for them, and re-layouts  3.04 us (4%)
  waiting for transfers between devices  2.99 us (4%)
  between operations  2.17 us (3%)
    pallas_call x1, Pallas kernels, step_tracers(): pl.pallas_call(tracer_kernel, in_specs=[SMEM] * 4 + [HBM] + [VMEM] * 4, o...  19.6 us
    ppermute x4, starting transfers between devices, swap(): lax.ppermute(to_last, axis, second)  8.03 us
    ppermute x2, starting transfers between devices, shifted(): lax.ppermute(x, axis, [(i, (i + by) % length) for i in range(length)])  7.84 us
    pallas_call x1, Pallas kernels, depth_sums(): pl.pallas_call(sums_kernel, in_specs=[SMEM] * 4 + [HBM, HBM], out_specs=[...  5.84 us
    pallas_call x1, Pallas kernels, link_strips(): pl.pallas_call(links_kernel, in_specs=[SMEM, SMEM, HBM, VMEM, VMEM], out_...  4.13 us
    pallas_call x1, Pallas kernels, column_strips(): pl.pallas_call(columns_kernel, in_specs=[SMEM, SMEM, HBM, ANY], out_specs...  3.84 us
    pallas_call x1, Pallas kernels, solve_basis(): pl.pallas_call(basis_kernel, in_specs=[SMEM, SMEM, VMEM, VMEM, VMEM], out...  3.72 us
    ppermute x4, waiting for transfers between devices, swap(): lax.ppermute(to_next, axis, first)  2.97 us
  transfers between devices with their start and end apart: 11, of which 1 were waited for; matrix products, arithmetic and copies ran while one was open for 5% of the time, Pallas kernels for 46%

profile of v3, /device:TPU:0, one launch (start us, length us, event | category | flops | bytes accessed | tf_op | source)
XLA Modules:
  0.0 71.9 jit_solution(11167502652814601189)
XLA Ops:
  0.6 0.0 copy-start.7
  0.6 0.7 broadcast_remainder_fusion
  1.4 0.0 copy-start.2
  1.4 0.1 pad_add_fusion
  1.4 0.0 copy-start
  1.4 1.0 %copy-done = f32[160,448]{1,0:T(8,128)S(1)} copy-done((f32[160,448]{1,0:T(8,128)S(1)}, f32[160,448]{1,0:T(8,128)}, u32[]{:S(2)}) %copy-start) | copy-done | bytes 286744
  2.4 0.0 copy-start.4
  2.4 0.7 copy-done.4
  3.1 0.0 copy-start.1
  3.1 5.8 %depth_sums.1 = (f32[504,128]{1,0:T(8,128)S(1)}, f32[504,128]{1,0:T(8,128)S(1)}, f32[440,128]{1,0:T(8,128)S(1)}, f32[440,128]{1,0:T(8,128)S(1)}, f32[48,128]{1,0:T(8,128)S(1)}, /*index=5*/s32[140]{0:T(256)S(1)}) custom-call(s32[4]{0:T(128)S(1)} %get-tuple-element.86.meta, s32[63]{0:T(128)S(1)} %get-tuple-element.85.code, f32[2,20]{1,0:T(2,128)S(1)} %copy-done.4, ...), custom_call_target="tpu_custom_call" | custom-call | tf_op jit(solution)/shard_map/depth_sums/pallas_call | solution.py:181
  8.9 3.1 %collective-permute-start.6 = (f32[48,128]{1,0:T(8,128)S(1)}, f32[48,128]{1,0:T(8,128)S(1)}, u32[]{:S(2)}, u32[]{:S(2)}) collective-permute-start(f32[48,128]{1,0:T(8,128)S(1)} %get-tuple-element.44), channel_id=1, source_target_pairs={{0,2},{1,3},{2,4},{3,5},{4,6},{5,7},{6,0},{7,1},{8,10},{9,11},{10,... | collective-permute-start | bytes 73736 | tf_op jit(solution)/shard_map/ppermute | solution.py:73
  12.0 3.2 %collective-permute-start.4 = (f32[440,128]{1,0:T(8,128)S(1)}, f32[440,128]{1,0:T(8,128)S(1)}, u32[]{:S(2)}, u32[]{:S(2)}) collective-permute-start(f32[440,128]{1,0:T(8,128)S(1)} %get-tuple-element.39), channel_id=1, source_target_pairs={{0,7},{1,2},{2,1},{3,4},{4,3},{5,6},{6,5},{7,0},{8,15},{9,10},{10,... | collective-permute-start | bytes 675848 | tf_op jit(solution)/shard_map/ppermute | solution.py:58
  15.2 0.0 copy-done.2
  15.2 0.0 collective-permute-start.5
  15.2 0.0 copy-done.7
  15.2 0.1 copy.139
  15.3 0.1 reshape.1063
  15.4 0.1 reshape.1064
  15.6 0.3 convert_reduce_fusion
  15.8 0.1 reduce_sum.39
  16.0 0.2 select_reduce_fusion
  16.2 0.1 broadcast_in_dim.144
  16.2 0.1 rem.522
  16.4 0.1 broadcast_in_dim.138
  16.4 0.1 add.593
  16.6 0.1 copy.140
  16.6 0.7 %and_reduce_fusion = pred[]{:T(512)} fusion(s32[63,4]{0,1:T(4,128)S(1)} %copy.140, s32[63,4]{0,1:T(4,128)S(1)} %copy-done.7, s32[]{:T(128)} %axis_index.42, s32[]{:T(128)} %axis_index.45), kind=kLoop, calls=%fused_computation.148 | loop fusion | flops 13859 | bytes 2025 | tf_op jit(solution)/shard_map/reduce_or | solution.py:860
  18.1 0.1 pad_add_fusion.1.meta
  18.2 0.0 copy-start.8
  18.2 0.0 collective-permute-done.6.far_ref.after_ref
  18.2 3.8 %column_strips.1 = (f32[160,128]{1,0:T(8,128)S(1)}, f32[160,128]{1,0:T(8,128)S(1)}) custom-call(s32[4]{0:T(128)S(1)} %get-tuple-element.86.meta, s32[140]{0:T(256)S(1)} %get-tuple-element.41.inv, f32[63,320,128]{2,1,0:T(8,128)} %bitcast.85, f32[48,128]{1,0:T(8,128)S(1)} %collective-permute-done.6.far_ref.after_ref), custom_call_target="tpu_custom_call" | custom-call | flops 1 | bytes 1 | tf_op jit(solution)/shard_map/column_strips/pallas_call | solution.py:532
  22.0 0.6 collective-permute-start.10
  22.6 1.1 %collective-permute-start.9 = (f32[160,128]{1,0:T(8,128)S(1)}, f32[160,128]{1,0:T(8,128)S(1)}, u32[]{:S(2)}, u32[]{:S(2)}) collective-permute-start(f32[160,128]{1,0:T(8,128)S(1)} %get-tuple-element.49), channel_id=1, source_target_pairs={{0,8},{8,0},{16,24},{24,16},{1,9},{9,1},{17,25},{25,17},{2,10},{10... | collective-permute-start | bytes 245768 | tf_op jit(solution)/shard_map/ppermute | solution.py:58
  23.7 0.0 collective-permute-done.4.b_ref
  23.7 3.0 %collective-permute-done.5.a_ref = f32[440,128]{1,0:T(8,128)S(1)} collective-permute-done((f32[440,128]{1,0:T(8,128)S(1)}, f32[440,128]{1,0:T(8,128)S(1)}, u32[]{:S(2)}, u32[]{:S(2)}) %collective-permute-start.5) | collective-permute-done | bytes 225312 | tf_op jit(solution)/shard_map/ppermute | solution.py:58
  26.7 0.1 select_reduce_fusion.1
  26.8 0.0 copy-done.1
  26.8 1.6 %region_fields.1 = (f32[4,4,176,128]{3,2,1,0:T(8,128)S(1)}, f32[24,128]{1,0:T(8,128)S(1)}, f32[24,128]{1,0:T(8,128)S(1)}) custom-call(s32[4]{0:T(128)S(1)} %get-tuple-element.86.meta, s32[140]{0:T(256)S(1)} %add.584.inv, f32[504,128]{1,0:T(8,128)S(1)} %get-tuple-element.42.s_ref, f32[504,128]{1,0:T(8,128)S(1)} %get-tuple-element.43.q_ref, ...), custom_call_target="tpu_custom_call" | custom-call | tf_op jit(solution)/shard_map/region_fields/pallas_call | solution.py:299
  28.4 0.1 collective-permute-start.7
  28.5 1.6 %collective-permute-start.8 = (f32[24,128]{1,0:T(8,128)S(1)}, f32[24,128]{1,0:T(8,128)S(1)}, u32[]{:S(2)}, u32[]{:S(2)}) collective-permute-start(f32[24,128]{1,0:T(8,128)S(1)} %get-tuple-element.47), channel_id=1, source_target_pairs={{0,24},{8,16},{16,8},{24,0},{1,25},{9,17},{17,9},{25,1},{2,26},{10... | collective-permute-start | bytes 36872 | tf_op jit(solution)/shard_map/ppermute | solution.py:58
  30.2 0.1 reduce_max.26
  30.2 0.1 reduce_max.27
  30.4 0.0 collective-permute-done.10.gb_ref
  30.4 0.0 collective-permute-done.9.ga_ref
  30.4 4.1 %link_strips.1 = (f32[328,128]{1,0:T(8,128)S(1)}, f32[328,128]{1,0:T(8,128)S(1)}) custom-call(s32[4]{0:T(128)S(1)} %get-tuple-element.86.meta, s32[44]{0:T(128)S(1)} %broadcast_add_fusion.1.table, f32[63,20,16,128]{3,2,1,0:T(8,128)} %bitcast.86, f32[160,128]{1,0:T(8,128)S(1)} %collective-permute-done.9.ga_ref, f32[160,128]{1,0:T(8,128)S(1)} %collective-permute-done.10.gb_ref), custom_call_target="tpu_custom_call" | custom-call | tf_op jit(solution)/shard_map/link_strips/pallas_call | solution.py:625
  34.5 0.1 collective-permute-start.11
  34.6 2.6 %collective-permute-start.12 = (f32[328,128]{1,0:T(8,128)S(1)}, f32[328,128]{1,0:T(8,128)S(1)}, u32[]{:S(2)}, u32[]{:S(2)}) collective-permute-start(f32[328,128]{1,0:T(8,128)S(1)} %get-tuple-element.52), channel_id=1, source_target_pairs={{0,7},{1,2},{2,1},{3,4},{4,3},{5,6},{6,5},{7,0},{8,15},{9,10},{10,... | collective-permute-start | bytes 503816 | tf_op jit(solution)/shard_map/ppermute | solution.py:58
  37.2 0.0 collective-permute-done.7.ca_ref
  37.2 0.0 collective-permute-done.8.cb_ref
  37.2 3.7 %solve_basis.1 = (f32[32,128]{1,0:T(8,128)}, f32[1680,128]{1,0:T(8,128)S(1)}, f32[528,128]{1,0:T(8,128)}) custom-call(s32[4]{0:T(128)S(1)} %pad_add_fusion.1.meta, s32[22]{0:T(128)S(1)} %fusion.47.moved, f32[4,4,176,128]{3,2,1,0:T(8,128)S(1)} %get-tuple-element.45.f_ref, f32[24,128]{1,0:T(8,128)S(1)} %collective-permute-done.7.ca_ref, ...), custom_call_target="tpu_custom_call" | custom-call | tf_op jit(solution)/shard_map/solve_basis/pallas_call | solution.py:409
  41.0 2.5 %all-to-all-start = ((f32[32,1,128]{2,1,0:T(1,128)}), f32[32,1,128]{2,1,0:T(1,128)S(1)}, u32[]{:S(2)}, u32[]{:S(2)}) async-start(f32[32,1,128]{2,1,0:T(1,128)} %bitcast.29), calls=%async_computation | async-start | bytes 32768 | tf_op jit(solution)/shard_map/all_to_all | solution.py:913
  43.5 4.8 %collective-permute-start.13 = (f32[528,128]{1,0:T(8,128)}, f32[528,128]{1,0:T(8,128)}, u32[]{:S(2)}, u32[]{:S(2)}) collective-permute-start(f32[528,128]{1,0:T(8,128)} %get-tuple-element.55), channel_id=1, source_target_pairs={{0,7},{1,0},{2,1},{3,2},{4,3},{5,4},{6,5},{7,6},{8,15},{9,8},{10,9... | collective-permute-start | bytes 811016 | tf_op jit(solution)/shard_map/ppermute | solution.py:73
  48.3 0.0 collective-permute-done.11.ha_ref
  48.3 0.0 collective-permute-done.12.hb_ref
  48.3 0.0 copy-done.8
  48.3 19.6 %step_tracers.1 = f32[63,320,128]{2,1,0:T(8,128)} custom-call(s32[4]{0:T(128)S(1)} %get-tuple-element.86.meta, s32[5,252]{1,0:T(8,128)S(1)} %stack.37.table, s32[9]{0:T(128)S(1)} %iota_maximum_fusion.need, f32[20]{0:T(128)S(1)} %copy-done.8, f32[63,320,128]{2,1,0:T(8,128)} %bitcast.87, f32[160,128]{1,0:T(8,128)S(1)} %collective-permute-done.9.ga_ref, ...), custom_call_target="tpu_custom_call" | custom-call | flops 36126720 | bytes 20643840 | tf_op jit(solution)/shard_map/step_tracers/pallas_call | solution.py:764
  67.9 0.0 all-to-all-done
  67.9 0.7 slice_reduce_fusion
  69.3 0.0 copy-start.3
  69.3 0.3 conditional.1
  69.6 0.0 collective-permute-done.13.back_ref
  69.6 0.4 copy-done.3
  70.0 2.0 %slot_pressure.1 = (f32[63,1024]{1,0:T(8,128)}, f32[63,20,16,128]{3,2,1,0:T(8,128)}) custom-call(s32[63]{0:T(128)S(1)} %copy-done.3, f32[32,128]{1,0:T(8,128)S(1)} %bitcast.77, f32[1680,128]{1,0:T(8,128)S(1)} %get-tuple-element.54.blocks_ref, f32[528,128]{1,0:T(8,128)} %collective-permute-done.13.back_ref, ...), custom_call_target="tpu_custom_call", output_to_operand_aliasing={{1}: (4, {})} | custom-call | tf_op jit(solution)/shard_map/slot_pressure/pallas_call | solution.py:477
  (14 shorter events, 0.2 us)
Async XLA Ops:
  0.6 14.6 %copy-start.7 = (s32[63,4]{0,1:T(4,128)S(1)}, s32[63,4]{0,1:T(4,128)}, u32[]{:S(2)}) copy-start(s32[63,4]{0,1:T(4,128)} %param.13) | copy-start | bytes 3028
  1.4 13.8 %copy-start.2 = (s32[63]{0:T(128)}, s32[63]{0:T(128)S(1)}, u32[]{:S(2)}) copy-start(s32[63]{0:T(128)S(1)} %get-tuple-element.85.code) | copy-start | bytes 760
  1.4 1.0 %copy-start = (f32[160,448]{1,0:T(8,128)S(1)}, f32[160,448]{1,0:T(8,128)}, u32[]{:S(2)}) copy-start(f32[160,448]{1,0:T(8,128)} %surf_ref.3) | copy-start | bytes 860164
  2.4 0.7 copy-start.4
  3.1 23.7 %copy-start.1 = (f32[160,448]{1,0:T(8,128)S(1)}, f32[160,448]{1,0:T(8,128)}, u32[]{:S(2)}) copy-start(f32[160,448]{1,0:T(8,128)} %surf_ref.3) | copy-start | bytes 860164
  8.9 9.2 %collective-permute-start.6 = (f32[48,128]{1,0:T(8,128)S(1)}, f32[48,128]{1,0:T(8,128)S(1)}, u32[]{:S(2)}, u32[]{:S(2)}) collective-permute-start(f32[48,128]{1,0:T(8,128)S(1)} %get-tuple-element.44), channel_id=1, source_target_pairs={{0,2},{1,3},{2,4},{3,5},{4,6},{5,7},{6,0},{7,1},{8,10},{9,11},{10,... | collective-permute-start | bytes 73736 | tf_op jit(solution)/shard_map/ppermute | solution.py:73
  12.0 11.7 %collective-permute-start.4 = (f32[440,128]{1,0:T(8,128)S(1)}, f32[440,128]{1,0:T(8,128)S(1)}, u32[]{:S(2)}, u32[]{:S(2)}) collective-permute-start(f32[440,128]{1,0:T(8,128)S(1)} %get-tuple-element.39), channel_id=1, source_target_pairs={{0,7},{1,2},{2,1},{3,4},{4,3},{5,6},{6,5},{7,0},{8,15},{9,10},{10,... | collective-permute-start | bytes 675848 | tf_op jit(solution)/shard_map/ppermute | solution.py:58
  15.2 11.5 %collective-permute-start.5 = (f32[440,128]{1,0:T(8,128)S(1)}, f32[440,128]{1,0:T(8,128)S(1)}, u32[]{:S(2)}, u32[]{:S(2)}) collective-permute-start(f32[440,128]{1,0:T(8,128)S(1)} %get-tuple-element.40), channel_id=1, source_target_pairs={{0,1},{1,0},{2,3},{3,2},{4,5},{5,4},{6,7},{7,6},{8,9},{9,8},{10,11... | collective-permute-start | bytes 675848 | tf_op jit(solution)/shard_map/ppermute | solution.py:58
  18.2 30.2 %copy-start.8 = (f32[20]{0:T(128)S(1)}, f32[20]{0:T(128)}, u32[]{:S(2)}) copy-start(f32[20]{0:T(128)} %diffusion.3) | copy-start | bytes 244
  22.0 8.4 %collective-permute-start.10 = (f32[160,128]{1,0:T(8,128)S(1)}, f32[160,128]{1,0:T(8,128)S(1)}, u32[]{:S(2)}, u32[]{:S(2)}) collective-permute-start(f32[160,128]{1,0:T(8,128)S(1)} %get-tuple-element.50), channel_id=1, source_target_pairs={{0,24},{8,16},{16,8},{24,0},{1,25},{9,17},{17,9},{25,1},{2,26},{10... | collective-permute-start | bytes 245768 | tf_op jit(solution)/shard_map/ppermute | solution.py:58
  22.6 7.8 %collective-permute-start.9 = (f32[160,128]{1,0:T(8,128)S(1)}, f32[160,128]{1,0:T(8,128)S(1)}, u32[]{:S(2)}, u32[]{:S(2)}) collective-permute-start(f32[160,128]{1,0:T(8,128)S(1)} %get-tuple-element.49), channel_id=1, source_target_pairs={{0,8},{8,0},{16,24},{24,16},{1,9},{9,1},{17,25},{25,17},{2,10},{10... | collective-permute-start | bytes 245768 | tf_op jit(solution)/shard_map/ppermute | solution.py:58
  28.4 8.8 %collective-permute-start.7 = (f32[24,128]{1,0:T(8,128)S(1)}, f32[24,128]{1,0:T(8,128)S(1)}, u32[]{:S(2)}, u32[]{:S(2)}) collective-permute-start(f32[24,128]{1,0:T(8,128)S(1)} %get-tuple-element.46), channel_id=1, source_target_pairs={{0,8},{8,0},{16,24},{24,16},{1,9},{9,1},{17,25},{25,17},{2,10},{10... | collective-permute-start | bytes 36872 | tf_op jit(solution)/shard_map/ppermute | solution.py:58
  28.5 8.7 %collective-permute-start.8 = (f32[24,128]{1,0:T(8,128)S(1)}, f32[24,128]{1,0:T(8,128)S(1)}, u32[]{:S(2)}, u32[]{:S(2)}) collective-permute-start(f32[24,128]{1,0:T(8,128)S(1)} %get-tuple-element.47), channel_id=1, source_target_pairs={{0,24},{8,16},{16,8},{24,0},{1,25},{9,17},{17,9},{25,1},{2,26},{10... | collective-permute-start | bytes 36872 | tf_op jit(solution)/shard_map/ppermute | solution.py:58
  34.5 13.8 %collective-permute-start.11 = (f32[328,128]{1,0:T(8,128)S(1)}, f32[328,128]{1,0:T(8,128)S(1)}, u32[]{:S(2)}, u32[]{:S(2)}) collective-permute-start(f32[328,128]{1,0:T(8,128)S(1)} %get-tuple-element.51), channel_id=1, source_target_pairs={{0,1},{1,0},{2,3},{3,2},{4,5},{5,4},{6,7},{7,6},{8,9},{9,8},{10,11... | collective-permute-start | bytes 503816 | tf_op jit(solution)/shard_map/ppermute | solution.py:58
  34.6 13.7 %collective-permute-start.12 = (f32[328,128]{1,0:T(8,128)S(1)}, f32[328,128]{1,0:T(8,128)S(1)}, u32[]{:S(2)}, u32[]{:S(2)}) collective-permute-start(f32[328,128]{1,0:T(8,128)S(1)} %get-tuple-element.52), channel_id=1, source_target_pairs={{0,7},{1,2},{2,1},{3,4},{4,3},{5,6},{6,5},{7,0},{8,15},{9,10},{10,... | collective-permute-start | bytes 503816 | tf_op jit(solution)/shard_map/ppermute | solution.py:58
  41.0 27.0 %all-to-all-start = ((f32[32,1,128]{2,1,0:T(1,128)}), f32[32,1,128]{2,1,0:T(1,128)S(1)}, u32[]{:S(2)}, u32[]{:S(2)}) async-start(f32[32,1,128]{2,1,0:T(1,128)} %bitcast.29), calls=%async_computation | async-start | bytes 32768 | tf_op jit(solution)/shard_map/all_to_all | solution.py:913
  43.5 26.1 %collective-permute-start.13 = (f32[528,128]{1,0:T(8,128)}, f32[528,128]{1,0:T(8,128)}, u32[]{:S(2)}, u32[]{:S(2)}) collective-permute-start(f32[528,128]{1,0:T(8,128)} %get-tuple-element.55), channel_id=1, source_target_pairs={{0,7},{1,0},{2,1},{3,2},{4,3},{5,4},{6,5},{7,6},{8,15},{9,8},{10,9... | collective-permute-start | bytes 811016 | tf_op jit(solution)/shard_map/ppermute | solution.py:73
  69.3 0.7 copy-start.3

commit v4 on v3

--- a/solution.py
+++ b/solution.py
@@ -643,7 +643,7 @@
 BOX = BOX_HIGH + LINK_ROWS
 
 
-def tracer_kernel(meta, table, need, diffusion, t_ref, ga_ref, gb_ref, ha_ref, hb_ref, out_ref, own, up, down, box, sems, out_sems):
+def tracer_kernel(meta, table, need, diffusion, t_ref, ga_ref, gb_ref, ha_ref, hb_ref, out_ref, own, inner, across, beside, box, perm, sems, out_sems):
     slots = own.shape[0]
     chunks = slots // STEP_SLOTS
 
@@ -659,8 +659,17 @@
         fetch(c).start()
     even_x = meta[0] % 2 == 0
     even_y = meta[1] % 2 == 0
-    up[slots] = jnp.zeros(up.shape[1:], F32)
-    down[slots] = jnp.zeros(up.shape[1:], F32)
+    src = lax.broadcasted_iota(jnp.int32, perm.shape, 0) % LANES
+    dst = lax.broadcasted_iota(jnp.int32, perm.shape, 1)
+    to = dst % LANES
+    gap = jnp.abs(src - to)
+    linked = ((gap == 1) & (src // BLOCK == to // BLOCK)) | (gap == BLOCK)
+    crossed = gap == LANES - BLOCK
+    swapped = (gap == BLOCK - 1) & (src // BLOCK == to // BLOCK)
+    hit = ((dst < LANES) & linked) | ((dst >= LANES) & (dst < 2 * LANES) & crossed) | ((dst >= 2 * LANES) & swapped)
+    perm[...] = jnp.where(hit, 1.0, 0.0).astype(jnp.bfloat16)
+    across[slots] = jnp.zeros(across.shape[1:], F32)
+    beside[slots] = jnp.zeros(beside.shape[1:], F32)
     for first, second, size, low, high in (
         (ga_ref, gb_ref, HALF * ROWS, 0, HALF * ROWS),
         (ha_ref, hb_ref, LINK_ROWS, BOX_LOW, BOX_HIGH),
@@ -668,36 +677,42 @@
         even = even_x if low == 0 else even_y
         box[pl.ds(low, size), :] = jnp.where(even, second[...], first[...])
         box[pl.ds(high, size), :] = jnp.where(even, first[...], second[...])
+
+    cells = (ROWS, LANES)
+    lane = lane_id(cells)
+    column = lane % BLOCK
+    row = lax.broadcasted_iota(jnp.int32, cells, 0)
+    row8, lane8 = row[:TILE], lane[:TILE]
+    outer = (lane8 < BLOCK) | (lane8 >= LANES - BLOCK)
     for way, low in enumerate((BOX_LOW, BOX_HIGH)):
         for level in range(LEVELS):
             x = box[pl.ds(low + HALF * ROWS + level * TILE, TILE), :]
             for d in range(4):
-                y = turn(x, BLOCK * d, 1)
-                up[slots + 1 + 4 * way + d, pl.ds(TILE + level * ROWS, TILE), :] = y
-                down[slots + 1 + 4 * way + d, pl.ds(TILE + level * ROWS, TILE), :] = y
+                y = jnp.where(outer, turn(x, BLOCK * d, 1), 0.0)
+                across[slots + 1 + 4 * way + d, pl.ds(TILE + level * ROWS, TILE), :] = y
     for level in range(LEVELS):
         part = level // HALF
         w = box[pl.ds((level % HALF) * ROWS, ROWS), :]
         e = box[pl.ds((HALF + level % HALF) * ROWS, ROWS), :]
         for k in range(2 * REG_Y):
-            down[slots + 9 + k, pl.ds(TILE + level * ROWS, ROWS), :] = turn(w, -1 - k - 16 * part, 1)
-            up[slots + 9 + k, pl.ds(TILE + level * ROWS, ROWS), :] = turn(e, BLOCK - k - 16 * part, 1)
+            y = jnp.where(column == BLOCK - 1, turn(e, BLOCK - 1 - k - 16 * part, 1), 0.0)
+            y = jnp.where(column == 0, turn(w, -k - 16 * part, 1), y)
+            beside[slots + 1 + k, pl.ds(level * ROWS, ROWS), :] = y
 
     def arrive(c, carry):
         fetch(c).wait()
         for n in range(STEP_SLOTS):
             s = c * STEP_SLOTS + n
-            for level in range(LEVELS):
-                x = own[s, pl.ds(level * ROWS, ROWS), :]
-                up[s, pl.ds(TILE + level * ROWS, ROWS), :] = pltpu.roll(x, BLOCK, 1)
-                down[s, pl.ds(TILE + level * ROWS, ROWS), :] = pltpu.roll(x, LANES - BLOCK, 1)
+            x = own[s]
+            high = x.astype(jnp.bfloat16)
+            low = (x - high.astype(F32)).astype(jnp.bfloat16)
+            pair = jnp.concatenate([high, low], axis=1)
+            moved = jnp.dot(pair, perm[...], preferred_element_type=F32)
+            inner[s] = moved[:, :LANES]
+            across[s, pl.ds(TILE, IMAGE), :] = moved[:, LANES : 2 * LANES]
+            beside[s] = moved[:, 2 * LANES :]
         return carry
 
-    cells = (ROWS, LANES)
-    lane = lane_id(cells)
-    column = lane % BLOCK
-    row = lax.broadcasted_iota(jnp.int32, cells, 0)
-    row8 = row[:TILE]
     edge = (
         jnp.where(column == 0, 1.0, 0.0),
         jnp.where(column == BLOCK - 1, 1.0, 0.0),
@@ -706,7 +721,7 @@
     )
 
     def unpack(n, s):
-        for t, dest in ((0, down), (1, up)):
+        for t in range(2):
             at = s * 4 + t
 
             @pl.when(table[1, at] == 1)
@@ -716,7 +731,8 @@
                     part = level // HALF
                     x = box[pl.ds(first + (level % HALF) * ROWS, ROWS), :]
                     x = pltpu.roll(x, (by + LANES - 16 * part) % LANES, 1)
-                    dest[slots + 19 + n, pl.ds(TILE + level * ROWS, ROWS), :] = x
+                    x = jnp.where(column == t * (BLOCK - 1), x, 0.0)
+                    beside[slots + 11 + 2 * n + t, pl.ds(level * ROWS, ROWS), :] = x
 
     def step(n, s):
         count = jnp.full(cells, 4.0, F32)
@@ -725,21 +741,20 @@
         west, east, south, north = [table[0, s * 4 + t] for t in range(4)]
         south_at, north_at = TILE + table[2, s * 4 + 2], TILE + table[2, s * 4 + 3]
         for level in range(LEVELS):
-            at = level * ROWS
-            x = own[s, pl.ds(at, ROWS), :]
-            under = up[s, pl.ds(TILE + at - 2, ROWS), :]
-            over = down[s, pl.ds(TILE + at + 2, ROWS), :]
-            low = up[south, pl.ds(south_at + at, TILE), :]
-            high = down[north, pl.ds(north_at + at, TILE), :]
-            under = jnp.concatenate([jnp.where(row8 < 2, low, under[:TILE]), under[TILE:]], axis=0)
-            over = jnp.concatenate([over[:TILE], jnp.where(row8 >= TILE - 2, high, over[TILE:])], axis=0)
-            total = jnp.where(lane < BLOCK, under, up[s, pl.ds(TILE + at, ROWS), :])
-            total = total + jnp.where(lane >= LANES - BLOCK, over, down[s, pl.ds(TILE + at, ROWS), :])
-            w = down[west, pl.ds(TILE + at, ROWS), :]
-            e = up[east, pl.ds(TILE + at, ROWS), :]
-            total = total + pltpu.roll(jnp.where(column == BLOCK - 1, w, x), 1, 1)
-            total = total + pltpu.roll(jnp.where(column == 0, e, x), LANES - 1, 1)
-            own[s, pl.ds(at, ROWS), :] = x + diffusion[level] * (total - count * x)
+            for h in range(2):
+                at = level * ROWS + h * TILE
+                x = own[s, pl.ds(at, TILE), :]
+                under = across[s, pl.ds(TILE + at - 2, TILE), :]
+                over = across[s, pl.ds(TILE + at + 2, TILE), :]
+                if h == 0:
+                    under = jnp.where(row8 < 2, across[south, pl.ds(south_at + level * ROWS, TILE), :], under)
+                else:
+                    over = jnp.where(row8 >= TILE - 2, across[north, pl.ds(north_at + level * ROWS, TILE), :], over)
+                total = inner[s, pl.ds(at, TILE), :] + jnp.where(lane8 < LANES // 2, under, over)
+                w, e = beside[west, pl.ds(at, TILE), :], beside[east, pl.ds(at, TILE), :]
+                total = total + jnp.where(lane8 % BLOCK == 0, w, jnp.where(lane8 % BLOCK == BLOCK - 1, e, 0.0))
+                part = count[h * TILE : (h + 1) * TILE]
+                own[s, pl.ds(at, TILE), :] = x + diffusion[level] * (total - part * x)
 
     def work(c, seen):
         upto = jnp.maximum(seen, need[c] + 1)
@@ -760,7 +775,6 @@
     slots = view.shape[0]
     chunks = slots // STEP_SLOTS
     size = slots * IMAGE * LANES
-    images = slots + 19 + STEP_SLOTS
     out = pl.pallas_call(
         tracer_kernel,
         in_specs=[SMEM] * 4 + [HBM] + [VMEM] * 4,
@@ -768,9 +782,11 @@
         out_shape=jax.ShapeDtypeStruct((slots, IMAGE, LANES), F32),
         scratch_shapes=[
             pltpu.VMEM((slots, IMAGE, LANES), F32),
-            pltpu.VMEM((images, IMAGE + 2 * TILE, LANES), F32),
-            pltpu.VMEM((images, IMAGE + 2 * TILE, LANES), F32),
+            pltpu.VMEM((slots, IMAGE, LANES), F32),
+            pltpu.VMEM((slots + 9, IMAGE + 2 * TILE, LANES), F32),
+            pltpu.VMEM((slots + 11 + 2 * STEP_SLOTS, IMAGE, LANES), F32),
             pltpu.VMEM((BOX, LANES), F32),
+            pltpu.VMEM((2 * LANES, 3 * LANES), jnp.bfloat16),
             pltpu.SemaphoreType.DMA((chunks,)),
             pltpu.SemaphoreType.DMA((chunks,)),
         ],
@@ -863,9 +879,9 @@
     north = kind == 1
     lane = jnp.where(same_x, RELAY + take, row % REG_Y + jnp.where(side == 0, 0, REG_Y))
     box = jnp.where(up, BOX_HIGH, BOX_LOW)
-    by = (jnp.where(side == 0, -1, BLOCK) - lane) % LANES
-    unpacked = slots + 19 + index // 4 % STEP_SLOTS
-    image_we = jnp.where(local, local_slot, jnp.where(here, slots + 9 + row, unpacked))
+    by = (jnp.where(side == 0, 0, BLOCK - 1) - lane) % LANES
+    unpacked = slots + 11 + 2 * (index // 4 % STEP_SLOTS) + side
+    image_we = jnp.where(local, local_slot, jnp.where(here, slots + 1 + row, unpacked))
     take = jnp.minimum(take, CAP_NS - 1)
     turns = jnp.where(side == 2, -take, 3 - take) % 4
     image_ns = jnp.where(local, local_slot, slots + 1 + jnp.where(up, 4, 0) + turns)

time: 72.2 us -> 69.8 us (0.967)
  Pallas kernels: 40.7 us -> 38 us
    pallas_call x1, Pallas kernels: 19.6 us -> 17.2 us  [step_tracers(): pl.pallas_call(tracer_kernel, in_specs=[SMEM] * 4 + [HBM] + [VMEM] * 4, o...]
  transfers between devices with their start and end apart: 11 -> 11, of which waited for: 1 -> 1; matrix products, arithmetic and copies ran while one was open for 5% -> 5% of each run, Pallas kernels for 46% -> 43%
where the time goes in v4:
time: 69.8 us; the launch traced here: 69.4 us
  Pallas kernels  38 us (54%)
  starting transfers between devices  20 us (29%)
  other arithmetic  3.15 us (5%)
  local copies, waits for them, and re-layouts  3.04 us (4%)
  waiting for transfers between devices  2.89 us (4%)
  between operations  2.17 us (3%)
    pallas_call x1, Pallas kernels, step_tracers(): pl.pallas_call(tracer_kernel, in_specs=[SMEM] * 4 + [HBM] + [VMEM] * 4, o...  17.2 us
    ppermute x4, starting transfers between devices, swap(): lax.ppermute(to_last, axis, second)  8.05 us
    ppermute x2, starting transfers between devices, shifted(): lax.ppermute(x, axis, [(i, (i + by) % length) for i in range(length)])  7.84 us
    pallas_call x1, Pallas kernels, depth_sums(): pl.pallas_call(sums_kernel, in_specs=[SMEM] * 4 + [HBM, HBM], out_specs=[...  5.84 us
    pallas_call x1, Pallas kernels, link_strips(): pl.pallas_call(links_kernel, in_specs=[SMEM, SMEM, HBM, VMEM, VMEM], out_...  3.92 us
    pallas_call x1, Pallas kernels, column_strips(): pl.pallas_call(columns_kernel, in_specs=[SMEM, SMEM, HBM, ANY], out_specs...  3.73 us
    pallas_call x1, Pallas kernels, solve_basis(): pl.pallas_call(basis_kernel, in_specs=[SMEM, SMEM, VMEM, VMEM, VMEM], out...  3.72 us
    all_to_all x1, starting transfers between devices, on_device(): sums = lax.all_to_all(sums[:, None], ('gx', 'gy'), 0, 0, tiled=True)  2.92 us
  transfers between devices with their start and end apart: 11, of which 1 were waited for; matrix products, arithmetic and copies ran while one was open for 5% of the time, Pallas kernels for 43%

profile of v4, /device:TPU:0, one launch (start us, length us, event | category | flops | bytes accessed | tf_op | source)
XLA Modules:
  0.0 69.4 jit_solution(8162353790376456806)
XLA Ops:
  0.6 0.0 copy-start.7
  0.6 0.7 %broadcast_remainder_fusion = (s32[63]{0:T(128)S(1)}, s32[63]{0:T(128)S(1)}, s32[63]{0:T(128)S(1)}) fusion(s32[]{:T(128)S(6)} %mul.164, s32[63]{0:T(128)} %param.12), kind=kLoop, calls=%fused_computation.208 | loop fusion | flops 2268 | bytes 1012 | tf_op jit(solution)/shard_map/jit(remainder)/rem | solution.py:880
  1.4 0.0 copy-start.2
  1.4 0.1 pad_add_fusion
  1.4 0.0 copy-start
  1.4 1.0 %copy-done = f32[160,448]{1,0:T(8,128)S(1)} copy-done((f32[160,448]{1,0:T(8,128)S(1)}, f32[160,448]{1,0:T(8,128)}, u32[]{:S(2)}) %copy-start) | copy-done | bytes 286744
  2.4 0.0 copy-start.4
  2.4 0.7 copy-done.4
  3.1 0.0 copy-start.1
  3.1 5.8 %depth_sums.1 = (f32[504,128]{1,0:T(8,128)S(1)}, f32[504,128]{1,0:T(8,128)S(1)}, f32[440,128]{1,0:T(8,128)S(1)}, f32[440,128]{1,0:T(8,128)S(1)}, f32[48,128]{1,0:T(8,128)S(1)}, /*index=5*/s32[140]{0:T(256)S(1)}) custom-call(s32[4]{0:T(128)S(1)} %get-tuple-element.86.meta, s32[63]{0:T(128)S(1)} %get-tuple-element.85.code, f32[2,20]{1,0:T(2,128)S(1)} %copy-done.4, ...), custom_call_target="tpu_custom_call" | custom-call | tf_op jit(solution)/shard_map/depth_sums/pallas_call | solution.py:181
  8.9 3.1 %collective-permute-start.6 = (f32[48,128]{1,0:T(8,128)S(1)}, f32[48,128]{1,0:T(8,128)S(1)}, u32[]{:S(2)}, u32[]{:S(2)}) collective-permute-start(f32[48,128]{1,0:T(8,128)S(1)} %get-tuple-element.44), channel_id=1, source_target_pairs={{0,2},{1,3},{2,4},{3,5},{4,6},{5,7},{6,0},{7,1},{8,10},{9,11},{10,... | collective-permute-start | bytes 73736 | tf_op jit(solution)/shard_map/ppermute | solution.py:73
  12.0 3.2 %collective-permute-start.4 = (f32[440,128]{1,0:T(8,128)S(1)}, f32[440,128]{1,0:T(8,128)S(1)}, u32[]{:S(2)}, u32[]{:S(2)}) collective-permute-start(f32[440,128]{1,0:T(8,128)S(1)} %get-tuple-element.39), channel_id=1, source_target_pairs={{0,7},{1,2},{2,1},{3,4},{4,3},{5,6},{6,5},{7,0},{8,15},{9,10},{10,... | collective-permute-start | bytes 675848 | tf_op jit(solution)/shard_map/ppermute | solution.py:58
  15.2 0.0 copy-done.2
  15.2 0.0 collective-permute-start.5
  15.2 0.0 copy-done.7
  15.2 0.1 copy.139
  15.3 0.1 reshape.1069
  15.4 0.1 reshape.1070
  15.6 0.3 convert_reduce_fusion
  15.8 0.1 reduce_sum.39
  16.0 0.2 select_reduce_fusion
  16.2 0.1 broadcast_in_dim.144
  16.2 0.1 rem.522
  16.4 0.1 broadcast_in_dim.138
  16.4 0.1 add.597
  16.6 0.1 copy.140
  16.6 0.7 %and_reduce_fusion = pred[]{:T(512)} fusion(s32[63,4]{0,1:T(4,128)S(1)} %copy.140, s32[63,4]{0,1:T(4,128)S(1)} %copy-done.7, s32[]{:T(128)} %axis_index.42, s32[]{:T(128)} %axis_index.45), kind=kLoop, calls=%fused_computation.148 | loop fusion | flops 13859 | bytes 2025 | tf_op jit(solution)/shard_map/reduce_or | solution.py:876
  18.1 0.1 pad_add_fusion.1.meta
  18.2 0.0 copy-start.8
  18.2 0.0 collective-permute-done.6.far_ref.after_ref
  18.2 3.7 %column_strips.1 = (f32[160,128]{1,0:T(8,128)S(1)}, f32[160,128]{1,0:T(8,128)S(1)}) custom-call(s32[4]{0:T(128)S(1)} %get-tuple-element.86.meta, s32[140]{0:T(256)S(1)} %get-tuple-element.41.inv, f32[63,320,128]{2,1,0:T(8,128)} %bitcast.85, f32[48,128]{1,0:T(8,128)S(1)} %collective-permute-done.6.far_ref.after_ref), custom_call_target="tpu_custom_call" | custom-call | flops 1 | bytes 1 | tf_op jit(solution)/shard_map/column_strips/pallas_call | solution.py:532
  21.9 0.9 %collective-permute-start.10 = (f32[160,128]{1,0:T(8,128)S(1)}, f32[160,128]{1,0:T(8,128)S(1)}, u32[]{:S(2)}, u32[]{:S(2)}) collective-permute-start(f32[160,128]{1,0:T(8,128)S(1)} %get-tuple-element.50), channel_id=1, source_target_pairs={{0,24},{8,16},{16,8},{24,0},{1,25},{9,17},{17,9},{25,1},{2,26},{10... | collective-permute-start | bytes 245768 | tf_op jit(solution)/shard_map/ppermute | solution.py:58
  22.8 1.0 %collective-permute-start.9 = (f32[160,128]{1,0:T(8,128)S(1)}, f32[160,128]{1,0:T(8,128)S(1)}, u32[]{:S(2)}, u32[]{:S(2)}) collective-permute-start(f32[160,128]{1,0:T(8,128)S(1)} %get-tuple-element.49), channel_id=1, source_target_pairs={{0,8},{8,0},{16,24},{24,16},{1,9},{9,1},{17,25},{25,17},{2,10},{10... | collective-permute-start | bytes 245768 | tf_op jit(solution)/shard_map/ppermute | solution.py:58
  23.8 0.0 collective-permute-done.4.b_ref
  23.8 2.9 %collective-permute-done.5.a_ref = f32[440,128]{1,0:T(8,128)S(1)} collective-permute-done((f32[440,128]{1,0:T(8,128)S(1)}, f32[440,128]{1,0:T(8,128)S(1)}, u32[]{:S(2)}, u32[]{:S(2)}) %collective-permute-start.5) | collective-permute-done | bytes 225312 | tf_op jit(solution)/shard_map/ppermute | solution.py:58
  26.7 0.1 select_reduce_fusion.1
  26.8 0.0 copy-done.1
  26.8 1.6 %region_fields.1 = (f32[4,4,176,128]{3,2,1,0:T(8,128)S(1)}, f32[24,128]{1,0:T(8,128)S(1)}, f32[24,128]{1,0:T(8,128)S(1)}) custom-call(s32[4]{0:T(128)S(1)} %get-tuple-element.86.meta, s32[140]{0:T(256)S(1)} %add.590.inv, f32[504,128]{1,0:T(8,128)S(1)} %get-tuple-element.42.s_ref, f32[504,128]{1,0:T(8,128)S(1)} %get-tuple-element.43.q_ref, ...), custom_call_target="tpu_custom_call" | custom-call | tf_op jit(solution)/shard_map/region_fields/pallas_call | solution.py:299
  28.4 0.1 collective-permute-start.7
  28.5 1.6 %collective-permute-start.8 = (f32[24,128]{1,0:T(8,128)S(1)}, f32[24,128]{1,0:T(8,128)S(1)}, u32[]{:S(2)}, u32[]{:S(2)}) collective-permute-start(f32[24,128]{1,0:T(8,128)S(1)} %get-tuple-element.47), channel_id=1, source_target_pairs={{0,24},{8,16},{16,8},{24,0},{1,25},{9,17},{17,9},{25,1},{2,26},{10... | collective-permute-start | bytes 36872 | tf_op jit(solution)/shard_map/ppermute | solution.py:58
  30.2 0.1 reduce_max.26
  30.2 0.1 reduce_max.27
  30.4 0.0 collective-permute-done.10.gb_ref
  30.4 0.0 collective-permute-done.9.ga_ref
  30.4 3.9 %link_strips.1 = (f32[328,128]{1,0:T(8,128)S(1)}, f32[328,128]{1,0:T(8,128)S(1)}) custom-call(s32[4]{0:T(128)S(1)} %get-tuple-element.86.meta, s32[44]{0:T(128)S(1)} %broadcast_add_fusion.1.table, f32[63,20,16,128]{3,2,1,0:T(8,128)} %bitcast.86, f32[160,128]{1,0:T(8,128)S(1)} %collective-permute-done.9.ga_ref, f32[160,128]{1,0:T(8,128)S(1)} %collective-permute-done.10.gb_ref), custom_call_target="tpu_custom_call" | custom-call | tf_op jit(solution)/shard_map/link_strips/pallas_call | solution.py:625
  34.3 0.1 collective-permute-start.11
  34.4 2.4 %collective-permute-start.12 = (f32[328,128]{1,0:T(8,128)S(1)}, f32[328,128]{1,0:T(8,128)S(1)}, u32[]{:S(2)}, u32[]{:S(2)}) collective-permute-start(f32[328,128]{1,0:T(8,128)S(1)} %get-tuple-element.52), channel_id=1, source_target_pairs={{0,7},{1,2},{2,1},{3,4},{4,3},{5,6},{6,5},{7,0},{8,15},{9,10},{10,... | collective-permute-start | bytes 503816 | tf_op jit(solution)/shard_map/ppermute | solution.py:58
  36.8 0.0 collective-permute-done.7.ca_ref
  36.8 0.0 collective-permute-done.8.cb_ref
  36.8 3.7 %solve_basis.1 = (f32[32,128]{1,0:T(8,128)}, f32[1680,128]{1,0:T(8,128)S(1)}, f32[528,128]{1,0:T(8,128)}) custom-call(s32[4]{0:T(128)S(1)} %pad_add_fusion.1.meta, s32[22]{0:T(128)S(1)} %fusion.48.moved, f32[4,4,176,128]{3,2,1,0:T(8,128)S(1)} %get-tuple-element.45.f_ref, f32[24,128]{1,0:T(8,128)S(1)} %collective-permute-done.7.ca_ref, ...), custom_call_target="tpu_custom_call" | custom-call | tf_op jit(solution)/shard_map/solve_basis/pallas_call | solution.py:409
  40.5 2.9 %all-to-all-start = ((f32[32,1,128]{2,1,0:T(1,128)}), f32[32,1,128]{2,1,0:T(1,128)S(1)}, u32[]{:S(2)}, u32[]{:S(2)}) async-start(f32[32,1,128]{2,1,0:T(1,128)} %bitcast.29), calls=%async_computation | async-start | bytes 32768 | tf_op jit(solution)/shard_map/all_to_all | solution.py:929
  43.4 4.8 %collective-permute-start.13 = (f32[528,128]{1,0:T(8,128)}, f32[528,128]{1,0:T(8,128)}, u32[]{:S(2)}, u32[]{:S(2)}) collective-permute-start(f32[528,128]{1,0:T(8,128)} %get-tuple-element.55), channel_id=1, source_target_pairs={{0,7},{1,0},{2,1},{3,2},{4,3},{5,4},{6,5},{7,6},{8,15},{9,8},{10,9... | collective-permute-start | bytes 811016 | tf_op jit(solution)/shard_map/ppermute | solution.py:73
  48.2 0.0 collective-permute-done.11.ha_ref
  48.2 0.0 collective-permute-done.12.hb_ref
  48.2 0.0 copy-done.8
  48.3 17.2 %step_tracers.1 = f32[63,320,128]{2,1,0:T(8,128)} custom-call(s32[4]{0:T(128)S(1)} %get-tuple-element.86.meta, s32[5,252]{1,0:T(8,128)S(1)} %stack.37.table, s32[9]{0:T(128)S(1)} %iota_maximum_fusion.need, f32[20]{0:T(128)S(1)} %copy-done.8, f32[63,320,128]{2,1,0:T(8,128)} %bitcast.87, f32[160,128]{1,0:T(8,128)S(1)} %collective-permute-done.9.ga_ref, ...), custom_call_target="tpu_custom_call" | custom-call | flops 36126720 | bytes 20643840 | tf_op jit(solution)/shard_map/step_tracers/pallas_call | solution.py:778
  65.4 0.0 all-to-all-done
  65.4 0.7 %slice_reduce_fusion = f32[]{:T(128)} fusion(f32[32,1,128]{2,1,0:T(1,128)S(1)} %all-to-all-done), kind=kLoop, calls=%fused_computation.70 | loop fusion | flops 31 | bytes 132 | tf_op jit(solution)/shard_map/reduce_max | solution.py:933
  66.8 0.0 copy-start.3
  66.8 0.3 conditional.1
  67.1 0.0 collective-permute-done.13.back_ref
  67.1 0.4 copy-done.3
  67.5 2.0 %slot_pressure.1 = (f32[63,1024]{1,0:T(8,128)}, f32[63,20,16,128]{3,2,1,0:T(8,128)}) custom-call(s32[63]{0:T(128)S(1)} %copy-done.3, f32[32,128]{1,0:T(8,128)S(1)} %bitcast.77, f32[1680,128]{1,0:T(8,128)S(1)} %get-tuple-element.54.blocks_ref, f32[528,128]{1,0:T(8,128)} %collective-permute-done.13.back_ref, ...), custom_call_target="tpu_custom_call", output_to_operand_aliasing={{1}: (4, {})} | custom-call | tf_op jit(solution)/shard_map/slot_pressure/pallas_call | solution.py:477
  (14 shorter events, 0.2 us)
Async XLA Ops:
  0.6 14.6 %copy-start.7 = (s32[63,4]{0,1:T(4,128)S(1)}, s32[63,4]{0,1:T(4,128)}, u32[]{:S(2)}) copy-start(s32[63,4]{0,1:T(4,128)} %param.13) | copy-start | bytes 3028
  1.4 13.8 %copy-start.2 = (s32[63]{0:T(128)}, s32[63]{0:T(128)S(1)}, u32[]{:S(2)}) copy-start(s32[63]{0:T(128)S(1)} %get-tuple-element.85.code) | copy-start | bytes 760
  1.4 1.0 %copy-start = (f32[160,448]{1,0:T(8,128)S(1)}, f32[160,448]{1,0:T(8,128)}, u32[]{:S(2)}) copy-start(f32[160,448]{1,0:T(8,128)} %surf_ref.3) | copy-start | bytes 860164
  2.4 0.7 copy-start.4
  3.1 23.7 %copy-start.1 = (f32[160,448]{1,0:T(8,128)S(1)}, f32[160,448]{1,0:T(8,128)}, u32[]{:S(2)}) copy-start(f32[160,448]{1,0:T(8,128)} %surf_ref.3) | copy-start | bytes 860164
  8.9 9.2 %collective-permute-start.6 = (f32[48,128]{1,0:T(8,128)S(1)}, f32[48,128]{1,0:T(8,128)S(1)}, u32[]{:S(2)}, u32[]{:S(2)}) collective-permute-start(f32[48,128]{1,0:T(8,128)S(1)} %get-tuple-element.44), channel_id=1, source_target_pairs={{0,2},{1,3},{2,4},{3,5},{4,6},{5,7},{6,0},{7,1},{8,10},{9,11},{10,... | collective-permute-start | bytes 73736 | tf_op jit(solution)/shard_map/ppermute | solution.py:73
  12.0 11.8 %collective-permute-start.4 = (f32[440,128]{1,0:T(8,128)S(1)}, f32[440,128]{1,0:T(8,128)S(1)}, u32[]{:S(2)}, u32[]{:S(2)}) collective-permute-start(f32[440,128]{1,0:T(8,128)S(1)} %get-tuple-element.39), channel_id=1, source_target_pairs={{0,7},{1,2},{2,1},{3,4},{4,3},{5,6},{6,5},{7,0},{8,15},{9,10},{10,... | collective-permute-start | bytes 675848 | tf_op jit(solution)/shard_map/ppermute | solution.py:58
  15.2 11.5 %collective-permute-start.5 = (f32[440,128]{1,0:T(8,128)S(1)}, f32[440,128]{1,0:T(8,128)S(1)}, u32[]{:S(2)}, u32[]{:S(2)}) collective-permute-start(f32[440,128]{1,0:T(8,128)S(1)} %get-tuple-element.40), channel_id=1, source_target_pairs={{0,1},{1,0},{2,3},{3,2},{4,5},{5,4},{6,7},{7,6},{8,9},{9,8},{10,11... | collective-permute-start | bytes 675848 | tf_op jit(solution)/shard_map/ppermute | solution.py:58
  18.2 30.1 %copy-start.8 = (f32[20]{0:T(128)S(1)}, f32[20]{0:T(128)}, u32[]{:S(2)}) copy-start(f32[20]{0:T(128)} %diffusion.3) | copy-start | bytes 244
  21.9 8.5 %collective-permute-start.10 = (f32[160,128]{1,0:T(8,128)S(1)}, f32[160,128]{1,0:T(8,128)S(1)}, u32[]{:S(2)}, u32[]{:S(2)}) collective-permute-start(f32[160,128]{1,0:T(8,128)S(1)} %get-tuple-element.50), channel_id=1, source_target_pairs={{0,24},{8,16},{16,8},{24,0},{1,25},{9,17},{17,9},{25,1},{2,26},{10... | collective-permute-start | bytes 245768 | tf_op jit(solution)/shard_map/ppermute | solution.py:58
  22.8 7.6 %collective-permute-start.9 = (f32[160,128]{1,0:T(8,128)S(1)}, f32[160,128]{1,0:T(8,128)S(1)}, u32[]{:S(2)}, u32[]{:S(2)}) collective-permute-start(f32[160,128]{1,0:T(8,128)S(1)} %get-tuple-element.49), channel_id=1, source_target_pairs={{0,8},{8,0},{16,24},{24,16},{1,9},{9,1},{17,25},{25,17},{2,10},{10... | collective-permute-start | bytes 245768 | tf_op jit(solution)/shard_map/ppermute | solution.py:58
  28.4 8.4 %collective-permute-start.7 = (f32[24,128]{1,0:T(8,128)S(1)}, f32[24,128]{1,0:T(8,128)S(1)}, u32[]{:S(2)}, u32[]{:S(2)}) collective-permute-start(f32[24,128]{1,0:T(8,128)S(1)} %get-tuple-element.46), channel_id=1, source_target_pairs={{0,8},{8,0},{16,24},{24,16},{1,9},{9,1},{17,25},{25,17},{2,10},{10... | collective-permute-start | bytes 36872 | tf_op jit(solution)/shard_map/ppermute | solution.py:58
  28.5 8.3 %collective-permute-start.8 = (f32[24,128]{1,0:T(8,128)S(1)}, f32[24,128]{1,0:T(8,128)S(1)}, u32[]{:S(2)}, u32[]{:S(2)}) collective-permute-start(f32[24,128]{1,0:T(8,128)S(1)} %get-tuple-element.47), channel_id=1, source_target_pairs={{0,24},{8,16},{16,8},{24,0},{1,25},{9,17},{17,9},{25,1},{2,26},{10... | collective-permute-start | bytes 36872 | tf_op jit(solution)/shard_map/ppermute | solution.py:58
  34.3 13.9 %collective-permute-start.11 = (f32[328,128]{1,0:T(8,128)S(1)}, f32[328,128]{1,0:T(8,128)S(1)}, u32[]{:S(2)}, u32[]{:S(2)}) collective-permute-start(f32[328,128]{1,0:T(8,128)S(1)} %get-tuple-element.51), channel_id=1, source_target_pairs={{0,1},{1,0},{2,3},{3,2},{4,5},{5,4},{6,7},{7,6},{8,9},{9,8},{10,11... | collective-permute-start | bytes 503816 | tf_op jit(solution)/shard_map/ppermute | solution.py:58
  34.4 13.8 %collective-permute-start.12 = (f32[328,128]{1,0:T(8,128)S(1)}, f32[328,128]{1,0:T(8,128)S(1)}, u32[]{:S(2)}, u32[]{:S(2)}) collective-permute-start(f32[328,128]{1,0:T(8,128)S(1)} %get-tuple-element.52), channel_id=1, source_target_pairs={{0,7},{1,2},{2,1},{3,4},{4,3},{5,6},{6,5},{7,0},{8,15},{9,10},{10,... | collective-permute-start | bytes 503816 | tf_op jit(solution)/shard_map/ppermute | solution.py:58
  40.5 24.9 %all-to-all-start = ((f32[32,1,128]{2,1,0:T(1,128)}), f32[32,1,128]{2,1,0:T(1,128)S(1)}, u32[]{:S(2)}, u32[]{:S(2)}) async-start(f32[32,1,128]{2,1,0:T(1,128)} %bitcast.29), calls=%async_computation | async-start | bytes 32768 | tf_op jit(solution)/shard_map/all_to_all | solution.py:929
  43.4 23.7 %collective-permute-start.13 = (f32[528,128]{1,0:T(8,128)}, f32[528,128]{1,0:T(8,128)}, u32[]{:S(2)}, u32[]{:S(2)}) collective-permute-start(f32[528,128]{1,0:T(8,128)} %get-tuple-element.55), channel_id=1, source_target_pairs={{0,7},{1,0},{2,1},{3,2},{4,3},{5,4},{6,5},{7,6},{8,15},{9,8},{10,9... | collective-permute-start | bytes 811016 | tf_op jit(solution)/shard_map/ppermute | solution.py:73
  66.8 0.7 copy-start.3

commit v5 on v4

--- a/solution.py
+++ b/solution.py
@@ -191,12 +191,13 @@
             pltpu.SemaphoreType.DMA,
             pltpu.SemaphoreType.DMA,
         ],
-        compiler_params=pltpu.CompilerParams(vmem_limit_bytes=52 << 20),
+        compiler_params=pltpu.CompilerParams(vmem_limit_bytes=53 << 20),
         name="depth_sums",
     )(meta, code, weight, diffusion, view.reshape(slots, IMAGE, LANES), surface)
 
 
-def field_kernel(meta, inv, s_ref, q_ref, a_ref, b_ref, far_ref, surf_ref, f_ref, ca_ref, cb_ref):
+def field_kernel(meta, inv, s_ref, q_ref, a_ref, b_ref, far_ref, surf_ref, after_ref, f_ref, ca_ref, cb_ref):
+    del after_ref
     slots = s_ref.shape[0] // TILE
     even = meta[1] % 2 == 0
     group = lane_id((TILE, LANES)) // BLOCK
@@ -295,10 +296,10 @@
         cb_ref[pl.ds(h * TILE, TILE), :] = jnp.where(east_even, west_out, east_out)
 
 
-def region_fields(meta, places, s, q, a, b, far, surface):
+def region_fields(meta, places, s, q, a, b, far, surface, after):
     return pl.pallas_call(
         field_kernel,
-        in_specs=[SMEM, SMEM] + [VMEM] * 6,
+        in_specs=[SMEM, SMEM] + [VMEM] * 6 + [ANY],
         out_specs=[VMEM] * 3,
         out_shape=[
             jax.ShapeDtypeStruct((4, FIELD_TILES, FIELD_ROWS, LANES), F32),
@@ -307,7 +308,7 @@
         ],
         compiler_params=pltpu.CompilerParams(vmem_limit_bytes=12 << 20),
         name="region_fields",
-    )(meta, places, s, q, a, b, far, surface)
+    )(meta, places, s, q, a, b, far, surface, after)
 
 
 def basis_kernel(meta, moved, f_ref, ca_ref, cb_ref, g_ref, blocks_ref, back_ref, u_ref):
@@ -545,45 +546,88 @@
     )(meta, places, view.reshape(view.shape[0], IMAGE, LANES), after)
 
 
-def links_kernel(meta, table, t_ref, ga_ref, gb_ref, a_ref, b_ref, whole, half, sem_we, sem_ns):
+def lines_kernel(meta, table, t_ref, after_ref, a_ref, b_ref, half, sems):
+    del after_ref
+    even = meta[1] % 2 == 0
+    links = [[jnp.maximum(table[way * (CAP_WE + CAP_NS) + CAP_WE + k], 2) for k in range(CAP_NS)] for way in range(2)]
+
+    def copy(way, k):
+        link = links[way][k]
+        rows = pl.ds(pl.multiple_of((link % 4 - 2) * TILE, TILE), TILE)
+        dest = half.at[way, k, :, pl.ds(TILE, TILE), :]
+        return pltpu.make_async_copy(t_ref.at[link // 4, :, rows, :], dest, sems.at[way, k])
+
+    for way in range(2):
+        for k in range(CAP_NS):
+            copy(way, k).start()
+    place = lax.broadcasted_iota(jnp.int32, (TILE, LANES), 0) // 2 * 4 + lane_id((TILE, LANES)) // BLOCK
+    values = []
+    for way in range(2):
+        first = [TILE + 6 * (links[way][k] % 4 - 2) - 2 * (k // 4) for k in range(CAP_NS)]
+        by = [(BLOCK * (k % 4) + BLOCK * (links[way][k] % 4 - 2)) % LANES for k in range(CAP_NS)]
+        for k in range(CAP_NS):
+            copy(way, k).wait()
+        for level in range(LEVELS):
+            value = jnp.zeros((TILE, LANES), F32)
+            for k in range(CAP_NS):
+                x = pltpu.roll(half[way, k, level, pl.ds(first[k], TILE), :], by[k], 1)
+                value = jnp.where(place == k, x, value)
+            at = pl.ds(level * TILE, TILE)
+            if way == 0:
+                a_ref[at, :] = value
+            else:
+                other = a_ref[at, :]
+                a_ref[at, :] = jnp.where(even, other, value)
+                b_ref[at, :] = jnp.where(even, value, other)
+
+
+def line_strips(meta, table, view, after):
+    return pl.pallas_call(
+        lines_kernel,
+        in_specs=[SMEM, SMEM, HBM, ANY],
+        out_specs=[VMEM] * 2,
+        out_shape=[jax.ShapeDtypeStruct((LEVELS * TILE, LANES), F32)] * 2,
+        scratch_shapes=[
+            pltpu.VMEM((2, CAP_NS, LEVELS, 3 * TILE, LANES), F32),
+            pltpu.SemaphoreType.DMA((2, CAP_NS)),
+        ],
+        compiler_params=pltpu.CompilerParams(vmem_limit_bytes=52 << 20),
+        name="line_strips",
+    )(meta, table, view, after)
+
+
+def links_kernel(meta, table, t_ref, ga_ref, gb_ref, na_ref, nb_ref, a_ref, b_ref, whole, sems):
     even_x = meta[0] % 2 == 0
     even_y = meta[1] % 2 == 0
 
-    def we_copy(way, k):
+    def copy(way, k):
         link = jnp.maximum(table[way * (CAP_WE + CAP_NS) + k], 0)
-        return pltpu.make_async_copy(t_ref.at[link // 4], whole.at[way, k], sem_we.at[way, k])
-
-    def ns_copy(way, k):
-        link = jnp.maximum(table[way * (CAP_WE + CAP_NS) + CAP_WE + k], 2)
-        rows = pl.ds(pl.multiple_of((link % 4 - 2) * TILE, TILE), TILE)
-        dest = half.at[way, k, :, pl.ds(TILE, TILE), :]
-        return pltpu.make_async_copy(t_ref.at[link // 4, :, rows, :], dest, sem_ns.at[way, k])
+        return pltpu.make_async_copy(t_ref.at[link // 4], whole.at[way, k], sems.at[way, k])
 
     for way in range(2):
         for k in range(CAP_WE):
             @pl.when(table[way * (CAP_WE + CAP_NS) + k] >= 0)
             def _():
-                we_copy(way, k).start()
-
-        for k in range(CAP_NS):
-            ns_copy(way, k).start()
+                copy(way, k).start()
 
     column = lane_id((HALF * ROWS, LANES)) % 16
     from_west = jnp.where(even_x, gb_ref[...], ga_ref[...])
     from_east = jnp.where(even_x, ga_ref[...], gb_ref[...])
     ways = ((turn(from_west, -5, 1), from_east), (from_west, turn(from_east, 5, 1)))
     relays = [jnp.where(column < 5, w, jnp.where(column < RELAY, e, 0.0)) for w, e in ways]
+    for out, lines in ((a_ref, na_ref), (b_ref, nb_ref)):
+        out[pl.ds(HALF * ROWS, LEVELS * TILE), :] = lines[...]
+        out[pl.ds(HALF * ROWS + LEVELS * TILE, TILE), :] = jnp.zeros((TILE, LANES), F32)
 
     def message(way, out):
         out[pl.ds(0, HALF * ROWS), :] = relays[way]
-        out[pl.ds(HALF * ROWS + LEVELS * TILE, TILE), :] = jnp.zeros((TILE, LANES), F32)
         lane32 = lane_id((ROWS, LANES)) % BLOCK
         for k in range(CAP_WE):
             link = table[way * (CAP_WE + CAP_NS) + k]
 
             @pl.when(link >= 0)
             def _():
-                we_copy(way, k).wait()
+                copy(way, k).wait()
                 start = (link % 4) * (BLOCK - 1)
                 for level in range(HALF):
                     at = pl.ds(level * ROWS, ROWS)
@@ -595,20 +639,6 @@
                         value = jnp.where(lane32 == lane, x, value)
                     out[at, :] = value
 
-        links = [jnp.maximum(table[way * (CAP_WE + CAP_NS) + CAP_WE + k], 2) for k in range(CAP_NS)]
-        first = [TILE + 6 * (links[k] % 4 - 2) - 2 * (k // 4) for k in range(CAP_NS)]
-        by = [(BLOCK * (k % 4) + BLOCK * (links[k] % 4 - 2)) % LANES for k in range(CAP_NS)]
-        for k in range(CAP_NS):
-            ns_copy(way, k).wait()
-        row = lax.broadcasted_iota(jnp.int32, (TILE, LANES), 0) // 2
-        place = row * 4 + lane_id((TILE, LANES)) // BLOCK
-        for level in range(LEVELS):
-            value = jnp.zeros((TILE, LANES), F32)
-            for k in range(CAP_NS):
-                x = pltpu.roll(half[way, k, level, pl.ds(first[k], TILE), :], by[k], 1)
-                value = jnp.where(place == k, x, value)
-            out[pl.ds(HALF * ROWS + level * TILE, TILE), :] = value
-
     @pl.when(even_y)
     def _():
         message(0, a_ref)
@@ -620,22 +650,19 @@
         message(1, a_ref)
 
 
-def link_strips(meta, table, view, ga, gb):
-    rows = LINK_ROWS
+def link_strips(meta, table, view, ga, gb, na, nb):
     return pl.pallas_call(
         links_kernel,
-        in_specs=[SMEM, SMEM, HBM, VMEM, VMEM],
+        in_specs=[SMEM, SMEM, HBM] + [VMEM] * 4,
         out_specs=[VMEM] * 2,
-        out_shape=[jax.ShapeDtypeStruct((rows, LANES), F32)] * 2,
+        out_shape=[jax.ShapeDtypeStruct((LINK_ROWS, LANES), F32)] * 2,
         scratch_shapes=[
             pltpu.VMEM((2, CAP_WE, LEVELS, ROWS, LANES), F32),
-            pltpu.VMEM((2, CAP_NS, LEVELS, 3 * TILE, LANES), F32),
             pltpu.SemaphoreType.DMA((2, CAP_WE)),
-            pltpu.SemaphoreType.DMA((2, CAP_NS)),
         ],
         compiler_params=pltpu.CompilerParams(vmem_limit_bytes=52 << 20),
         name="link_strips",
-    )(meta, table, view, ga, gb)
+    )(meta, table, view, ga, gb, na, nb)
 
 
 BOX_LOW = 2 * HALF * ROWS
@@ -913,15 +940,17 @@
 
     source, places = lax.optimization_barrier((halo_source, places))
     table, need, send, over = strip_tables(source, code, at_x, at_y, count_x, count_y)
-    ga, gb = swap(*column_strips(meta, places, view, rfar), "gx", count_x)
+    columns = column_strips(meta, places, view, rfar)
+    ga, gb = swap(*columns, "gx", count_x)
+    na, nb = line_strips(meta, send, view, columns[0])
 
     moved = jnp.where(at_y % 2 == 0, rb[IDS, :MOVED], ra[IDS, :MOVED]).astype(jnp.int32)
     spot = jnp.arange(2 * REGION, dtype=jnp.int32)[:, None]
     index = jnp.arange(MOVED, dtype=jnp.int32)[None, :]
     both = places + jnp.sum(jnp.where(moved[None, :] == spot, index + 1 + slots, 0), axis=1)
-    fields, ca, cb = region_fields(meta, both, s, q, ra, rb, rfar, surface_term)
+    fields, ca, cb = region_fields(meta, both, s, q, ra, rb, rfar, surface_term, na)
     ca, cb = swap(ca, cb, "gx", count_x)
-    ha, hb = swap(*link_strips(meta, send, view, ga, gb), "gy", count_y)
+    ha, hb = swap(*link_strips(meta, send, view, ga, gb, na, nb), "gy", count_y)
 
     meta_over = jnp.stack([at_x, at_y, zero + count_y, over]).astype(jnp.int32)
     sums, blocks, back = solve_basis(meta_over, moved, fields, ca, cb, count_x * count_y)

time: 69.8 us -> 69.3 us (level)
  waiting for transfers between devices: 2.89 us -> 0.03 us
  starting transfers between devices: 20 us -> 21.7 us
  Pallas kernels: 38 us -> 39.6 us
  local copies, waits for them, and re-layouts: 3.04 us -> 2.05 us
    ppermute x4, waiting for transfers between devices: 2.87 us -> 0.01 us  [swap(): lax.ppermute(to_next, axis, first)]
    pallas_call x2 -> x3, Pallas kernels: 5.55 us -> 6.87 us  [the longest x1 3.21 us: line_strips(): pl.pallas_call(lines_kernel, in_specs=[SMEM, SMEM, HBM, ANY], out_specs=[...]
    all_to_all x1, starting transfers between devices: 2.92 us -> 4.1 us  [on_device(): sums = lax.all_to_all(sums[:, None], ('gx', 'gy'), 0, 0, tiled=True)]
    unnamed x14, local copies, waits for them, and re-layouts: 2.06 us -> 1.07 us
    ppermute x4, starting transfers between devices: 1.14 us -> 1.94 us  [swap(): lax.ppermute(to_next, axis, first)]
  transfers between devices with their start and end apart: 11 -> 11, of which waited for: 1 -> 0; matrix products, arithmetic and copies ran while one was open for 5% -> 5% of each run, Pallas kernels for 43% -> 46%
where the time goes in v5:
time: 69.3 us; the launch traced here: 68.9 us
  Pallas kernels  39.6 us (57%)
  starting transfers between devices  21.7 us (31%)
  other arithmetic  3.08 us (4%)
  between operations  2.15 us (3%)
  local copies, waits for them, and re-layouts  2.05 us (3%)
    pallas_call x1, Pallas kernels, step_tracers(): pl.pallas_call(tracer_kernel, in_specs=[SMEM] * 4 + [HBM] + [VMEM] * 4, o...  17.3 us
    ppermute x4, starting transfers between devices, swap(): lax.ppermute(to_last, axis, second)  7.85 us
    ppermute x2, starting transfers between devices, shifted(): lax.ppermute(x, axis, [(i, (i + by) % length) for i in range(length)])  7.84 us
    pallas_call x1, Pallas kernels, depth_sums(): pl.pallas_call(sums_kernel, in_specs=[SMEM] * 4 + [HBM, HBM], out_specs=[...  5.81 us
    all_to_all x1, starting transfers between devices, on_device(): sums = lax.all_to_all(sums[:, None], ('gx', 'gy'), 0, 0, tiled=True)  4.1 us
    pallas_call x1, Pallas kernels, column_strips(): pl.pallas_call(columns_kernel, in_specs=[SMEM, SMEM, HBM, ANY], out_specs...  3.88 us
    pallas_call x1, Pallas kernels, solve_basis(): pl.pallas_call(basis_kernel, in_specs=[SMEM, SMEM, VMEM, VMEM, VMEM], out...  3.81 us
    pallas_call x1, Pallas kernels, line_strips(): pl.pallas_call(lines_kernel, in_specs=[SMEM, SMEM, HBM, ANY], out_specs=[...  3.21 us
  transfers between devices with their start and end apart: 11, of which 0 were waited for; matrix products, arithmetic and copies ran while one was open for 5% of the time, Pallas kernels for 46%

profile of v5, /device:TPU:0, one launch (start us, length us, event | category | flops | bytes accessed | tf_op | source)
XLA Modules:
  0.0 68.9 jit_solution(11885534275528843792)
XLA Ops:
  0.6 0.0 copy-start.10
  0.6 0.7 %broadcast_remainder_fusion = (s32[63]{0:T(128)S(1)}, s32[63]{0:T(128)S(1)}, s32[63]{0:T(128)S(1)}) fusion(s32[]{:T(128)S(6)} %mul.164, s32[63]{0:T(128)} %param.12), kind=kLoop, calls=%fused_computation.207 | loop fusion | flops 2268 | bytes 1012 | tf_op jit(solution)/shard_map/jit(remainder)/rem | solution.py:907
  1.4 0.0 copy-start.2
  1.4 0.1 pad_add_fusion
  1.4 0.0 copy-start.4
  1.4 0.7 copy-done.4
  2.1 5.8 %depth_sums.1 = (f32[504,128]{1,0:T(8,128)S(1)}, f32[504,128]{1,0:T(8,128)}, f32[440,128]{1,0:T(8,128)S(1)}, f32[440,128]{1,0:T(8,128)S(1)}, f32[48,128]{1,0:T(8,128)S(1)}, /*index=5*/s32[140]{0:T(256)S(1)}) custom-call(s32[4]{0:T(128)S(1)} %get-tuple-element.90.meta, s32[63]{0:T(128)S(1)} %get-tuple-element.89.code, f32[2,20]{1,0:T(2,128)S(1)} %copy-done.4, ...), custom_call_target="tpu_custom_call" | custom-call | tf_op jit(solution)/shard_map/depth_sums/pallas_call | solution.py:181
  7.9 3.1 %collective-permute-start.6 = (f32[48,128]{1,0:T(8,128)S(1)}, f32[48,128]{1,0:T(8,128)S(1)}, u32[]{:S(2)}, u32[]{:S(2)}) collective-permute-start(f32[48,128]{1,0:T(8,128)S(1)} %get-tuple-element.46), channel_id=1, source_target_pairs={{0,2},{1,3},{2,4},{3,5},{4,6},{5,7},{6,0},{7,1},{8,10},{9,11},{10,... | collective-permute-start | bytes 73736 | tf_op jit(solution)/shard_map/ppermute | solution.py:73
  11.0 3.2 %collective-permute-start.4 = (f32[440,128]{1,0:T(8,128)S(1)}, f32[440,128]{1,0:T(8,128)S(1)}, u32[]{:S(2)}, u32[]{:S(2)}) collective-permute-start(f32[440,128]{1,0:T(8,128)S(1)} %get-tuple-element.41), channel_id=1, source_target_pairs={{0,7},{1,2},{2,1},{3,4},{4,3},{5,6},{6,5},{7,0},{8,15},{9,10},{10,... | collective-permute-start | bytes 675848 | tf_op jit(solution)/shard_map/ppermute | solution.py:58
  14.2 0.0 copy-done.2
  14.2 0.0 collective-permute-start.5
  14.2 0.0 copy-done.10
  14.2 0.1 copy.139
  14.3 0.1 reshape.1069
  14.4 0.1 reshape.1071
  14.6 0.3 convert_reduce_fusion
  14.9 0.1 reduce_sum.39
  15.0 0.2 select_reduce_fusion
  15.2 0.1 broadcast_in_dim.146
  15.2 0.1 rem.524
  15.4 0.1 broadcast_in_dim.140
  15.4 0.1 add.602
  15.6 0.1 copy.140
  15.6 0.7 and_reduce_fusion
  17.0 0.1 pad_add_fusion.1.meta
  17.0 0.0 copy-start
  17.0 0.0 copy-start.1
  17.0 0.0 collective-permute-done.6.after_ref.far_ref
  17.1 3.9 %column_strips.1 = (f32[160,128]{1,0:T(8,128)S(1)}, f32[160,128]{1,0:T(8,128)S(1)}) custom-call(s32[4]{0:T(128)S(1)} %get-tuple-element.90.meta, s32[140]{0:T(256)S(1)} %get-tuple-element.43.inv, f32[63,320,128]{2,1,0:T(8,128)} %bitcast.87, f32[48,128]{1,0:T(8,128)S(1)} %collective-permute-done.6.after_ref.far_ref), custom_call_target="tpu_custom_call" | custom-call | flops 1 | bytes 1 | tf_op jit(solution)/shard_map/column_strips/pallas_call | solution.py:533
  20.9 0.1 collective-permute-start.9
  21.0 1.6 %collective-permute-start.10 = (f32[160,128]{1,0:T(8,128)S(1)}, f32[160,128]{1,0:T(8,128)S(1)}, u32[]{:S(2)}, u32[]{:S(2)}) collective-permute-start(f32[160,128]{1,0:T(8,128)S(1)} %get-tuple-element.53), channel_id=1, source_target_pairs={{0,24},{8,16},{16,8},{24,0},{1,25},{9,17},{17,9},{25,1},{2,26},{10... | collective-permute-start | bytes 245768 | tf_op jit(solution)/shard_map/ppermute | solution.py:58
  22.6 0.0 copy-start.11
  22.6 3.2 %line_strips.1 = (f32[160,128]{1,0:T(8,128)S(1)}, f32[160,128]{1,0:T(8,128)S(1)}) custom-call(s32[4]{0:T(128)S(1)} %get-tuple-element.90.meta, s32[44]{0:T(128)S(1)} %broadcast_add_fusion.2.table, f32[63,20,16,128]{3,2,1,0:T(8,128)} %bitcast.88, f32[160,128]{1,0:T(8,128)S(1)} %get-tuple-element.47.after_ref), custom_call_target="tpu_custom_call" | custom-call | tf_op jit(solution)/shard_map/line_strips/pallas_call | solution.py:585
  25.8 0.0 collective-permute-done.4.b_ref
  25.8 0.0 collective-permute-done.5.a_ref
  25.9 0.1 select_reduce_fusion.1
  26.0 0.0 copy-done
  26.0 0.0 copy-done.1
  26.0 1.6 %region_fields.1 = (f32[4,4,176,128]{3,2,1,0:T(8,128)S(1)}, f32[24,128]{1,0:T(8,128)S(1)}, f32[24,128]{1,0:T(8,128)S(1)}) custom-call(s32[4]{0:T(128)S(1)} %get-tuple-element.90.meta, s32[140]{0:T(256)S(1)} %add.590.inv, f32[504,128]{1,0:T(8,128)S(1)} %get-tuple-element.44.s_ref, f32[504,128]{1,0:T(8,128)S(1)} %copy-done.1, ...), custom_call_target="tpu_custom_call" | custom-call | tf_op jit(solution)/shard_map/region_fields/pallas_call | solution.py:300
  27.6 0.3 collective-permute-start.7
  27.9 1.2 %collective-permute-start.8 = (f32[24,128]{1,0:T(8,128)S(1)}, f32[24,128]{1,0:T(8,128)S(1)}, u32[]{:S(2)}, u32[]{:S(2)}) collective-permute-start(f32[24,128]{1,0:T(8,128)S(1)} %get-tuple-element.51), channel_id=1, source_target_pairs={{0,24},{8,16},{16,8},{24,0},{1,25},{9,17},{17,9},{25,1},{2,26},{10... | collective-permute-start | bytes 36872 | tf_op jit(solution)/shard_map/ppermute | solution.py:58
  29.2 0.1 reduce_max.26
  29.3 0.1 reduce_max.27
  29.4 0.0 collective-permute-done.9.ga_ref
  29.4 0.0 collective-permute-done.10.gb_ref
  29.4 2.0 %link_strips.1 = (f32[328,128]{1,0:T(8,128)S(1)}, f32[328,128]{1,0:T(8,128)S(1)}) custom-call(s32[4]{0:T(128)S(1)} %get-tuple-element.90.meta, s32[44]{0:T(128)S(1)} %broadcast_add_fusion.2.table, f32[63,20,16,128]{3,2,1,0:T(8,128)} %bitcast.89, f32[160,128]{1,0:T(8,128)S(1)} %collective-permute-done.9.ga_ref, ...), custom_call_target="tpu_custom_call" | custom-call | tf_op jit(solution)/shard_map/link_strips/pallas_call | solution.py:654
  31.4 1.6 %collective-permute-start.11 = (f32[328,128]{1,0:T(8,128)S(1)}, f32[328,128]{1,0:T(8,128)S(1)}, u32[]{:S(2)}, u32[]{:S(2)}) collective-permute-start(f32[328,128]{1,0:T(8,128)S(1)} %get-tuple-element.55), channel_id=1, source_target_pairs={{0,1},{1,0},{2,3},{3,2},{4,5},{5,4},{6,7},{7,6},{8,9},{9,8},{10,11... | collective-permute-start | bytes 503816 | tf_op jit(solution)/shard_map/ppermute | solution.py:58
  33.0 1.8 %collective-permute-start.12 = (f32[328,128]{1,0:T(8,128)S(1)}, f32[328,128]{1,0:T(8,128)S(1)}, u32[]{:S(2)}, u32[]{:S(2)}) collective-permute-start(f32[328,128]{1,0:T(8,128)S(1)} %get-tuple-element.56), channel_id=1, source_target_pairs={{0,7},{1,2},{2,1},{3,4},{4,3},{5,6},{6,5},{7,0},{8,15},{9,10},{10,... | collective-permute-start | bytes 503816 | tf_op jit(solution)/shard_map/ppermute | solution.py:58
  34.9 0.0 collective-permute-done.7.ca_ref
  34.9 0.0 collective-permute-done.8.cb_ref
  34.9 3.8 %solve_basis.1 = (f32[32,128]{1,0:T(8,128)}, f32[1680,128]{1,0:T(8,128)S(1)}, f32[528,128]{1,0:T(8,128)}) custom-call(s32[4]{0:T(128)S(1)} %pad_add_fusion.1.meta, s32[22]{0:T(128)S(1)} %fusion.48.moved, f32[4,4,176,128]{3,2,1,0:T(8,128)S(1)} %get-tuple-element.49.f_ref, f32[24,128]{1,0:T(8,128)S(1)} %collective-permute-done.7.ca_ref, ...), custom_call_target="tpu_custom_call" | custom-call | tf_op jit(solution)/shard_map/solve_basis/pallas_call | solution.py:410
  38.7 4.1 %all-to-all-start = ((f32[32,1,128]{2,1,0:T(1,128)}), f32[32,1,128]{2,1,0:T(1,128)S(1)}, u32[]{:S(2)}, u32[]{:S(2)}) async-start(f32[32,1,128]{2,1,0:T(1,128)} %bitcast.32), calls=%async_computation | async-start | bytes 32768 | tf_op jit(solution)/shard_map/all_to_all | solution.py:958
  42.8 4.8 %collective-permute-start.13 = (f32[528,128]{1,0:T(8,128)}, f32[528,128]{1,0:T(8,128)}, u32[]{:S(2)}, u32[]{:S(2)}) collective-permute-start(f32[528,128]{1,0:T(8,128)} %get-tuple-element.59), channel_id=1, source_target_pairs={{0,7},{1,0},{2,1},{3,2},{4,3},{5,4},{6,5},{7,6},{8,15},{9,8},{10,9... | collective-permute-start | bytes 811016 | tf_op jit(solution)/shard_map/ppermute | solution.py:73
  47.6 0.0 collective-permute-done.11.ha_ref
  47.6 0.0 collective-permute-done.12.hb_ref
  47.6 0.0 copy-done.11
  47.7 17.3 %step_tracers.1 = f32[63,320,128]{2,1,0:T(8,128)} custom-call(s32[4]{0:T(128)S(1)} %get-tuple-element.90.meta, s32[5,252]{1,0:T(8,128)S(1)} %stack.37.table, s32[9]{0:T(128)S(1)} %iota_maximum_fusion.need, f32[20]{0:T(128)S(1)} %copy-done.11, f32[63,320,128]{2,1,0:T(8,128)} %bitcast.90, f32[160,128]{1,0:T(8,128)S(1)} %collective-permute-done.9.ga_ref, ...), custom_call_target="tpu_custom_call" | custom-call | flops 36126720 | bytes 20643840 | tf_op jit(solution)/shard_map/step_tracers/pallas_call | solution.py:805
  64.9 0.0 all-to-all-done
  64.9 0.7 %slice_reduce_fusion = f32[]{:T(128)} fusion(f32[32,1,128]{2,1,0:T(1,128)S(1)} %all-to-all-done), kind=kLoop, calls=%fused_computation.70 | loop fusion | flops 31 | bytes 132 | tf_op jit(solution)/shard_map/reduce_max | solution.py:962
  66.3 0.0 copy-start.3
  66.3 0.3 conditional.1
  66.6 0.0 collective-permute-done.13.back_ref
  66.6 0.4 copy-done.3
  67.0 2.0 %slot_pressure.1 = (f32[63,1024]{1,0:T(8,128)}, f32[63,20,16,128]{3,2,1,0:T(8,128)}) custom-call(s32[63]{0:T(128)S(1)} %copy-done.3, f32[32,128]{1,0:T(8,128)S(1)} %bitcast.77, f32[1680,128]{1,0:T(8,128)S(1)} %get-tuple-element.58.blocks_ref, f32[528,128]{1,0:T(8,128)} %collective-permute-done.13.back_ref, ...), custom_call_target="tpu_custom_call", output_to_operand_aliasing={{1}: (4, {})} | custom-call | tf_op jit(solution)/shard_map/slot_pressure/pallas_call | solution.py:478
  (14 shorter events, 0.2 us)
Async XLA Ops:
  0.6 13.6 %copy-start.10 = (s32[63,4]{0,1:T(4,128)S(1)}, s32[63,4]{0,1:T(4,128)}, u32[]{:S(2)}) copy-start(s32[63,4]{0,1:T(4,128)} %param.13) | copy-start | bytes 3028
  1.4 12.8 %copy-start.2 = (s32[63]{0:T(128)}, s32[63]{0:T(128)S(1)}, u32[]{:S(2)}) copy-start(s32[63]{0:T(128)S(1)} %get-tuple-element.89.code) | copy-start | bytes 760
  1.4 0.7 copy-start.4
  7.9 9.1 %collective-permute-start.6 = (f32[48,128]{1,0:T(8,128)S(1)}, f32[48,128]{1,0:T(8,128)S(1)}, u32[]{:S(2)}, u32[]{:S(2)}) collective-permute-start(f32[48,128]{1,0:T(8,128)S(1)} %get-tuple-element.46), channel_id=1, source_target_pairs={{0,2},{1,3},{2,4},{3,5},{4,6},{5,7},{6,0},{7,1},{8,10},{9,11},{10,... | collective-permute-start | bytes 73736 | tf_op jit(solution)/shard_map/ppermute | solution.py:73
  11.0 14.8 %collective-permute-start.4 = (f32[440,128]{1,0:T(8,128)S(1)}, f32[440,128]{1,0:T(8,128)S(1)}, u32[]{:S(2)}, u32[]{:S(2)}) collective-permute-start(f32[440,128]{1,0:T(8,128)S(1)} %get-tuple-element.41), channel_id=1, source_target_pairs={{0,7},{1,2},{2,1},{3,4},{4,3},{5,6},{6,5},{7,0},{8,15},{9,10},{10,... | collective-permute-start | bytes 675848 | tf_op jit(solution)/shard_map/ppermute | solution.py:58
  14.2 11.6 %collective-permute-start.5 = (f32[440,128]{1,0:T(8,128)S(1)}, f32[440,128]{1,0:T(8,128)S(1)}, u32[]{:S(2)}, u32[]{:S(2)}) collective-permute-start(f32[440,128]{1,0:T(8,128)S(1)} %get-tuple-element.42), channel_id=1, source_target_pairs={{0,1},{1,0},{2,3},{3,2},{4,5},{5,4},{6,7},{7,6},{8,9},{9,8},{10,11... | collective-permute-start | bytes 675848 | tf_op jit(solution)/shard_map/ppermute | solution.py:58
  17.0 8.9 %copy-start = (f32[160,448]{1,0:T(8,128)S(1)}, f32[160,448]{1,0:T(8,128)}, u32[]{:S(2)}) copy-start(f32[160,448]{1,0:T(8,128)} %surf_ref.3) | copy-start | bytes 860164
  17.0 8.9 %copy-start.1 = (f32[504,128]{1,0:T(8,128)S(1)}, f32[504,128]{1,0:T(8,128)}, u32[]{:S(2)}) copy-start(f32[504,128]{1,0:T(8,128)} %get-tuple-element.45.q_ref) | copy-start | bytes 774148
  20.9 8.4 %collective-permute-start.9 = (f32[160,128]{1,0:T(8,128)S(1)}, f32[160,128]{1,0:T(8,128)S(1)}, u32[]{:S(2)}, u32[]{:S(2)}) collective-permute-start(f32[160,128]{1,0:T(8,128)S(1)} %get-tuple-element.47.after_ref), channel_id=1, source_target_pairs={{0,8},{8,0},{16,24},{24,16},{1,9},{9,1},{17,25},{25,17},{2,10},{10... | collective-permute-start | bytes 245768 | tf_op jit(solution)/shard_map/ppermute | solution.py:58
  21.0 8.4 %collective-permute-start.10 = (f32[160,128]{1,0:T(8,128)S(1)}, f32[160,128]{1,0:T(8,128)S(1)}, u32[]{:S(2)}, u32[]{:S(2)}) collective-permute-start(f32[160,128]{1,0:T(8,128)S(1)} %get-tuple-element.53), channel_id=1, source_target_pairs={{0,24},{8,16},{16,8},{24,0},{1,25},{9,17},{17,9},{25,1},{2,26},{10... | collective-permute-start | bytes 245768 | tf_op jit(solution)/shard_map/ppermute | solution.py:58
  22.6 25.0 %copy-start.11 = (f32[20]{0:T(128)S(1)}, f32[20]{0:T(128)}, u32[]{:S(2)}) copy-start(f32[20]{0:T(128)} %diffusion.3) | copy-start | bytes 244
  27.6 7.3 %collective-permute-start.7 = (f32[24,128]{1,0:T(8,128)S(1)}, f32[24,128]{1,0:T(8,128)S(1)}, u32[]{:S(2)}, u32[]{:S(2)}) collective-permute-start(f32[24,128]{1,0:T(8,128)S(1)} %get-tuple-element.50), channel_id=1, source_target_pairs={{0,8},{8,0},{16,24},{24,16},{1,9},{9,1},{17,25},{25,17},{2,10},{10... | collective-permute-start | bytes 36872 | tf_op jit(solution)/shard_map/ppermute | solution.py:58
  27.9 7.0 %collective-permute-start.8 = (f32[24,128]{1,0:T(8,128)S(1)}, f32[24,128]{1,0:T(8,128)S(1)}, u32[]{:S(2)}, u32[]{:S(2)}) collective-permute-start(f32[24,128]{1,0:T(8,128)S(1)} %get-tuple-element.51), channel_id=1, source_target_pairs={{0,24},{8,16},{16,8},{24,0},{1,25},{9,17},{17,9},{25,1},{2,26},{10... | collective-permute-start | bytes 36872 | tf_op jit(solution)/shard_map/ppermute | solution.py:58
  31.4 16.2 %collective-permute-start.11 = (f32[328,128]{1,0:T(8,128)S(1)}, f32[328,128]{1,0:T(8,128)S(1)}, u32[]{:S(2)}, u32[]{:S(2)}) collective-permute-start(f32[328,128]{1,0:T(8,128)S(1)} %get-tuple-element.55), channel_id=1, source_target_pairs={{0,1},{1,0},{2,3},{3,2},{4,5},{5,4},{6,7},{7,6},{8,9},{9,8},{10,11... | collective-permute-start | bytes 503816 | tf_op jit(solution)/shard_map/ppermute | solution.py:58
  33.0 14.6 %collective-permute-start.12 = (f32[328,128]{1,0:T(8,128)S(1)}, f32[328,128]{1,0:T(8,128)S(1)}, u32[]{:S(2)}, u32[]{:S(2)}) collective-permute-start(f32[328,128]{1,0:T(8,128)S(1)} %get-tuple-element.56), channel_id=1, source_target_pairs={{0,7},{1,2},{2,1},{3,4},{4,3},{5,6},{6,5},{7,0},{8,15},{9,10},{10,... | collective-permute-start | bytes 503816 | tf_op jit(solution)/shard_map/ppermute | solution.py:58
  38.7 26.2 %all-to-all-start = ((f32[32,1,128]{2,1,0:T(1,128)}), f32[32,1,128]{2,1,0:T(1,128)S(1)}, u32[]{:S(2)}, u32[]{:S(2)}) async-start(f32[32,1,128]{2,1,0:T(1,128)} %bitcast.32), calls=%async_computation | async-start | bytes 32768 | tf_op jit(solution)/shard_map/all_to_all | solution.py:958
  42.8 23.8 %collective-permute-start.13 = (f32[528,128]{1,0:T(8,128)}, f32[528,128]{1,0:T(8,128)}, u32[]{:S(2)}, u32[]{:S(2)}) collective-permute-start(f32[528,128]{1,0:T(8,128)} %get-tuple-element.59), channel_id=1, source_target_pairs={{0,7},{1,0},{2,1},{3,2},{4,3},{5,4},{6,5},{7,6},{8,15},{9,8},{10,9... | collective-permute-start | bytes 811016 | tf_op jit(solution)/shard_map/ppermute | solution.py:73
  66.3 0.7 copy-start.3
